TPU v7x, 32 devices: a whole 2x2x4 slice. The times are simulated.
32 devices in a mesh: context: 8 (over y, x, core), tensor: 4 (over z).
Axes of the slice: x: 2, y: 2, z: 4, core: 2. Of those that a mesh axis runs over, the one named last changes fastest.
Arguments:
- tokens_t: bfloat16 [6144, 2048], P('tensor', 'context'), may hold values from -6 to 6
- qkv_weight: bfloat16 [6144, 24576], P(None, 'tensor'), may hold values from -1.5309311 to 1.5309311, as said below
- prior_state: float32 [64, 128, 128], P('tensor'), may hold values from -192 to 192
- norm_gain: float32 [8192], P('tensor'), may hold values from 0.1 to 1.9
Outputs:
- mixed: bfloat16 [2048, 8192], P('context', 'tensor')
Inputs may be any that keep to these rules, and one draw needn't show every extreme that they name: `qkv_weight`: column h * 3 * 128 + p * 128 + e projects onto feature e of head h, with p = 0, 1, 2 for query, key and value.
All inputs are finite; a program needn't handle non-finite values.
Results may differ from a plain program's by a relative error of at most 0.0034.
Values may be sent and summed in bfloat16 or wider, within the bound.
No kernel may reach another device: no remote copies, remote signals or barrier semaphores. Data moves between devices by JAX's collectives and lax.ppermute only.
A program may use at most 128 MiB of HBM per device.

v0:
```python
import jax
import jax.numpy as jnp
from jax import lax
from jax.sharding import PartitionSpec as P

H = 64
HEAD = 128


EPSILON = 1e-06
PRECISE = lax.Precision.HIGHEST


def body(tokens_t, qkv_weight, prior_state, norm_gain):
    tok_rows = tokens_t.shape[1]
    head_count = prior_state.shape[0]
    head_width = prior_state.shape[1]
    projected = lax.dot_general(
        lax.all_gather(tokens_t, "tensor", axis=0, tiled=True),
        qkv_weight,
        (((0,), (0,)), ((), ())),
        preferred_element_type=jnp.float32,
    )
    activated = (
        jax.nn.silu(projected).astype(jnp.bfloat16).reshape(tok_rows, head_count, 3, head_width)
    )
    queries = activated[:, :, 0]
    key_rows = activated[:, :, 1]
    value_rows = activated[:, :, 2]
    group_state = jnp.einsum(
        "thd,the->hde", key_rows, value_rows, preferred_element_type=jnp.float32
    )
    my_index = lax.axis_index("context")
    block_part = lax.all_gather(group_state[None], "context", axis=0, tiled=True)
    positions = jnp.arange(block_part.shape[0])
    keep_rows = (positions < my_index).astype(jnp.float32)
    earlier = jnp.sum(keep_rows[:, None, None, None] * block_part, axis=0)
    carried = prior_state + earlier
    causal = jnp.arange(tok_rows)[:, None] >= jnp.arange(tok_rows)[None, :]
    scores = jnp.einsum("thd,shd->hts", queries, key_rows, preferred_element_type=jnp.float32)
    scores = jnp.where(causal[None], scores, 0.0).astype(jnp.bfloat16)
    within_term = jnp.einsum("hts,shd->thd", scores, value_rows, preferred_element_type=jnp.float32)
    carried_term = jnp.einsum(
        "thd,hde->the", queries.astype(jnp.float32), carried, precision=PRECISE
    )
    attended = (within_term + carried_term).reshape(tok_rows, head_count * head_width)
    square_sum = lax.psum(jnp.sum(attended * attended, axis=1), "tensor")
    inverse_rms = lax.rsqrt(square_sum / (H * HEAD) + EPSILON)
    return (attended * inverse_rms[:, None] * norm_gain[None, :]).astype(jnp.bfloat16)


def solution(mesh):
    in_specs = (P("tensor", "context"), P(None, "tensor"), P("tensor", None, None), P("tensor"))
    out_specs = P("context", "tensor")
    return jax.shard_map(body, mesh=mesh, in_specs=in_specs, out_specs=out_specs, check_vma=False)
```

profile of v0, /device:TPU:0, one launch (start us, length us, event | category | flops | bytes accessed | tf_op | source)
XLA Modules:
  0.0 193.4 jit_solution(15778325930603307656)
XLA Ops:
  6.5 0.0 all-gather.4.cloned.1.call-start
  6.5 0.7 all-gather.4.cloned.1.call-update
  7.3 0.0 all-gather.6.cloned.1.call-start
  7.3 67.9 %all-gather.4.cloned.1.call-done = bf16[6144,256]{1,0:T(8,128)(2,1)} async-done(((bf16[1536,256]{1,0:T(8,128)(2,1)}), bf16[6144,256]{1,0:T(8,128)(2,1)}) %all-gather.4.cloned.1.call-update) | async-done | bytes 3145744 | tf_op jit(solution)/shard_map/all_gather | solution.py:19
  75.2 31.3 %multiply_convert_fusion = bf16[256,6144]{1,0:T(8,128)(2,1)} fusion(bf16[6144,256]{1,0:T(8,128)(2,1)} %all-gather.4.cloned.1.call-done, bf16[6144,6144]{1,0:T(8,128)(2,1)} %param.5), kind=kOutput, calls=%fused_computation.1 | convolution fusion | flops 19335217152 | bytes 81788928 | tf_op jit(solution)/shard_map/dot_general | solution.py:18
  106.5 3.2 %copy.18 = bf16[256,6144]{0,1:T(8,128)(2,1)S(1)} copy(bf16[256,6144]{1,0:T(8,128)(2,1)} %multiply_convert_fusion) | data formatting | bytes 6291456 | tf_op jit(solution)/shard_map/convert_element_type | solution.py:25
  109.7 1.4 fusion.3
  111.1 0.0 all-gather.6.cloned.1.call-update
  111.1 2.8 %fusion.1 = f32[16,128,256]{2,1,0:T(8,128)} fusion(pred[256,256]{1,0:T(8,128)(4,1)S(1)} %iota_compare_fusion, bf16[256,16,3,128]{0,3,2,1:T(8,128)(2,1)S(1)} %bitcast.33), kind=kOutput, calls=%fused_computation.6 | convolution fusion | flops 538968064 | bytes 5308416 | tf_op jit(solution)/shard_map/hts,shd->thd/dot_general | solution.py:42
  113.9 50.4 %all-gather.6.cloned.1.call-done = f32[128,128,128]{2,1,0:T(8,128)} async-done(((f32[16,128,128]{2,1,0:T(8,128)}), f32[128,128,128]{2,1,0:T(8,128)}) %all-gather.6.cloned.1.call-update) | async-done | bytes 8388624 | tf_op jit(solution)/shard_map/all_gather | solution.py:34
  164.3 0.0 copy-start
  164.3 0.0 copy-start.1
  164.3 4.7 %multiply_reduce_fusion = f32[16,128,128]{2,1,0:T(8,128)S(1)} fusion(f32[8,16,128,128]{3,2,1,0:T(8,128)} %bitcast.35, f32[8]{0:T(128)S(1)} %compare_convert_fusion), kind=kLoop, calls=%fused_computation | loop fusion | flops 3932160 | bytes 9437216 | tf_op jit(solution)/shard_map/reduce_sum | solution.py:37
  169.0 0.0 copy-done
  169.0 0.0 copy-done.1
  169.0 2.6 %fusion = (f32[256]{0:T(256)S(1)}, f32[16,128,256]{2,1,0:T(8,128)}) fusion(f32[16,128,256]{2,1,0:T(8,128)S(1)} %copy-done, bf16[256,16,3,128]{0,3,2,1:T(8,128)(2,1)S(1)} %bitcast.34, f32[16,128,128]{2,1,0:T(8,128)S(1)} %copy-done.1, f32[16,128,128]{2,1,0:T(8,128)S(1)} %multiply_reduce_fusion), kind=kOutput, calls=%fused_computation.4 | convolution fusion | flops 807141120 | bytes 7341056 | tf_op jit(solution)/shard_map/thd,hde->the/dot_general | solution.py:43
  171.6 0.0 copy-start.2
  171.6 11.8 %psum.7 = f32[256]{0:T(256)S(1)} all-reduce(f32[256]{0:T(256)S(1)} %get-tuple-element.5), channel_id=1, replica_groups=mesh['context'=8,'tensor'=4] {'tensor'}, use_global_device_ids=true, to_apply=%region_2.3 | all-reduce | flops 256 | bytes 2048 | tf_op jit(solution)/shard_map/psum | solution.py:47
  183.4 1.9 copy.25
  185.4 0.0 copy-done.2
  185.4 1.2 multiply_convert_fusion.1
  (3 shorter events, 0.0 us)
Async XLA Ops:
  6.5 68.6 %all-gather.4.cloned.1.call-start = ((), (), s32[]{:S(2)}) async-start(), calls=%async_computation | async-start | bytes 3932160 | tf_op jit(solution)/shard_map/all_gather | solution.py:19
  7.3 157.0 %all-gather.6.cloned.1.call-start = ((), (), s32[]{:S(2)}) async-start(), calls=%async_computation.1 | async-start | bytes 9437184 | tf_op jit(solution)/shard_map/all_gather | solution.py:34
  164.3 4.7 %copy-start = (f32[16,128,256]{2,1,0:T(8,128)S(1)}, f32[16,128,256]{2,1,0:T(8,128)}, u32[]{:S(2)}) copy-start(f32[16,128,256]{2,1,0:T(8,128)} %fusion.1) | copy-start | bytes 6291460
  164.3 4.7 %copy-start.1 = (f32[16,128,128]{2,1,0:T(8,128)S(1)}, f32[16,128,128]{2,1,0:T(8,128)}, u32[]{:S(2)}) copy-start(f32[16,128,128]{2,1,0:T(8,128)} %param.6) | copy-start | bytes 3145732
  171.6 13.7 %copy-start.2 = (f32[2048]{0:T(1024)S(1)}, f32[2048]{0:T(1024)}, u32[]{:S(2)}) copy-start(f32[2048]{0:T(1024)} %param.7) | copy-start | bytes 24580
Sparse Core Ops, SparseCore 0:
  8.9 66.1 all-gather.3
  111.2 53.0 all-gather.5
where the time goes:
time: 194 us; the launch traced here: 193 us
  waiting for transfers between devices  119 us (61%)
  matrix products  38.1 us (20%)
  between operations  13.5 us (7%)
  blocking collectives  11.8 us (6%)
  other arithmetic  5.98 us (3%)
  local copies, waits for them, and re-layouts  5.1 us (3%)
    all_gather x1, waiting for transfers between devices, body(): lax.all_gather(tokens_t, 'tensor', axis=0, tiled=True)  67.9 us
    all_gather x1, waiting for transfers between devices, body(): lax.all_gather(group_state[None], 'context', axis=0, tiled=True)  50.4 us
    dot_general x1, matrix products, body(): lax.dot_general(lax.all_gather(tokens_t, 'tensor', axis=0, tiled=True), q...  31.3 us
    psum x1, blocking collectives, body(): square_sum = lax.psum(jnp.sum(attended * attended, axis=1), 'tensor')  11.8 us
    reduce_sum x1, other arithmetic, body(): earlier = jnp.sum(keep_rows[:, None, None, None] * block_part, axis=0)  4.72 us
  transfers between devices with their start and end apart: 2, of which 2 were waited for; matrix products, arithmetic and copies ran while one was open for 1% of the time, Pallas kernels for 0%

commit v1 on v0

v1 whole, which is shorter than its diff:
```python
import functools

import jax
import jax.numpy as jnp
from jax import lax
from jax.experimental import pallas as pl
from jax.experimental.pallas import tpu as pltpu
from jax.sharding import PartitionSpec as P

EPSILON = 1e-06
PARTS = 3
CHUNKS = 2
COLUMNS = 1024
VMEM_LIMIT = 32 * 1024 * 1024

F32 = jnp.float32
BF16 = jnp.bfloat16


def params():
    return pltpu.CompilerParams(vmem_limit_bytes=VMEM_LIMIT)


WHOLE = pl.BlockSpec(memory_space=pltpu.VMEM)
ANY = pl.BlockSpec(memory_space=pl.ANY)


def feature_copies(pieces, raw, sems):
    rows = pieces[0].shape[0]
    return [
        pltpu.make_async_copy(piece, raw.at[pl.ds(j * rows, rows)], sems.at[j])
        for j, piece in enumerate(pieces)
    ]


def start_features(pick, choices, raw, sems):
    for c, pieces in enumerate(choices):

        @pl.when(pick == c)
        def _(pieces=pieces):
            for copy in feature_copies(pieces, raw, sems):
                copy.start()


def wait_features(choices, raw, sems):
    for copy in feature_copies(choices[0], raw, sems):
        copy.wait()


def column_blocks(columns):
    width = COLUMNS if columns % COLUMNS == 0 else columns
    return [pl.ds(at, width) for at in range(0, columns, width)]


def project_kernel(n_choices, n_pieces, first, ahead, info, *refs):
    count = n_choices * n_pieces
    choices = [refs[c * n_pieces : (c + 1) * n_pieces] for c in range(n_choices)]
    weight = refs[count]
    refs = refs[count + (1 if first else 2) :]
    total, refs = refs[0], refs[1:]
    if ahead:
        slab, refs = refs[0], refs[1:]
    raw, turned, held, sems, weight_sems = refs
    rows, columns = held.shape
    blocks = column_blocks(columns)

    start_features(info[0], choices, raw, sems)
    at = pl.ds(pl.multiple_of(info[1] * rows, rows), rows)
    copies = [
        pltpu.make_async_copy(weight.at[at, block], held.at[:, block], weight_sems.at[b])
        for b, block in enumerate(blocks)
    ]
    for copy in copies:
        copy.start()
    if ahead:
        later = pl.ds(pl.multiple_of(info[2] * ahead, ahead), ahead)
        slab_copy = pltpu.make_async_copy(
            weight.at[later, :], slab, weight_sems.at[len(blocks)]
        )
        slab_copy.start()
    wait_features(choices, raw, sems)
    turned[...] = raw[...].T
    for copy, block in zip(copies, blocks):
        copy.wait()
        product = jnp.dot(turned[...], held[:, block], preferred_element_type=F32)
        if first:
            total[:, block] = product
        else:
            total[:, block] += product
    if ahead:
        slab_copy.wait()


def project(choices, info, weight, total, ahead=0):
    n_choices, n_pieces = len(choices), len(choices[0])
    piece_rows, tokens = choices[0][0].shape
    rows, columns = piece_rows * n_pieces, weight.shape[1]
    first = total is None
    flat = [piece for pieces in choices for piece in pieces]
    operands = flat + [weight] + ([] if first else [total])
    out_shape = [pltpu.VMEM((tokens, columns), F32)]
    if ahead:
        out_shape.append(pltpu.VMEM((ahead, columns), BF16))
    out = pl.pallas_call(
        functools.partial(project_kernel, n_choices, n_pieces, first, ahead),
        out_shape=out_shape,
        in_specs=[pl.BlockSpec(memory_space=pltpu.SMEM)]
        + [ANY] * (len(flat) + 1)
        + ([] if first else [WHOLE]),
        out_specs=[WHOLE] * len(out_shape),
        scratch_shapes=[
            pltpu.VMEM((rows, tokens), BF16),
            pltpu.VMEM((tokens, rows), BF16),
            pltpu.VMEM((rows, columns), BF16),
            pltpu.SemaphoreType.DMA((n_pieces,)),
            pltpu.SemaphoreType.DMA((len(column_blocks(columns)) + 1,)),
        ],
        input_output_aliases={} if first else {len(operands): 0},
        compiler_params=params(),
        cost_estimate=pl.CostEstimate(
            flops=2 * tokens * rows * columns,
            bytes_accessed=(rows + ahead) * columns * 2 + rows * tokens * 2,
            transcendentals=0,
        ),
        name="project",
    )(info, *operands)
    return out if ahead else out[0]


def activate_kernel(n_choices, width, info, *refs):
    choices = [[ref] for ref in refs[:n_choices]]
    slab, total, act_ref, state_ref, raw, turned, sems = refs[n_choices:]
    heads = state_ref.shape[0]
    start_features(info[0], choices, raw, sems)
    wait_features(choices, raw, sems)
    turned[...] = raw[...].T
    group = PARTS * width
    for h in range(heads):
        block = pl.ds(h * group, group)
        projected = total[:, block] + jnp.dot(
            turned[...], slab[:, block], preferred_element_type=F32
        )
        act = (projected / (1.0 + jnp.exp(-projected))).astype(BF16)
        act_ref[:, block] = act
        state_ref[lax.rem(h + info[1], heads)] = lax.dot_general(
            act[:, width : 2 * width],
            act[:, 2 * width :],
            (((0,), (0,)), ((), ())),
            preferred_element_type=F32,
        )


def activate(choices, info, slab, total, width):
    tokens = choices[0].shape[1]
    rows, columns = slab.shape
    heads = columns // (PARTS * width)
    return pl.pallas_call(
        functools.partial(activate_kernel, len(choices), width),
        out_shape=(
            pltpu.VMEM((tokens, columns), BF16),
            jax.ShapeDtypeStruct((heads, width, width), F32),
        ),
        in_specs=[pl.BlockSpec(memory_space=pltpu.SMEM)] + [ANY] * len(choices) + [WHOLE] * 2,
        out_specs=(WHOLE, WHOLE),
        scratch_shapes=[
            pltpu.VMEM((rows, tokens), BF16),
            pltpu.VMEM((tokens, rows), BF16),
            pltpu.SemaphoreType.DMA((1,)),
        ],
        compiler_params=params(),
        cost_estimate=pl.CostEstimate(
            flops=2 * tokens * rows * columns + 2 * heads * tokens * width * width,
            bytes_accessed=rows * tokens * 2,
            transcendentals=tokens * columns,
        ),
        name="activate",
    )(info, *choices, slab, total)


def within_kernel(width, act_ref, within_ref):
    tokens, columns = act_ref.shape
    causal = lax.broadcasted_iota(jnp.int32, (tokens, tokens), 0) >= lax.broadcasted_iota(
        jnp.int32, (tokens, tokens), 1
    )
    for h in range(columns // (PARTS * width)):
        at = h * PARTS * width
        queries = act_ref[:, at : at + width]
        keys = act_ref[:, at + width : at + 2 * width]
        values = act_ref[:, at + 2 * width : at + 3 * width]
        scores = lax.dot_general(
            queries, keys, (((1,), (1,)), ((), ())), preferred_element_type=F32
        )
        scores = jnp.where(causal, scores, 0.0).astype(BF16)
        within_ref[:, h * width : (h + 1) * width] = jnp.dot(
            scores, values, preferred_element_type=F32
        )


def attend_within(act, width):
    tokens, columns = act.shape
    heads = columns // (PARTS * width)
    return pl.pallas_call(
        functools.partial(within_kernel, width),
        out_shape=pltpu.VMEM((tokens, heads * width), F32),
        in_specs=[WHOLE],
        out_specs=WHOLE,
        compiler_params=params(),
        cost_estimate=pl.CostEstimate(
            flops=4 * heads * tokens * tokens * width,
            bytes_accessed=tokens * columns * 2,
            transcendentals=0,
        ),
        name="within",
    )(act)


def across_kernel(info, act, within, prior, mine, other, att_ref, square_ref):
    width = prior.shape[1]
    half = mine.shape[0]
    squares = None
    for step in range(half):
        for side, earlier in ((info[0], mine), (1 - info[0], other)):
            head = side * half + step
            carried = prior[head] + earlier[step]
            upper = carried.astype(BF16)
            lower = (carried - upper.astype(F32)).astype(BF16)
            queries = act[:, pl.ds(pl.multiple_of(head * (PARTS * width), width), width)]
            columns = pl.ds(pl.multiple_of(head * width, width), width)
            attended = within[:, columns] + jnp.dot(
                jnp.concatenate([queries, queries], axis=1),
                jnp.concatenate([upper, lower], axis=0),
                preferred_element_type=F32,
            )
            att_ref[:, columns] = attended
            square = attended * attended
            squares = square if squares is None else squares + square
    square_ref[...] = lax.dot_general(
        jnp.ones((8, width), F32),
        squares,
        (((1,), (1,)), ((), ())),
        preferred_element_type=F32,
        precision=lax.Precision.HIGHEST,
    )


def attend_across(info, act, within, prior, mine, other):
    tokens = act.shape[0]
    heads, width, _ = prior.shape
    return pl.pallas_call(
        across_kernel,
        out_shape=(
            pltpu.VMEM((tokens, heads * width), F32),
            jax.ShapeDtypeStruct((8, tokens), F32),
        ),
        in_specs=[pl.BlockSpec(memory_space=pltpu.SMEM)] + [WHOLE] * 5,
        out_specs=(WHOLE, WHOLE),
        input_output_aliases={2: 0},
        compiler_params=params(),
        cost_estimate=pl.CostEstimate(
            flops=4 * heads * tokens * width * width, bytes_accessed=0, transcendentals=0
        ),
        name="across",
    )(info, act, within, prior, mine, other)


def norm_kernel(features, att_ref, square_ref, gain_ref, out_ref):
    ones = jnp.ones((square_ref.shape[0], 128), F32)
    mean_sq = lax.dot_general(
        square_ref[...] * (1.0 / square_ref.shape[0] / features),
        ones,
        (((0,), (0,)), ((), ())),
        preferred_element_type=F32,
        precision=lax.Precision.HIGHEST,
    )
    inverse = lax.rsqrt(mean_sq + EPSILON)
    for at in range(0, att_ref.shape[1], 128):
        out_ref[:, at : at + 128] = (
            att_ref[:, at : at + 128] * inverse * gain_ref[:, at : at + 128]
        ).astype(BF16)


def normalize(att, squares, gain, features):
    tokens, columns = att.shape
    return pl.pallas_call(
        functools.partial(norm_kernel, features),
        out_shape=jax.ShapeDtypeStruct((tokens, columns), BF16),
        in_specs=[WHOLE] * 3,
        out_specs=WHOLE,
        compiler_params=params(),
        cost_estimate=pl.CostEstimate(
            flops=2 * tokens * columns, bytes_accessed=2 * tokens * columns, transcendentals=0
        ),
        name="normalize",
    )(att, squares, gain[None, :])


def sum_over_tensor(x, n):
    if n & (n - 1):
        return lax.psum(x, "tensor")
    bit = 1
    while bit < n:
        x = x + lax.ppermute(x, "tensor", [(i, i ^ bit) for i in range(n)])
        bit *= 2
    return x


def earlier_states(states, n):
    half = states.shape[0] // 2
    index = lax.axis_index("context")
    core, chip, chips = index % 2, index // 2, n // 2
    swap = [(i, i ^ 1) for i in range(n)]
    own = states[half:]
    theirs = lax.ppermute(states[:half], "context", swap)
    total = own + theirs
    before = jnp.zeros_like(own)
    bit = 1
    while bit < chips:
        last = bit * 2 >= chips
        pairs = [
            (2 * i + c, 2 * (i ^ bit) + c)
            for i in range(chips)
            for c in range(2)
            if not (last and i & bit)
        ]
        arrived = lax.ppermute(total.astype(BF16), "context", pairs).astype(F32)
        before = before + (arrived if last else jnp.where(chip & bit, arrived, 0.0))
        total = total + arrived
        bit *= 2
    for_mate = before + jnp.where(core == 0, own, 0.0)
    mine = before + jnp.where(core == 1, theirs, 0.0)
    other = lax.ppermute(for_mate, "context", swap)
    return mine, other


def body(n_tensor, n_context, tokens_t, qkv_weight, prior_state, norm_gain):
    share = tokens_t.shape[0]
    heads, width, _ = prior_state.shape
    place = lax.axis_index("tensor")
    core = lax.axis_index("context") % 2

    piece = share // CHUNKS
    left = [[tokens_t[j * piece : (j + 1) * piece] for j in range(CHUNKS)]]
    right = [left[0]]
    for s in range(1, n_tensor):
        up = [(i, i + 1) for i in range(s - 1, n_tensor - 1)]
        down = [(i, i - 1) for i in range(1, n_tensor - s + 1)]
        left.append([])
        right.append([])
        for j in range(CHUNKS):
            left[s].append(lax.ppermute(left[s - 1][j], "tensor", up))
            right[s].append(lax.ppermute(right[s - 1][j], "tensor", down))

    def ints(*values):
        return jnp.stack([jnp.asarray(v, jnp.int32) for v in values])

    def source(m):
        return jnp.where(place >= m, place - m, m)

    last = n_tensor - 1
    piece_last = source(last) * CHUNKS + CHUNKS - 1
    total, slab = project(
        [[tokens_t]], ints(0, place, piece_last), qkv_weight, None, ahead=piece
    )
    for m in range(1, n_tensor):
        pick = jnp.where(place >= m, 0, m - place)
        choices = [left[m]] + [right[s] for s in range(1, m + 1)]
        if m < last:
            total = project(choices, ints(pick, source(m)), qkv_weight, total)
        else:
            for j in range(CHUNKS - 1):
                one = [[c[j]] for c in choices]
                total = project(one, ints(pick, source(m) * CHUNKS + j), qkv_weight, total)
            one = [c[CHUNKS - 1] for c in choices]
            shift = jnp.where(core == 0, heads // 2, 0)
            act, states = activate(one, ints(pick, shift), slab, total, width)
    mine, other = earlier_states(states, n_context)
    within = attend_within(act, width)
    att, squares = attend_across(ints(core), act, within, prior_state, mine, other)
    squares = sum_over_tensor(squares, n_tensor)
    return normalize(att, squares, norm_gain, n_tensor * heads * width)


def solution(mesh):
    n_tensor, n_context = mesh.shape["tensor"], mesh.shape["context"]
    in_specs = (P("tensor", "context"), P(None, "tensor"), P("tensor", None, None), P("tensor"))
    return jax.shard_map(
        functools.partial(body, n_tensor, n_context),
        mesh=mesh,
        in_specs=in_specs,
        out_specs=P("context", "tensor"),
        check_vma=False,
    )
```

time: 194 us -> 118 us (0.61)
  waiting for transfers between devices: 119 us -> 22.9 us
  Pallas kernels: 0 us -> 45.2 us
  matrix products: 38.1 us -> 0 us
  starting transfers between devices: 0.04 us -> 37.3 us
  between operations: 13.5 us -> 0.31 us
  blocking collectives: 11.8 us -> 0 us
  local copies, waits for them, and re-layouts: 5.1 us -> 9.69 us
  other arithmetic: 5.98 us -> 2.51 us
    all_gather x2 -> x0, waiting for transfers between devices: 118 us -> none  [the longest x1 67.9 us: body(): lax.all_gather(tokens_t, 'tensor', axis=0, tiled=True)]
    pallas_call x0 -> x8, Pallas kernels: none -> 45.2 us  [the longest x4 33.5 us: project(): pl.pallas_call(functools.partial(project_kernel, n_choices, n_pieces, fir...]
    dot_general x4 -> x0, matrix products: 38.1 us -> none  [the longest x1 31.3 us: body(): lax.dot_general(lax.all_gather(tokens_t, 'tensor', axis=0, tiled=True), q...]
    ppermute x0 -> x18, starting transfers between devices: none -> 37.3 us  [the longest x6 12.9 us: body(): left[s].append(lax.ppermute(left[s - 1][j], 'tensor', up))]
    ppermute x0 -> x18, waiting for transfers between devices: none -> 22.9 us  [the longest x2 11.2 us: earlier_states(): arrived = lax.ppermute(total.astype(BF16), 'context', pairs).astype(F32)]
    psum x1 -> x0, blocking collectives: 11.8 us -> none  [body(): square_sum = lax.psum(jnp.sum(attended * attended, axis=1), 'tensor')]
    unnamed x6 -> x14, local copies, waits for them, and re-layouts: 0.01 us -> 8.49 us
    reduce_sum x1 -> x0, other arithmetic: 4.72 us -> none  [body(): earlier = jnp.sum(keep_rows[:, None, None, None] * block_part, axis=0)]
  transfers between devices with their start and end apart: 2 -> 18, of which waited for: 2 -> 10; matrix products, arithmetic and copies ran while one was open for 1% -> 0% of each run, Pallas kernels for 0% -> 30%
where the time goes in v1:
time: 118 us
  Pallas kernels  45.2 us (38%)
  starting transfers between devices  37.3 us (32%)
  waiting for transfers between devices  22.9 us (19%)
  local copies, waits for them, and re-layouts  9.69 us (8%)
  other arithmetic  2.51 us (2%)
    pallas_call x4, Pallas kernels, project(): pl.pallas_call(functools.partial(project_kernel, n_choices, n_pieces, fir...  33.5 us
    ppermute x6, starting transfers between devices, body(): left[s].append(lax.ppermute(left[s - 1][j], 'tensor', up))  12.9 us
    ppermute x2, waiting for transfers between devices, earlier_states(): arrived = lax.ppermute(total.astype(BF16), 'context', pairs).astype(F32)  11.2 us
    ppermute x2, starting transfers between devices, sum_over_tensor(): x = x + lax.ppermute(x, 'tensor', [(i, i ^ bit) for i in range(n)])  10.2 us
    unnamed x14, local copies, waits for them, and re-layouts  8.49 us
    ppermute x6, starting transfers between devices, body(): right[s].append(lax.ppermute(right[s - 1][j], 'tensor', down))  7.72 us
    pallas_call x1, Pallas kernels, activate(): pl.pallas_call(functools.partial(activate_kernel, len(choices), width), o...  7.3 us
    ppermute x2, starting transfers between devices, earlier_states(): arrived = lax.ppermute(total.astype(BF16), 'context', pairs).astype(F32)  6.34 us
  transfers between devices with their start and end apart: 18, of which 10 were waited for; matrix products, arithmetic and copies ran while one was open for 0% of the time, Pallas kernels for 30%

profile of v1, /device:TPU:0, one launch (start us, length us, event | category | flops | bytes accessed | tf_op | source)
XLA Modules:
  0.0 118.0 jit_solution(3000244752607886061)
XLA Ops:
  0.0 1.2 fusion.3
  1.2 1.3 %collective-permute-start.3 = (bf16[768,256]{1,0:T(8,128)(2,1)S(1)}, bf16[768,256]{1,0:T(8,128)(2,1)S(1)}, u32[]{:S(2)}, u32[]{:S(2)}) collective-permute-start(bf16[768,256]{1,0:T(8,128)(2,1)S(1)} %get-tuple-element.18), channel_id=1, source_target_pairs={{1,0},{2,1},{3,2},{5,4},{6,5},{7,6},{9,8},{10,9},{11,10},{13,12},{... | collective-permute-start | bytes 1179656 | tf_op jit(solution)/shard_map/ppermute | solution.py:351
  2.5 5.6 %collective-permute-start = (bf16[768,256]{1,0:T(8,128)(2,1)S(1)}, bf16[768,256]{1,0:T(8,128)(2,1)S(1)}, u32[]{:S(2)}, u32[]{:S(2)}) collective-permute-start(bf16[768,256]{1,0:T(8,128)(2,1)S(1)} %get-tuple-element.18), channel_id=1, source_target_pairs={{0,1},{1,2},{2,3},{4,5},{5,6},{6,7},{8,9},{9,10},{10,11},{12,13},{... | collective-permute-start | bytes 1179656 | tf_op jit(solution)/shard_map/ppermute | solution.py:350
  8.1 1.3 %collective-permute-start.9 = (bf16[768,256]{1,0:T(8,128)(2,1)S(1)}, bf16[768,256]{1,0:T(8,128)(2,1)S(1)}, u32[]{:S(2)}, u32[]{:S(2)}) collective-permute-start(bf16[768,256]{1,0:T(8,128)(2,1)S(1)} %get-tuple-element.17), channel_id=1, source_target_pairs={{1,0},{2,1},{3,2},{5,4},{6,5},{7,6},{9,8},{10,9},{11,10},{13,12},{... | collective-permute-start | bytes 1179656 | tf_op jit(solution)/shard_map/ppermute | solution.py:351
  9.4 4.6 %collective-permute-start.6 = (bf16[768,256]{1,0:T(8,128)(2,1)S(1)}, bf16[768,256]{1,0:T(8,128)(2,1)S(1)}, u32[]{:S(2)}, u32[]{:S(2)}) collective-permute-start(bf16[768,256]{1,0:T(8,128)(2,1)S(1)} %get-tuple-element.17), channel_id=1, source_target_pairs={{0,1},{1,2},{2,3},{4,5},{5,6},{6,7},{8,9},{9,10},{10,11},{12,13},{... | collective-permute-start | bytes 1179656 | tf_op jit(solution)/shard_map/ppermute | solution.py:350
  14.0 0.1 pad_add_fusion.2.info
  14.1 0.1 pad_add_fusion.info
  14.1 0.1 pad_add_fusion.4.info
  14.2 0.1 pad_add_fusion.3.info
  14.3 0.1 pad_add_fusion.1.info
  14.4 1.1 copy-done.3
  15.5 9.9 %project.4 = (f32[256,6144]{1,0:T(8,128)S(1)}, bf16[768,6144]{1,0:T(8,128)(2,1)S(1)}) custom-call(s32[3]{0:T(128)S(1)} %pad_add_fusion.1.info, bf16[1536,256]{1,0:T(8,128)(2,1)S(1)} %copy-done.3, bf16[6144,6144]{1,0:T(8,128)(2,1)} %refs_4_.3), custom_call_target="tpu_custom_call" | custom-call | flops 4831838208 | bytes 29097984 | tf_op jit(solution)/shard_map/project/pallas_call | solution.py:104
  25.4 3.7 %copy-done = bf16[768,6144]{1,0:T(8,128)(2,1)} copy-done((bf16[768,6144]{1,0:T(8,128)(2,1)}, bf16[768,6144]{1,0:T(8,128)(2,1)S(1)}, u32[]{:S(2)}) %copy-start) | copy-done | bytes 9437208
  29.0 1.3 %collective-permute-start.10 = (bf16[768,256]{1,0:T(8,128)(2,1)S(1)}, bf16[768,256]{1,0:T(8,128)(2,1)S(1)}, u32[]{:S(2)}, u32[]{:S(2)}) collective-permute-start(bf16[768,256]{1,0:T(8,128)(2,1)S(1)} %collective-permute-done.9.refs_2_.refs_1_), channel_id=1, source_target_pairs={{1,0},{2,1},{5,4},{6,5},{9,8},{10,9},{13,12},{14,13},{17,16},{18,1... | collective-permute-start | bytes 1179656 | tf_op jit(solution)/shard_map/ppermute | solution.py:351
  30.3 1.3 %collective-permute-start.4 = (bf16[768,256]{1,0:T(8,128)(2,1)S(1)}, bf16[768,256]{1,0:T(8,128)(2,1)S(1)}, u32[]{:S(2)}, u32[]{:S(2)}) collective-permute-start(bf16[768,256]{1,0:T(8,128)(2,1)S(1)} %collective-permute-done.3.refs_3_.refs_1_), channel_id=1, source_target_pairs={{1,0},{2,1},{5,4},{6,5},{9,8},{10,9},{13,12},{14,13},{17,16},{18,1... | collective-permute-start | bytes 1179656 | tf_op jit(solution)/shard_map/ppermute | solution.py:351
  31.7 0.7 collective-permute-start.1
  32.4 0.7 collective-permute-start.7
  33.1 8.8 %project.5.refs_7_ = f32[256,6144]{1,0:T(8,128)S(1)} custom-call(s32[2]{0:T(128)S(1)} %pad_add_fusion.4.info, bf16[768,256]{1,0:T(8,128)(2,1)S(1)} %collective-permute-done.6.refs_0_, bf16[768,256]{1,0:T(8,128)(2,1)S(1)} %collective-permute-done.refs_1_, bf16[768,256]{1,0:T(8,128)(2,1)S(1)} %collective-permute-done.9.refs_2_.refs_1_, ...), custom_call_target="tpu_custom_call", output_to_operand_aliasing={{}: (6, {})} | custom-call | flops 4831838208 | bytes 19660800 | tf_op jit(solution)/shard_map/project/pallas_call | solution.py:104
  41.9 1.1 collective-permute-done.10.refs_4_.refs_2_
  43.0 1.3 %collective-permute-start.11 = (bf16[768,256]{1,0:T(8,128)(2,1)S(1)}, bf16[768,256]{1,0:T(8,128)(2,1)S(1)}, u32[]{:S(2)}, u32[]{:S(2)}) collective-permute-start(bf16[768,256]{1,0:T(8,128)(2,1)S(1)} %collective-permute-done.10.refs_4_.refs_2_), channel_id=1, source_target_pairs={{1,0},{5,4},{9,8},{13,12},{17,16},{21,20},{25,24},{29,28}} | collective-permute-start | bytes 1179656 | tf_op jit(solution)/shard_map/ppermute | solution.py:351
  44.3 0.7 collective-permute-start.8
  45.0 4.4 %collective-permute-done.4.refs_5_.refs_2_ = bf16[768,256]{1,0:T(8,128)(2,1)S(1)} collective-permute-done((bf16[768,256]{1,0:T(8,128)(2,1)S(1)}, bf16[768,256]{1,0:T(8,128)(2,1)S(1)}, u32[]{:S(2)}, u32[]{:S(2)}) %collective-permute-start.4) | collective-permute-done | bytes 393248 | tf_op jit(solution)/shard_map/ppermute | solution.py:351
  49.4 1.3 %collective-permute-start.5 = (bf16[768,256]{1,0:T(8,128)(2,1)S(1)}, bf16[768,256]{1,0:T(8,128)(2,1)S(1)}, u32[]{:S(2)}, u32[]{:S(2)}) collective-permute-start(bf16[768,256]{1,0:T(8,128)(2,1)S(1)} %collective-permute-done.4.refs_5_.refs_2_), channel_id=1, source_target_pairs={{1,0},{5,4},{9,8},{13,12},{17,16},{21,20},{25,24},{29,28}} | collective-permute-start | bytes 1179656 | tf_op jit(solution)/shard_map/ppermute | solution.py:351
  50.7 0.7 collective-permute-start.2
  51.4 9.0 %project.6.refs_5_ = f32[256,6144]{1,0:T(8,128)S(1)} custom-call(s32[2]{0:T(128)S(1)} %pad_add_fusion.3.info, bf16[768,256]{1,0:T(8,128)(2,1)S(1)} %collective-permute-done.7.refs_0_, bf16[768,256]{1,0:T(8,128)(2,1)S(1)} %collective-permute-done.1.refs_1_, ...), custom_call_target="tpu_custom_call", output_to_operand_aliasing={{}: (8, {})} | custom-call | flops 4831838208 | bytes 19660800 | tf_op jit(solution)/shard_map/project/pallas_call | solution.py:104
  60.4 0.6 collective-permute-done.11.refs_3_
  61.0 5.8 %project.7.refs_5_ = f32[256,6144]{1,0:T(8,128)S(1)} custom-call(s32[2]{0:T(128)S(1)} %pad_add_fusion.2.info, bf16[768,256]{1,0:T(8,128)(2,1)S(1)} %collective-permute-done.8.refs_0_, bf16[768,256]{1,0:T(8,128)(2,1)S(1)} %collective-permute-done.9.refs_2_.refs_1_, ...), custom_call_target="tpu_custom_call", output_to_operand_aliasing={{}: (6, {})} | custom-call | flops 2415919104 | bytes 9830400 | tf_op jit(solution)/shard_map/project/pallas_call | solution.py:104
  66.8 0.1 collective-permute-done.5.refs_3_
  66.8 3.7 %copy-done.1 = bf16[768,6144]{1,0:T(8,128)(2,1)S(1)} copy-done((bf16[768,6144]{1,0:T(8,128)(2,1)S(1)}, bf16[768,6144]{1,0:T(8,128)(2,1)}, u32[]{:S(2)}) %copy-start.1) | copy-done | bytes 9437208
  70.5 7.3 %activate.1 = (bf16[256,6144]{1,0:T(8,128)(2,1)S(1)}, f32[16,128,128]{2,1,0:T(8,128)S(1)}) custom-call(s32[2]{0:T(128)S(1)} %pad_add_fusion.info, bf16[768,256]{1,0:T(8,128)(2,1)S(1)} %collective-permute-done.2.refs_0_, bf16[768,256]{1,0:T(8,128)(2,1)S(1)} %collective-permute-done.3.refs_3_.refs_1_, ...), custom_call_target="tpu_custom_call" | custom-call | flops 2550136832 | bytes 393216 | tf_op jit(solution)/shard_map/activate/pallas_call | solution.py:157
  77.9 0.1 collective-permute-start.12
  78.0 1.9 %collective-permute-done.12 = f32[8,128,128]{2,1,0:T(8,128)S(1)} collective-permute-done((f32[8,128,128]{2,1,0:T(8,128)S(1)}, f32[8,128,128]{2,1,0:T(8,128)S(1)}, u32[]{:S(2)}, u32[]{:S(2)}) %collective-permute-start.12) | collective-permute-done | bytes 524320 | tf_op jit(solution)/shard_map/ppermute | solution.py:313
  79.9 0.1 fusion.2
  79.9 2.0 %collective-permute-start.13 = (bf16[8,128,128]{2,1,0:T(8,128)(2,1)S(1)}, bf16[8,128,128]{2,1,0:T(8,128)(2,1)S(1)}, u32[]{:S(2)}, u32[]{:S(2)}) collective-permute-start(bf16[8,128,128]{2,1,0:T(8,128)(2,1)S(1)} %fusion.2), channel_id=1, source_target_pairs={{0,8},{4,12},{8,0},{12,4},{16,24},{20,28},{24,16},{28,20},{1,9},{5... | collective-permute-start | bytes 786440 | tf_op jit(solution)/shard_map/ppermute | solution.py:325
  81.9 6.6 %collective-permute-done.13 = bf16[8,128,128]{2,1,0:T(8,128)(2,1)S(1)} collective-permute-done((bf16[8,128,128]{2,1,0:T(8,128)(2,1)S(1)}, bf16[8,128,128]{2,1,0:T(8,128)(2,1)S(1)}, u32[]{:S(2)}, u32[]{:S(2)}) %collective-permute-start.13) | collective-permute-done | bytes 262176 | tf_op jit(solution)/shard_map/ppermute | solution.py:325
  88.5 0.8 fusion.1
  89.3 4.4 %collective-permute-start.14 = (bf16[8,128,128]{2,1,0:T(8,128)(2,1)}, bf16[8,128,128]{2,1,0:T(8,128)(2,1)}, u32[]{:S(2)}, u32[]{:S(2)}) collective-permute-start(bf16[8,128,128]{2,1,0:T(8,128)(2,1)} %fusion.1), channel_id=1, source_target_pairs={{0,16},{4,20},{8,24},{12,28},{1,17},{5,21},{9,25},{13,29},{2,18},{... | collective-permute-start | bytes 786440 | tf_op jit(solution)/shard_map/ppermute | solution.py:325
  93.7 4.6 %collective-permute-done.14 = bf16[8,128,128]{2,1,0:T(8,128)(2,1)} collective-permute-done((bf16[8,128,128]{2,1,0:T(8,128)(2,1)}, bf16[8,128,128]{2,1,0:T(8,128)(2,1)}, u32[]{:S(2)}, u32[]{:S(2)}) %collective-permute-start.14) | collective-permute-done | bytes 262176 | tf_op jit(solution)/shard_map/ppermute | solution.py:325
  98.3 1.3 %select_add_fusion = (f32[8,128,128]{2,1,0:T(8,128)S(1)}, f32[8,128,128]{2,1,0:T(8,128)S(1)}) fusion(f32[16,128,128]{2,1,0:T(8,128)} %copy-done.2, bf16[8,128,128]{2,1,0:T(8,128)(2,1)} %collective-permute-done.14, bf16[8,128,128]{2,1,0:T(8,128)(2,1)S(1)} %collective-permute-done.13, pred[]{:T(512)S(6)} %eq.10, pred[]{:T(512)S(6)} %ne.20, ...), kind=kLoop, calls=%fused_computation.4 | loop fusion | flops 1048576 | bytes 2621443 | tf_op jit(solution)/shard_map/add | solution.py:329
  99.6 0.1 collective-permute-start.15
  99.7 1.5 %within.1 = f32[256,2048]{1,0:T(8,128)S(1)} custom-call(bf16[256,6144]{1,0:T(8,128)(2,1)S(1)} %get-tuple-element.13.act_ref.act), custom_call_target="tpu_custom_call" | custom-call | flops 536870912 | bytes 3145728 | tf_op jit(solution)/shard_map/within/pallas_call | solution.py:202
  101.2 0.4 collective-permute-done.15.other
  101.6 1.4 %across.1 = (f32[256,2048]{1,0:T(8,128)S(1)}, f32[8,256]{1,0:T(8,128)S(1)}) custom-call(s32[1]{0:T(128)} %bitcast.info, bf16[256,6144]{1,0:T(8,128)(2,1)S(1)} %get-tuple-element.13.act_ref.act, f32[256,2048]{1,0:T(8,128)S(1)} %within.1, f32[16,128,128]{2,1,0:T(8,128)S(1)} %copy-done.4, ...), custom_call_target="tpu_custom_call", output_to_operand_aliasing={{0}: (2, {})} | custom-call | flops 268435456 | tf_op jit(solution)/shard_map/across/pallas_call | solution.py:249
  103.0 4.8 %collective-permute-start.16 = (f32[8,256]{1,0:T(8,128)S(1)}, f32[8,256]{1,0:T(8,128)S(1)}, u32[]{:S(2)}, u32[]{:S(2)}) collective-permute-start(f32[8,256]{1,0:T(8,128)S(1)} %get-tuple-element.16), channel_id=1, source_target_pairs={{0,1},{1,0},{2,3},{3,2},{4,5},{5,4},{6,7},{7,6},{8,9},{9,8},{10,11... | collective-permute-start | bytes 24584 | tf_op jit(solution)/shard_map/ppermute | solution.py:302
  107.7 1.6 %collective-permute-done.16 = f32[8,256]{1,0:T(8,128)S(1)} collective-permute-done((f32[8,256]{1,0:T(8,128)S(1)}, f32[8,256]{1,0:T(8,128)S(1)}, u32[]{:S(2)}, u32[]{:S(2)}) %collective-permute-start.16) | collective-permute-done | bytes 8224 | tf_op jit(solution)/shard_map/ppermute | solution.py:302
  109.4 5.5 %collective-permute-start.17 = (f32[8,256]{1,0:T(8,128)S(1)}, f32[8,256]{1,0:T(8,128)S(1)}, u32[]{:S(2)}, u32[]{:S(2)}) collective-permute-start(f32[8,256]{1,0:T(8,128)S(1)} %add.40), channel_id=1, source_target_pairs={{0,2},{1,3},{2,0},{3,1},{4,6},{5,7},{6,4},{7,5},{8,10},{9,11},{10,... | collective-permute-start | bytes 24584 | tf_op jit(solution)/shard_map/ppermute | solution.py:302
  114.8 1.6 %collective-permute-done.17 = f32[8,256]{1,0:T(8,128)S(1)} collective-permute-done((f32[8,256]{1,0:T(8,128)S(1)}, f32[8,256]{1,0:T(8,128)S(1)}, u32[]{:S(2)}, u32[]{:S(2)}) %collective-permute-start.17) | collective-permute-done | bytes 8224 | tf_op jit(solution)/shard_map/ppermute | solution.py:302
  116.5 1.5 %normalize.1 = bf16[256,2048]{1,0:T(8,128)(2,1)} custom-call(f32[256,2048]{1,0:T(8,128)S(1)} %get-tuple-element.15.att_ref, f32[8,256]{1,0:T(8,128)S(1)} %add.41.square_ref, f32[1,2048]{1,0:T(1,128)S(1)} %bitcast.11), custom_call_target="tpu_custom_call" | custom-call | flops 1048576 | bytes 1048576 | tf_op jit(solution)/shard_map/normalize/pallas_call | solution.py:284
  (22 shorter events, 0.1 us)
Async XLA Ops:
  1.2 29.2 %collective-permute-start.3 = (bf16[768,256]{1,0:T(8,128)(2,1)S(1)}, bf16[768,256]{1,0:T(8,128)(2,1)S(1)}, u32[]{:S(2)}, u32[]{:S(2)}) collective-permute-start(bf16[768,256]{1,0:T(8,128)(2,1)S(1)} %get-tuple-element.18), channel_id=1, source_target_pairs={{1,0},{2,1},{3,2},{5,4},{6,5},{7,6},{9,8},{10,9},{11,10},{13,12},{... | collective-permute-start | bytes 1179656 | tf_op jit(solution)/shard_map/ppermute | solution.py:351
  2.5 29.2 %collective-permute-start = (bf16[768,256]{1,0:T(8,128)(2,1)S(1)}, bf16[768,256]{1,0:T(8,128)(2,1)S(1)}, u32[]{:S(2)}, u32[]{:S(2)}) collective-permute-start(bf16[768,256]{1,0:T(8,128)(2,1)S(1)} %get-tuple-element.18), channel_id=1, source_target_pairs={{0,1},{1,2},{2,3},{4,5},{5,6},{6,7},{8,9},{9,10},{10,11},{12,13},{... | collective-permute-start | bytes 1179656 | tf_op jit(solution)/shard_map/ppermute | solution.py:350
  8.1 21.0 %collective-permute-start.9 = (bf16[768,256]{1,0:T(8,128)(2,1)S(1)}, bf16[768,256]{1,0:T(8,128)(2,1)S(1)}, u32[]{:S(2)}, u32[]{:S(2)}) collective-permute-start(bf16[768,256]{1,0:T(8,128)(2,1)S(1)} %get-tuple-element.17), channel_id=1, source_target_pairs={{1,0},{2,1},{3,2},{5,4},{6,5},{7,6},{9,8},{10,9},{11,10},{13,12},{... | collective-permute-start | bytes 1179656 | tf_op jit(solution)/shard_map/ppermute | solution.py:351
  9.4 23.0 %collective-permute-start.6 = (bf16[768,256]{1,0:T(8,128)(2,1)S(1)}, bf16[768,256]{1,0:T(8,128)(2,1)S(1)}, u32[]{:S(2)}, u32[]{:S(2)}) collective-permute-start(bf16[768,256]{1,0:T(8,128)(2,1)S(1)} %get-tuple-element.17), channel_id=1, source_target_pairs={{0,1},{1,2},{2,3},{4,5},{5,6},{6,7},{8,9},{9,10},{10,11},{12,13},{... | collective-permute-start | bytes 1179656 | tf_op jit(solution)/shard_map/ppermute | solution.py:350
  14.4 1.1 copy-start.3
  25.4 3.7 %copy-start = (bf16[768,6144]{1,0:T(8,128)(2,1)}, bf16[768,6144]{1,0:T(8,128)(2,1)S(1)}, u32[]{:S(2)}) copy-start(bf16[768,6144]{1,0:T(8,128)(2,1)S(1)} %get-tuple-element.11.refs_4_) | copy-start | bytes 28311556
  29.0 13.9 %collective-permute-start.10 = (bf16[768,256]{1,0:T(8,128)(2,1)S(1)}, bf16[768,256]{1,0:T(8,128)(2,1)S(1)}, u32[]{:S(2)}, u32[]{:S(2)}) collective-permute-start(bf16[768,256]{1,0:T(8,128)(2,1)S(1)} %collective-permute-done.9.refs_2_.refs_1_), channel_id=1, source_target_pairs={{1,0},{2,1},{5,4},{6,5},{9,8},{10,9},{13,12},{14,13},{17,16},{18,1... | collective-permute-start | bytes 1179656 | tf_op jit(solution)/shard_map/ppermute | solution.py:351
  30.3 19.0 %collective-permute-start.4 = (bf16[768,256]{1,0:T(8,128)(2,1)S(1)}, bf16[768,256]{1,0:T(8,128)(2,1)S(1)}, u32[]{:S(2)}, u32[]{:S(2)}) collective-permute-start(bf16[768,256]{1,0:T(8,128)(2,1)S(1)} %collective-permute-done.3.refs_3_.refs_1_), channel_id=1, source_target_pairs={{1,0},{2,1},{5,4},{6,5},{9,8},{10,9},{13,12},{14,13},{17,16},{18,1... | collective-permute-start | bytes 1179656 | tf_op jit(solution)/shard_map/ppermute | solution.py:351
  31.7 19.0 %collective-permute-start.1 = (bf16[768,256]{1,0:T(8,128)(2,1)S(1)}, bf16[768,256]{1,0:T(8,128)(2,1)S(1)}, u32[]{:S(2)}, u32[]{:S(2)}) collective-permute-start(bf16[768,256]{1,0:T(8,128)(2,1)S(1)} %collective-permute-done.refs_1_), channel_id=1, source_target_pairs={{1,2},{2,3},{5,6},{6,7},{9,10},{10,11},{13,14},{14,15},{17,18},{18... | collective-permute-start | bytes 1179656 | tf_op jit(solution)/shard_map/ppermute | solution.py:350
  32.4 11.9 %collective-permute-start.7 = (bf16[768,256]{1,0:T(8,128)(2,1)S(1)}, bf16[768,256]{1,0:T(8,128)(2,1)S(1)}, u32[]{:S(2)}, u32[]{:S(2)}) collective-permute-start(bf16[768,256]{1,0:T(8,128)(2,1)S(1)} %collective-permute-done.6.refs_0_), channel_id=1, source_target_pairs={{1,2},{2,3},{5,6},{6,7},{9,10},{10,11},{13,14},{14,15},{17,18},{18... | collective-permute-start | bytes 1179656 | tf_op jit(solution)/shard_map/ppermute | solution.py:350
  43.0 18.0 %collective-permute-start.11 = (bf16[768,256]{1,0:T(8,128)(2,1)S(1)}, bf16[768,256]{1,0:T(8,128)(2,1)S(1)}, u32[]{:S(2)}, u32[]{:S(2)}) collective-permute-start(bf16[768,256]{1,0:T(8,128)(2,1)S(1)} %collective-permute-done.10.refs_4_.refs_2_), channel_id=1, source_target_pairs={{1,0},{5,4},{9,8},{13,12},{17,16},{21,20},{25,24},{29,28}} | collective-permute-start | bytes 1179656 | tf_op jit(solution)/shard_map/ppermute | solution.py:351
  44.3 16.7 %collective-permute-start.8 = (bf16[768,256]{1,0:T(8,128)(2,1)S(1)}, bf16[768,256]{1,0:T(8,128)(2,1)S(1)}, u32[]{:S(2)}, u32[]{:S(2)}) collective-permute-start(bf16[768,256]{1,0:T(8,128)(2,1)S(1)} %collective-permute-done.7.refs_0_), channel_id=1, source_target_pairs={{2,3},{6,7},{10,11},{14,15},{18,19},{22,23},{26,27},{30,31}} | collective-permute-start | bytes 1179656 | tf_op jit(solution)/shard_map/ppermute | solution.py:350
  49.4 17.5 %collective-permute-start.5 = (bf16[768,256]{1,0:T(8,128)(2,1)S(1)}, bf16[768,256]{1,0:T(8,128)(2,1)S(1)}, u32[]{:S(2)}, u32[]{:S(2)}) collective-permute-start(bf16[768,256]{1,0:T(8,128)(2,1)S(1)} %collective-permute-done.4.refs_5_.refs_2_), channel_id=1, source_target_pairs={{1,0},{5,4},{9,8},{13,12},{17,16},{21,20},{25,24},{29,28}} | collective-permute-start | bytes 1179656 | tf_op jit(solution)/shard_map/ppermute | solution.py:351
  50.7 16.2 %collective-permute-start.2 = (bf16[768,256]{1,0:T(8,128)(2,1)S(1)}, bf16[768,256]{1,0:T(8,128)(2,1)S(1)}, u32[]{:S(2)}, u32[]{:S(2)}) collective-permute-start(bf16[768,256]{1,0:T(8,128)(2,1)S(1)} %collective-permute-done.1.refs_1_), channel_id=1, source_target_pairs={{2,3},{6,7},{10,11},{14,15},{18,19},{22,23},{26,27},{30,31}} | collective-permute-start | bytes 1179656 | tf_op jit(solution)/shard_map/ppermute | solution.py:350
  66.8 3.7 %copy-start.1 = (bf16[768,6144]{1,0:T(8,128)(2,1)S(1)}, bf16[768,6144]{1,0:T(8,128)(2,1)}, u32[]{:S(2)}) copy-start(bf16[768,6144]{1,0:T(8,128)(2,1)} %copy-done) | copy-start | bytes 28311556
  77.8 10.7 %copy-start.2 = (f32[16,128,128]{2,1,0:T(8,128)}, f32[16,128,128]{2,1,0:T(8,128)S(1)}, u32[]{:S(2)}) copy-start(f32[16,128,128]{2,1,0:T(8,128)S(1)} %get-tuple-element.14) | copy-start | bytes 3145732
  77.9 2.0 %collective-permute-start.12 = (f32[8,128,128]{2,1,0:T(8,128)S(1)}, f32[8,128,128]{2,1,0:T(8,128)S(1)}, u32[]{:S(2)}, u32[]{:S(2)}) collective-permute-start(f32[8,128,128]{2,1,0:T(8,128)S(1)} %slice.15), channel_id=1, source_target_pairs={{0,4},{4,0},{8,12},{12,8},{16,20},{20,16},{24,28},{28,24},{1,5},{5... | collective-permute-start | bytes 1572872 | tf_op jit(solution)/shard_map/ppermute | solution.py:313
  79.9 9.5 %copy-start.6 = (f32[8,128,128]{2,1,0:T(8,128)}, f32[8,128,128]{2,1,0:T(8,128)S(1)}, u32[]{:S(2)}) copy-start(f32[8,128,128]{2,1,0:T(8,128)S(1)} %collective-permute-done.12) | copy-start | bytes 1572868
  79.9 8.6 %collective-permute-start.13 = (bf16[8,128,128]{2,1,0:T(8,128)(2,1)S(1)}, bf16[8,128,128]{2,1,0:T(8,128)(2,1)S(1)}, u32[]{:S(2)}, u32[]{:S(2)}) collective-permute-start(bf16[8,128,128]{2,1,0:T(8,128)(2,1)S(1)} %fusion.2), channel_id=1, source_target_pairs={{0,8},{4,12},{8,0},{12,4},{16,24},{20,28},{24,16},{28,20},{1,9},{5... | collective-permute-start | bytes 786440 | tf_op jit(solution)/shard_map/ppermute | solution.py:325
  89.3 9.0 %collective-permute-start.14 = (bf16[8,128,128]{2,1,0:T(8,128)(2,1)}, bf16[8,128,128]{2,1,0:T(8,128)(2,1)}, u32[]{:S(2)}, u32[]{:S(2)}) collective-permute-start(bf16[8,128,128]{2,1,0:T(8,128)(2,1)} %fusion.1), channel_id=1, source_target_pairs={{0,16},{4,20},{8,24},{12,28},{1,17},{5,21},{9,25},{13,29},{2,18},{... | collective-permute-start | bytes 786440 | tf_op jit(solution)/shard_map/ppermute | solution.py:325
  93.7 7.9 %copy-start.4 = (f32[16,128,128]{2,1,0:T(8,128)S(1)}, f32[16,128,128]{2,1,0:T(8,128)}, u32[]{:S(2)}) copy-start(f32[16,128,128]{2,1,0:T(8,128)} %prior.1) | copy-start | bytes 3145732
  99.6 2.0 %collective-permute-start.15 = (f32[8,128,128]{2,1,0:T(8,128)S(1)}, f32[8,128,128]{2,1,0:T(8,128)S(1)}, u32[]{:S(2)}, u32[]{:S(2)}) collective-permute-start(f32[8,128,128]{2,1,0:T(8,128)S(1)} %get-tuple-element.19), channel_id=1, source_target_pairs={{0,4},{4,0},{8,12},{12,8},{16,20},{20,16},{24,28},{28,24},{1,5},{5... | collective-permute-start | bytes 1572872 | tf_op jit(solution)/shard_map/ppermute | solution.py:331
  99.7 16.8 %copy-start.5 = (f32[2048]{0:T(1024)S(1)}, f32[2048]{0:T(1024)}, u32[]{:S(2)}) copy-start(f32[2048]{0:T(1024)} %param.7) | copy-start | bytes 24580
  103.0 6.4 %collective-permute-start.16 = (f32[8,256]{1,0:T(8,128)S(1)}, f32[8,256]{1,0:T(8,128)S(1)}, u32[]{:S(2)}, u32[]{:S(2)}) collective-permute-start(f32[8,256]{1,0:T(8,128)S(1)} %get-tuple-element.16), channel_id=1, source_target_pairs={{0,1},{1,0},{2,3},{3,2},{4,5},{5,4},{6,7},{7,6},{8,9},{9,8},{10,11... | collective-permute-start | bytes 24584 | tf_op jit(solution)/shard_map/ppermute | solution.py:302
  109.4 7.1 %collective-permute-start.17 = (f32[8,256]{1,0:T(8,128)S(1)}, f32[8,256]{1,0:T(8,128)S(1)}, u32[]{:S(2)}, u32[]{:S(2)}) collective-permute-start(f32[8,256]{1,0:T(8,128)S(1)} %add.40), channel_id=1, source_target_pairs={{0,2},{1,3},{2,0},{3,1},{4,6},{5,7},{6,4},{7,5},{8,10},{9,11},{10,... | collective-permute-start | bytes 24584 | tf_op jit(solution)/shard_map/ppermute | solution.py:302

commit v2 on v0

v2 whole, which is shorter than its diff:
```python
import functools

import jax
import jax.numpy as jnp
from jax import lax
from jax.experimental import pallas as pl
from jax.experimental.pallas import tpu as pltpu
from jax.sharding import PartitionSpec as P

EPSILON = 1e-06
PARTS = 3
COLUMNS = 1536
VMEM_EXTRA = 4 * 1024 * 1024

F32 = jnp.float32
BF16 = jnp.bfloat16


def params(scratch):
    return pltpu.CompilerParams(vmem_limit_bytes=scratch + VMEM_EXTRA)


HBM = pl.BlockSpec(memory_space=pltpu.HBM)
WHOLE = pl.BlockSpec(memory_space=pltpu.VMEM)
ANY = pl.BlockSpec(memory_space=pl.ANY)


def start_features(pick, choices, raw, sem):
    for c, pieces in enumerate(choices):

        @pl.when(pick == c)
        def _(pieces=pieces):
            at = 0
            for piece in pieces:
                there = raw.at[pl.ds(at, piece.shape[0])]
                pltpu.make_async_copy(piece, there, sem).start()
                at += piece.shape[0]


def wait_features(raw, sem):
    pltpu.make_async_copy(raw, raw, sem).wait()


def of_place(values):
    place = lax.axis_index("tensor")
    found = jnp.int32(values[0])
    for i, value in enumerate(values[1:], 1):
        if value != values[0]:
            found = jnp.where(place == i, jnp.int32(value), found)
    return found


def column_blocks(columns):
    width = COLUMNS if columns % COLUMNS == 0 else columns
    return [pl.ds(at, width) for at in range(0, columns, width)]


def project_kernel(counts, first, picks, weight_rows, *refs):
    refs = list(refs)
    choices = [[refs.pop(0) for _ in range(count)] for count in counts]
    weight = refs.pop(0)
    if not first:
        refs.pop(0)
    total, done, raw, turned, held, sem, weight_sems = refs
    done[...] = jnp.zeros_like(done)
    rows, columns = held.shape
    blocks = column_blocks(columns)

    start_features(of_place(picks), choices, raw, sem)
    at = pl.ds(pl.multiple_of(of_place(weight_rows), 16), rows)
    copies = [
        pltpu.make_async_copy(weight.at[at, block], held.at[:, block], weight_sems.at[b])
        for b, block in enumerate(blocks)
    ]
    for copy in copies:
        copy.start()
    wait_features(raw, sem)
    turned[...] = raw[...].T
    for copy, block in zip(copies, blocks):
        copy.wait()
        product = jnp.dot(turned[...], held[:, block], preferred_element_type=F32)
        if first:
            total[:, block] = product
        else:
            total[:, block] += product


def project(choices, picks, weight_rows, weight, total):
    counts = [len(pieces) for pieces in choices]
    rows = sum(piece.shape[0] for piece in choices[0])
    tokens, columns = choices[0][0].shape[1], weight.shape[1]
    first = total is None
    flat = [piece for pieces in choices for piece in pieces]
    operands = flat + [weight] + ([] if first else [total])
    return pl.pallas_call(
        functools.partial(project_kernel, counts, first, picks, weight_rows),
        out_shape=(pltpu.VMEM((tokens, columns), F32), pltpu.VMEM((8, 128), F32)),
        in_specs=[HBM if first else ANY] * len(flat) + [HBM] + ([] if first else [WHOLE]),
        out_specs=(WHOLE, WHOLE),
        scratch_shapes=[
            pltpu.VMEM((rows, tokens), BF16),
            pltpu.VMEM((tokens, rows), BF16),
            pltpu.VMEM((rows, columns), BF16),
            pltpu.SemaphoreType.DMA,
            pltpu.SemaphoreType.DMA((len(column_blocks(columns)),)),
        ],
        input_output_aliases={} if first else {len(operands) - 1: 0},
        compiler_params=params(2 * rows * (columns + 2 * tokens)),
        cost_estimate=pl.CostEstimate(
            flops=2 * tokens * rows * columns,
            bytes_accessed=rows * columns * 2 + rows * tokens * 2,
            transcendentals=0,
        ),
        name="project",
    )(*operands)


def heads_at_once(half):
    return next(g for g in (4, 2, 1) if half % g == 0)


def activate_heads(first_column, width, turned, held, total, act_ref, state_ref, arrived):
    half = state_ref.shape[0]
    group = PARTS * width
    at_once = heads_at_once(half)
    for h in range(0, half, at_once):
        arrived(h // at_once)
        here = slice(h * group, (h + at_once) * group)
        block = pl.ds(pl.multiple_of(first_column + h * group, group), at_once * group)
        projected = total[:, block] + jnp.dot(
            turned[...], held[:, here], preferred_element_type=F32
        )
        act = (projected / (1.0 + jnp.exp(-projected))).astype(BF16)
        act_ref[:, here] = act
        for g in range(at_once):
            at = g * group
            state_ref[h + g] = lax.dot_general(
                act[:, at + width : at + 2 * width],
                act[:, at + 2 * width : at + group],
                (((0,), (0,)), ((), ())),
                preferred_element_type=F32,
            )


def first_kernel(n_choices, width, picks, weight_rows, *refs):
    choices = [[ref] for ref in refs[:n_choices]]
    weight, total, turned, rest, act_ref, state_ref, raw, held, sem, weight_sems = refs[
        n_choices:
    ]
    rows, columns = held.shape
    block = heads_at_once(state_ref.shape[0]) * PARTS * width
    core = lax.axis_index("context") % 2
    start_features(of_place(picks), choices, raw, sem)
    at = pl.ds(pl.multiple_of(of_place(weight_rows), 16), rows)
    copies = []
    for b in range(columns // block):
        here = pl.ds(pl.multiple_of((1 - core) * columns + b * block, block), block)
        there = held.at[:, pl.ds(b * block, block)]
        copies.append(pltpu.make_async_copy(weight.at[at, here], there, weight_sems.at[b]))
    here = pl.ds(pl.multiple_of(core * columns, block), columns)
    rest_copy = pltpu.make_async_copy(weight.at[at, here], rest, weight_sems.at[len(copies)])
    for copy in copies:
        copy.start()
    rest_copy.start()
    wait_features(raw, sem)
    turned[...] = raw[...].T
    activate_heads(
        (1 - core) * columns,
        width,
        turned,
        held,
        total,
        act_ref,
        state_ref,
        lambda b: copies[b].wait(),
    )
    rest_copy.wait()


def second_kernel(width, turned, held, total, act_ref, state_ref):
    core = lax.axis_index("context") % 2
    activate_heads(
        core * held.shape[1], width, turned, held, total, act_ref, state_ref, lambda b: None
    )


def activate(choices, picks, weight_rows, weight, total, heads, width):
    rows, tokens = choices[0].shape
    half = heads // 2
    columns = half * PARTS * width
    blocks = half // heads_at_once(half)
    outs = (
        pltpu.VMEM((tokens, columns), BF16),
        pltpu.VMEM((half, width, width), F32),
    )
    cost = pl.CostEstimate(
        flops=2 * tokens * rows * columns + 2 * half * tokens * width * width,
        bytes_accessed=rows * tokens * 2,
        transcendentals=tokens * columns,
    )
    turned, rest, act_other, state_other = pl.pallas_call(
        functools.partial(first_kernel, len(choices), width, picks, weight_rows),
        out_shape=(pltpu.VMEM((tokens, rows), BF16), pltpu.VMEM((rows, columns), BF16)) + outs,
        in_specs=[ANY] * len(choices) + [HBM, WHOLE],
        out_specs=(WHOLE,) * 4,
        scratch_shapes=[
            pltpu.VMEM((rows, tokens), BF16),
            pltpu.VMEM((rows, columns), BF16),
            pltpu.SemaphoreType.DMA,
            pltpu.SemaphoreType.DMA((blocks + 1,)),
        ],
        compiler_params=params(2 * rows * (columns + tokens)),
        cost_estimate=cost,
        name="activate",
    )(*choices, weight, total)
    act_own, state_own = pl.pallas_call(
        functools.partial(second_kernel, width),
        out_shape=outs,
        in_specs=[WHOLE] * 3,
        out_specs=(WHOLE,) * 2,
        compiler_params=params(0),
        cost_estimate=cost,
        name="activate",
    )(turned, rest, total)
    return act_other, state_other, act_own, state_own


def within_kernel(width, *refs):
    tokens, columns = refs[0].shape
    causal = lax.broadcasted_iota(jnp.int32, (tokens, tokens), 0) >= lax.broadcasted_iota(
        jnp.int32, (tokens, tokens), 1
    )
    refs[4][...] = jnp.zeros_like(refs[4])
    for act_ref, within_ref in ((refs[0], refs[2]), (refs[1], refs[3])):
        for h in range(columns // (PARTS * width)):
            at = h * PARTS * width
            queries = act_ref[:, at : at + width]
            keys = act_ref[:, at + width : at + 2 * width]
            values = act_ref[:, at + 2 * width : at + 3 * width]
            scores = lax.dot_general(
                queries, keys, (((1,), (1,)), ((), ())), preferred_element_type=F32
            )
            scores = jnp.where(causal, scores, 0.0).astype(BF16)
            within_ref[:, h * width : (h + 1) * width] = jnp.dot(
                scores, values, preferred_element_type=F32
            )


def attend_within(act_other, act_own, width):
    tokens, columns = act_own.shape
    heads = columns // (PARTS * width)
    return pl.pallas_call(
        functools.partial(within_kernel, width),
        out_shape=(pltpu.VMEM((tokens, heads * width), F32),) * 2 + (pltpu.VMEM((8, 128), F32),),
        in_specs=[WHOLE] * 2,
        out_specs=(WHOLE,) * 3,
        compiler_params=params(0),
        cost_estimate=pl.CostEstimate(
            flops=8 * heads * tokens * tokens * width,
            bytes_accessed=tokens * columns * 4,
            transcendentals=0,
        ),
        name="within",
    )(act_other, act_own)


def across_kernel(
    act_other, act_own, within_other, within_own, prior, other, own, att_ref, square_ref
):
    half, width, _ = own.shape
    core = lax.axis_index("context") % 2
    sides = (
        (1 - core, act_other, within_other, other),
        (core, act_own, within_own, own),
    )
    squares = None
    for h in range(half):
        for side, act, within, earlier in sides:
            head = side * half + h
            carried = prior[head] + earlier[h]
            upper = carried.astype(BF16)
            lower = (carried - upper.astype(F32)).astype(BF16)
            at = h * PARTS * width
            queries = act[:, at : at + width]
            attended = within[:, h * width : (h + 1) * width] + jnp.dot(
                jnp.concatenate([queries, queries], axis=1),
                jnp.concatenate([upper, lower], axis=0),
                preferred_element_type=F32,
            )
            att_ref[:, pl.ds(pl.multiple_of(head * width, width), width)] = attended
            square = attended * attended
            squares = square if squares is None else squares + square
    square_ref[...] = lax.dot_general(
        jnp.ones((8, width), F32),
        squares,
        (((1,), (1,)), ((), ())),
        preferred_element_type=F32,
        precision=lax.Precision.HIGHEST,
    )


def attend_across(acts, withins, prior, other, own):
    tokens = acts[0].shape[0]
    heads, width, _ = prior.shape
    return pl.pallas_call(
        across_kernel,
        out_shape=(
            pltpu.VMEM((tokens, heads * width), F32),
            jax.ShapeDtypeStruct((8, tokens), F32),
        ),
        in_specs=[WHOLE] * 7,
        out_specs=(WHOLE, WHOLE),
        compiler_params=params(0),
        cost_estimate=pl.CostEstimate(
            flops=4 * heads * tokens * width * width, bytes_accessed=0, transcendentals=0
        ),
        name="across",
    )(*acts, *withins, prior, other, own)


def norm_kernel(features, att_ref, gain_ref, *refs):
    out_ref = refs[-1]
    squares = sum(ref[...] for ref in refs[1:-1]) + refs[0][...]
    ones = jnp.ones((squares.shape[0], 128), F32)
    mean_sq = lax.dot_general(
        squares * (1.0 / squares.shape[0] / features),
        ones,
        (((0,), (0,)), ((), ())),
        preferred_element_type=F32,
        precision=lax.Precision.HIGHEST,
    )
    inverse = lax.rsqrt(mean_sq + EPSILON)
    for at in range(0, att_ref.shape[1], 128):
        out_ref[:, at : at + 128] = (
            att_ref[:, at : at + 128] * inverse * gain_ref[:, at : at + 128]
        ).astype(BF16)


def normalize(att, squares, gain, features):
    tokens, columns = att.shape
    return pl.pallas_call(
        functools.partial(norm_kernel, features),
        out_shape=jax.ShapeDtypeStruct((tokens, columns), BF16),
        in_specs=[WHOLE] * (2 + len(squares)),
        out_specs=WHOLE,
        compiler_params=params(0),
        cost_estimate=pl.CostEstimate(
            flops=2 * tokens * columns, bytes_accessed=2 * tokens * columns, transcendentals=0
        ),
        name="normalize",
    )(att, gain[None, :], *squares)


def terms_over_tensor(x, n):
    if n <= 4:
        return [x] + [
            lax.ppermute(x, "tensor", [(i, (i + d) % n) for i in range(n)]) for d in range(1, n)
        ]
    if n & (n - 1):
        return [lax.psum(x, "tensor")]
    bit = 1
    while bit * 2 < n:
        x = x + lax.ppermute(x, "tensor", [(i, i ^ bit) for i in range(n)])
        bit *= 2
    return [x, lax.ppermute(x, "tensor", [(i, i ^ bit) for i in range(n)])]


def meet_kernel(bits, n_up, n_down, final, *refs):
    own, theirs = refs[0], refs[1]
    ups, downs = refs[2 : 2 + n_up], refs[2 + n_up : 2 + n_up + n_down]
    index = lax.axis_index("context")
    core, chip = index % 2, index // 2
    cut = own.shape[0] // 2

    def has(bit):
        return chip // bit % 2 == 1

    for h in range(own.shape[0]):
        total = own[h] + theirs[h]
        before = jnp.zeros_like(total)
        if h < cut:
            for bit, ref in zip(bits, ups):
                got = ref[h].astype(F32)
                before = before + jnp.where(has(bit), got, 0.0)
                total = total + got
            message = total
        else:
            for ref in downs:
                before = before + ref[h - cut].astype(F32)
            message = total
            if n_down and not final:
                message = before + jnp.where(has(bits[-1 - n_down]), 0.0, total)
        if final:
            for_mate, mine = refs[-2:]
            for_mate[h] = before + jnp.where(core == 0, own[h], 0.0)
            mine[h] = before + jnp.where(core == 1, theirs[h], 0.0)
        elif h < cut:
            refs[-2][h] = message.astype(BF16)
        else:
            refs[-1][h - cut] = message.astype(BF16)


def meet(bits, own, theirs, ups, downs, after, final):
    half, width, _ = own.shape
    cut = half // 2
    if final:
        out_shape = [pltpu.VMEM(own.shape, F32)] * 2
    else:
        out_shape = [
            pltpu.VMEM((n, width, width), BF16) for n in (cut, half - cut) if n
        ]
    operands = [own, theirs] + ups + downs + after
    return pl.pallas_call(
        functools.partial(meet_kernel, bits, len(ups), len(downs), final),
        out_shape=out_shape,
        in_specs=[WHOLE] * len(operands),
        out_specs=[WHOLE] * len(out_shape),
        compiler_params=params(0),
        cost_estimate=pl.CostEstimate(
            flops=4 * half * width * width, bytes_accessed=0, transcendentals=0
        ),
        name="meet",
    )(*operands)


def earlier_states(other_states, own, after, n):
    chips, cut = n // 2, own.shape[0] // 2
    swap = [(i, i ^ 1) for i in range(n)]
    theirs = lax.ppermute(other_states, "context", swap)
    bits = [1 << b for b in range((chips - 1).bit_length())]

    def send(x, bit, both):
        pairs = [
            (2 * i + c, 2 * (i ^ bit) + c)
            for i in range(chips)
            for c in range(2)
            if both or not i & bit
        ]
        return lax.ppermute(x, "context", pairs)

    ups, downs = [], []
    for step, (rise, fall) in enumerate(zip(bits, bits[::-1])):
        messages = meet(bits, own, theirs, ups, downs, after if step == 1 else [], False)
        if cut:
            ups = ups + [send(messages[0], rise, step < len(bits) - 1)]
        downs = downs + [send(messages[-1], fall, step > 0)]
    for_mate, mine = meet(bits, own, theirs, ups, downs, [], True)
    return lax.ppermute(for_mate, "context", swap), mine


def hops(n):
    pairs = [[[] for _ in range(n - 1)] for _ in range(2)]
    arrivals = [[] for _ in range(n)]
    for t in range(n - 1):
        for chain in range(2):
            for share in range(n):
                way = 1 if share % 2 == chain else -1
                here = share + way * t
                if 0 <= here < n and 0 <= here + way < n:
                    pairs[chain][t].append((here, here + way))
                    arrivals[here + way].append((t, chain, share))
    return pairs, arrivals


def body(n_tensor, n_context, tokens_t, qkv_weight, prior_state, norm_gain):
    share = tokens_t.shape[0]
    heads, width, _ = prior_state.shape
    early = share // 2

    def cut(x):
        return [x[:early], x[early:]]

    pairs, arrivals = hops(n_tensor)
    starts = [i * share for i in range(n_tensor)]
    total, done = project([[tokens_t]], [0] * n_tensor, starts, qkv_weight, None)
    held = [[tokens_t], [tokens_t]]
    came = {}
    for t in range(n_tensor - 1):
        for chain in range(2):
            if t == 1:
                held[chain], _ = lax.optimization_barrier((held[chain], done))
            if t == 1 and chain == 0:
                held[0] = cut(held[0][0])
            if pairs[chain][t]:
                held[chain] = [lax.ppermute(x, "tensor", pairs[chain][t]) for x in held[chain]]
                came[t, chain] = held[chain]

    for m in range(n_tensor - 1):
        keys = sorted({came_at[m][:2] for came_at in arrivals})
        picks = [keys.index(came_at[m][:2]) for came_at in arrivals]
        rows = [came_at[m][2] * share for came_at in arrivals]
        choices = [came[key] for key in keys]
        if m < n_tensor - 2:
            total, _ = project(choices, picks, rows, qkv_weight, total)
        else:
            choices = [c if len(c) == 2 else cut(c[0]) for c in choices]
            total, _ = project([c[:1] for c in choices], picks, rows, qkv_weight, total)
            rows = [row + early for row in rows]
            other_act, other_states, own_act, own_states = activate(
                [c[1] for c in choices], picks, rows, qkv_weight, total, heads, width
            )
    acts = (other_act, own_act)
    *withins, done = attend_within(*acts, width)
    other, own = earlier_states(other_states, own_states, [done], n_context)
    att, squares = attend_across(acts, withins, prior_state, other, own)
    squares = terms_over_tensor(squares, n_tensor)
    return normalize(att, squares, norm_gain, n_tensor * heads * width)


def solution(mesh):
    n_tensor, n_context = mesh.shape["tensor"], mesh.shape["context"]
    in_specs = (P("tensor", "context"), P(None, "tensor"), P("tensor", None, None), P("tensor"))
    return jax.shard_map(
        functools.partial(body, n_tensor, n_context),
        mesh=mesh,
        in_specs=in_specs,
        out_specs=P("context", "tensor"),
        check_vma=False,
    )
```

time: 194 us -> 95.6 us (0.49)
  waiting for transfers between devices: 119 us -> 25.6 us
  Pallas kernels: 0 us -> 40.4 us
  matrix products: 38.1 us -> 0 us
  starting transfers between devices: 0.04 us -> 27.9 us
  between operations: 13.5 us -> 0.22 us
  blocking collectives: 11.8 us -> 0 us
  other arithmetic: 5.98 us -> 0 us
  local copies, waits for them, and re-layouts: 5.1 us -> 1.23 us
    all_gather x2 -> x0, waiting for transfers between devices: 118 us -> none  [the longest x1 67.9 us: body(): lax.all_gather(tokens_t, 'tensor', axis=0, tiled=True)]
    pallas_call x0 -> x12, Pallas kernels: none -> 40.4 us  [the longest x4 29.6 us: project(): pl.pallas_call(functools.partial(project_kernel, counts, first, picks, we...]
    dot_general x4 -> x0, matrix products: 38.1 us -> none  [the longest x1 31.3 us: body(): lax.dot_general(lax.all_gather(tokens_t, 'tensor', axis=0, tiled=True), q...]
    ppermute x0 -> x16, starting transfers between devices: none -> 27.9 us  [the longest x7 11.8 us: body(): lax.ppermute(x, 'tensor', pairs[chain][t])]
    ppermute x0 -> x16, waiting for transfers between devices: none -> 25.6 us  [the longest x7 16.5 us: body(): lax.ppermute(x, 'tensor', pairs[chain][t])]
    psum x1 -> x0, blocking collectives: 11.8 us -> none  [body(): square_sum = lax.psum(jnp.sum(attended * attended, axis=1), 'tensor')]
    reduce_sum x1 -> x0, other arithmetic: 4.72 us -> none  [body(): earlier = jnp.sum(keep_rows[:, None, None, None] * block_part, axis=0)]
    convert_element_type x1 -> x0, local copies, waits for them, and re-layouts: 3.17 us -> none  [body(): jax.nn.silu(projected).astype(jnp.bfloat16)]
  transfers between devices with their start and end apart: 2 -> 16, of which waited for: 2 -> 10; matrix products, arithmetic and copies ran while one was open for 1% -> 0% of each run, Pallas kernels for 0% -> 35%
where the time goes in v2:
time: 95.6 us; the launch traced here: 95.3 us
  Pallas kernels  40.4 us (42%)
  starting transfers between devices  27.9 us (29%)
  waiting for transfers between devices  25.6 us (27%)
  local copies, waits for them, and re-layouts  1.23 us (1%)
    pallas_call x4, Pallas kernels, project(): pl.pallas_call(functools.partial(project_kernel, counts, first, picks, we...  29.6 us
    ppermute x7, waiting for transfers between devices, body(): lax.ppermute(x, 'tensor', pairs[chain][t])  16.5 us
    ppermute x7, starting transfers between devices, body(): lax.ppermute(x, 'tensor', pairs[chain][t])  11.8 us
    ppermute x4, starting transfers between devices, send(): return lax.ppermute(x, 'context', pairs)  10.2 us
    ppermute x4, waiting for transfers between devices, send(): return lax.ppermute(x, 'context', pairs)  5.82 us
    ppermute x3, starting transfers between devices, terms_over_tensor(): lax.ppermute(x, 'tensor', [(i, (i + d) % n) for i in range(n)])  5.72 us
    pallas_call x1, Pallas kernels, activate(): pl.pallas_call(functools.partial(first_kernel, len(choices), width, picks...  4.33 us
    pallas_call x1, Pallas kernels, activate(): pl.pallas_call(functools.partial(second_kernel, width), out_shape=outs, i...  2.18 us
  transfers between devices with their start and end apart: 16, of which 10 were waited for; matrix products, arithmetic and copies ran while one was open for 0% of the time, Pallas kernels for 35%

profile of v2, /device:TPU:0, one launch (start us, length us, event | category | flops | bytes accessed | tf_op | source)
XLA Modules:
  0.0 95.3 jit_solution(4154745849590685985)
XLA Ops:
  0.0 0.7 collective-permute-start.5
  0.7 5.9 %collective-permute-start = (bf16[1536,256]{1,0:T(8,128)(2,1)}, bf16[1536,256]{1,0:T(8,128)(2,1)S(1)}, u32[]{:S(2)}, u32[]{:S(2)}) collective-permute-start(bf16[1536,256]{1,0:T(8,128)(2,1)} %refs_0_.1), channel_id=1, source_target_pairs={{0,1},{1,0},{2,3},{3,2},{4,5},{5,4},{6,7},{7,6},{8,9},{9,8},{10,11... | collective-permute-start | bytes 2359304 | tf_op jit(solution)/shard_map/ppermute | solution.py:485
  6.6 1.2 %copy-done.1 = bf16[1536,256]{1,0:T(8,128)(2,1)S(1)} copy-done((bf16[1536,256]{1,0:T(8,128)(2,1)S(1)}, bf16[1536,256]{1,0:T(8,128)(2,1)}, u32[]{:S(2)}) %copy-start.1) | copy-done | bytes 786456
  7.7 8.0 %project.4 = (f32[256,6144]{1,0:T(8,128)S(1)}, f32[8,128]{1,0:T(8,128)}) custom-call(bf16[1536,256]{1,0:T(8,128)(2,1)S(1)} %copy-done.1, bf16[6144,6144]{1,0:T(8,128)(2,1)} %refs_2_.5), custom_call_target="tpu_custom_call" | custom-call | flops 4831838208 | bytes 19660800 | tf_op jit(solution)/shard_map/project/pallas_call | solution.py:95
  15.8 0.0 collective-permute-done.5.refs_0_
  15.8 1.3 %collective-permute-start.6 = (bf16[1536,256]{1,0:T(8,128)(2,1)S(1)}, bf16[1536,256]{1,0:T(8,128)(2,1)S(1)}, u32[]{:S(2)}, u32[]{:S(2)}) collective-permute-start(bf16[1536,256]{1,0:T(8,128)(2,1)S(1)} %collective-permute-done.5.refs_0_), channel_id=1, source_target_pairs={{2,3},{1,0},{6,7},{5,4},{10,11},{9,8},{14,15},{13,12},{18,19},{17,... | collective-permute-start | bytes 2359304 | tf_op jit(solution)/shard_map/ppermute | solution.py:485
  17.1 6.9 %collective-permute-done.refs_0_ = bf16[1536,256]{1,0:T(8,128)(2,1)S(1)} collective-permute-done((bf16[1536,256]{1,0:T(8,128)(2,1)}, bf16[1536,256]{1,0:T(8,128)(2,1)S(1)}, u32[]{:S(2)}, u32[]{:S(2)}) %collective-permute-start) | collective-permute-done | bytes 786464 | tf_op jit(solution)/shard_map/ppermute | solution.py:485
  24.0 0.1 fusion
  24.1 0.7 collective-permute-start.3
  24.8 0.7 collective-permute-start.1
  25.5 8.1 %project.5 = (f32[256,6144]{1,0:T(8,128)S(1)}, f32[8,128]{1,0:T(8,128)}) custom-call(bf16[1536,256]{1,0:T(8,128)(2,1)S(1)} %collective-permute-done.refs_0_, bf16[6144,6144]{1,0:T(8,128)(2,1)} %refs_2_.5, f32[256,6144]{1,0:T(8,128)S(1)} %get-tuple-element.32.refs_2_), custom_call_target="tpu_custom_call", output_to_operand_aliasing={{0}: (2, {})} | custom-call | flops 4831838208 | bytes 19660800 | tf_op jit(solution)/shard_map/project/pallas_call | solution.py:95
  33.6 0.0 collective-permute-done.3.refs_0_
  33.6 1.3 %collective-permute-start.4 = (bf16[768,256]{1,0:T(8,128)(2,1)S(1)}, bf16[768,256]{1,0:T(8,128)(2,1)S(1)}, u32[]{:S(2)}, u32[]{:S(2)}) collective-permute-start(bf16[768,256]{1,0:T(8,128)(2,1)S(1)} %collective-permute-done.3.refs_0_), channel_id=1, source_target_pairs={{2,3},{1,0},{6,7},{5,4},{10,11},{9,8},{14,15},{13,12},{18,19},{17,... | collective-permute-start | bytes 1179656 | tf_op jit(solution)/shard_map/ppermute | solution.py:485
  34.9 0.0 collective-permute-done.1.refs_0_
  34.9 1.3 %collective-permute-start.2 = (bf16[768,256]{1,0:T(8,128)(2,1)S(1)}, bf16[768,256]{1,0:T(8,128)(2,1)S(1)}, u32[]{:S(2)}, u32[]{:S(2)}) collective-permute-start(bf16[768,256]{1,0:T(8,128)(2,1)S(1)} %collective-permute-done.1.refs_0_), channel_id=1, source_target_pairs={{2,3},{1,0},{6,7},{5,4},{10,11},{9,8},{14,15},{13,12},{18,19},{17,... | collective-permute-start | bytes 1179656 | tf_op jit(solution)/shard_map/ppermute | solution.py:485
  36.2 7.9 %collective-permute-done.6.refs_1_ = bf16[1536,256]{1,0:T(8,128)(2,1)S(1)} collective-permute-done((bf16[1536,256]{1,0:T(8,128)(2,1)S(1)}, bf16[1536,256]{1,0:T(8,128)(2,1)S(1)}, u32[]{:S(2)}, u32[]{:S(2)}) %collective-permute-start.6) | collective-permute-done | bytes 786464 | tf_op jit(solution)/shard_map/ppermute | solution.py:485
  44.1 8.3 %project.6 = (f32[256,6144]{1,0:T(8,128)S(1)}, f32[8,128]{1,0:T(8,128)}) custom-call(bf16[1536,256]{1,0:T(8,128)(2,1)S(1)} %collective-permute-done.5.refs_0_, bf16[1536,256]{1,0:T(8,128)(2,1)S(1)} %collective-permute-done.6.refs_1_, bf16[6144,6144]{1,0:T(8,128)(2,1)} %refs_2_.5, ...), custom_call_target="tpu_custom_call", output_to_operand_aliasing={{0}: (3, {})} | custom-call | flops 4831838208 | bytes 19660800 | tf_op jit(solution)/shard_map/project/pallas_call | solution.py:95
  52.4 0.1 collective-permute-done.4.refs_1_
  52.5 5.1 %project.7 = (f32[256,6144]{1,0:T(8,128)S(1)}, f32[8,128]{1,0:T(8,128)}) custom-call(bf16[768,256]{1,0:T(8,128)(2,1)S(1)} %collective-permute-done.3.refs_0_, bf16[768,256]{1,0:T(8,128)(2,1)S(1)} %collective-permute-done.4.refs_1_, bf16[6144,6144]{1,0:T(8,128)(2,1)} %refs_2_.5, ...), custom_call_target="tpu_custom_call", output_to_operand_aliasing={{0}: (3, {})} | custom-call | flops 2415919104 | bytes 9830400 | tf_op jit(solution)/shard_map/project/pallas_call | solution.py:95
  57.7 1.5 %collective-permute-done.2.refs_1_ = bf16[768,256]{1,0:T(8,128)(2,1)S(1)} collective-permute-done((bf16[768,256]{1,0:T(8,128)(2,1)S(1)}, bf16[768,256]{1,0:T(8,128)(2,1)S(1)}, u32[]{:S(2)}, u32[]{:S(2)}) %collective-permute-start.2) | collective-permute-done | bytes 393248 | tf_op jit(solution)/shard_map/ppermute | solution.py:485
  59.2 4.3 %activate.2 = (bf16[256,768]{1,0:T(8,128)(2,1)S(1)}, bf16[768,3072]{1,0:T(8,128)(2,1)S(1)}, bf16[256,3072]{1,0:T(8,128)(2,1)S(1)}, f32[8,128,128]{2,1,0:T(8,128)S(1)}) custom-call(bf16[768,256]{1,0:T(8,128)(2,1)S(1)} %collective-permute-done.1.refs_0_, bf16[768,256]{1,0:T(8,128)(2,1)S(1)} %collective-permute-done.2.refs_1_, bf16[6144,6144]{1,0:T(8,128)(2,1)} %refs_2_.5, ...), custom_call_target="tpu_custom_call" | custom-call | flops 1275068416 | bytes 393216 | tf_op jit(solution)/shard_map/activate/pallas_call | solution.py:201
  63.5 0.1 collective-permute-start.7
  63.6 2.2 %activate.3 = (bf16[256,3072]{1,0:T(8,128)(2,1)S(1)}, f32[8,128,128]{2,1,0:T(8,128)S(1)}) custom-call(bf16[256,768]{1,0:T(8,128)(2,1)S(1)} %get-tuple-element.37.turned, bf16[768,3072]{1,0:T(8,128)(2,1)S(1)} %get-tuple-element.38.held, f32[256,6144]{1,0:T(8,128)S(1)} %get-tuple-element.35.refs_3_.total), custom_call_target="tpu_custom_call" | custom-call | flops 1275068416 | bytes 393216 | tf_op jit(solution)/shard_map/activate/pallas_call | solution.py:216
  65.8 0.0 copy-start
  65.8 0.0 collective-permute-done.7.refs_1_
  65.8 0.1 meet.3
  65.9 1.6 %collective-permute-start.8 = (bf16[4,128,128]{2,1,0:T(8,128)(2,1)S(1)}, bf16[4,128,128]{2,1,0:T(8,128)(2,1)S(1)}, u32[]{:S(2)}, u32[]{:S(2)}) collective-permute-start(bf16[4,128,128]{2,1,0:T(8,128)(2,1)S(1)} %get-tuple-element.44), channel_id=1, source_target_pairs={{0,8},{4,12},{8,0},{12,4},{16,24},{20,28},{24,16},{28,20},{1,9},{5... | collective-permute-start | bytes 393224 | tf_op jit(solution)/shard_map/ppermute | solution.py:439
  67.4 3.6 %collective-permute-start.9 = (bf16[4,128,128]{2,1,0:T(8,128)(2,1)S(1)}, bf16[4,128,128]{2,1,0:T(8,128)(2,1)S(1)}, u32[]{:S(2)}, u32[]{:S(2)}) collective-permute-start(bf16[4,128,128]{2,1,0:T(8,128)(2,1)S(1)} %get-tuple-element.45), channel_id=1, source_target_pairs={{0,16},{4,20},{8,24},{12,28},{1,17},{5,21},{9,25},{13,29},{2,18},{... | collective-permute-start | bytes 393224 | tf_op jit(solution)/shard_map/ppermute | solution.py:439
  71.1 0.0 copy-start.2
  71.1 1.5 %within.1 = (f32[256,1024]{1,0:T(8,128)S(1)}, f32[256,1024]{1,0:T(8,128)S(1)}, f32[8,128]{1,0:T(8,128)S(1)}) custom-call(bf16[256,3072]{1,0:T(8,128)(2,1)S(1)} %get-tuple-element.36.refs_0_.act_other, bf16[256,3072]{1,0:T(8,128)(2,1)S(1)} %get-tuple-element.39.refs_1_.act_own), custom_call_target="tpu_custom_call" | custom-call | flops 536870912 | bytes 3145728 | tf_op jit(solution)/shard_map/within/pallas_call | solution.py:252
  72.6 0.0 collective-permute-done.8.refs_2_
  72.6 1.4 %collective-permute-done.9.refs_3_.refs_4_ = bf16[4,128,128]{2,1,0:T(8,128)(2,1)S(1)} collective-permute-done((bf16[4,128,128]{2,1,0:T(8,128)(2,1)S(1)}, bf16[4,128,128]{2,1,0:T(8,128)(2,1)S(1)}, u32[]{:S(2)}, u32[]{:S(2)}) %collective-permute-start.9) | collective-permute-done | bytes 131104 | tf_op jit(solution)/shard_map/ppermute | solution.py:439
  74.0 0.1 meet.4
  74.1 4.4 %collective-permute-start.10 = (bf16[4,128,128]{2,1,0:T(8,128)(2,1)S(1)}, bf16[4,128,128]{2,1,0:T(8,128)(2,1)S(1)}, u32[]{:S(2)}, u32[]{:S(2)}) collective-permute-start(bf16[4,128,128]{2,1,0:T(8,128)(2,1)S(1)} %get-tuple-element.47), channel_id=1, source_target_pairs={{0,16},{4,20},{8,24},{12,28},{1,17},{5,21},{9,25},{13,29},{2,18},{... | collective-permute-start | bytes 393224 | tf_op jit(solution)/shard_map/ppermute | solution.py:439
  78.5 0.6 collective-permute-start.11
  79.1 1.9 %collective-permute-done.10.refs_3_ = bf16[4,128,128]{2,1,0:T(8,128)(2,1)S(1)} collective-permute-done((bf16[4,128,128]{2,1,0:T(8,128)(2,1)S(1)}, bf16[4,128,128]{2,1,0:T(8,128)(2,1)S(1)}, u32[]{:S(2)}, u32[]{:S(2)}) %collective-permute-start.10) | collective-permute-done | bytes 131104 | tf_op jit(solution)/shard_map/ppermute | solution.py:439
  81.0 2.5 %collective-permute-done.11.refs_5_ = bf16[4,128,128]{2,1,0:T(8,128)(2,1)S(1)} collective-permute-done((bf16[4,128,128]{2,1,0:T(8,128)(2,1)S(1)}, bf16[4,128,128]{2,1,0:T(8,128)(2,1)S(1)}, u32[]{:S(2)}, u32[]{:S(2)}) %collective-permute-start.11) | collective-permute-done | bytes 131104 | tf_op jit(solution)/shard_map/ppermute | solution.py:439
  83.5 0.1 meet.5
  83.6 0.1 collective-permute-start.12
  83.7 1.9 %collective-permute-done.12.other = f32[8,128,128]{2,1,0:T(8,128)S(1)} collective-permute-done((f32[8,128,128]{2,1,0:T(8,128)S(1)}, f32[8,128,128]{2,1,0:T(8,128)S(1)}, u32[]{:S(2)}, u32[]{:S(2)}) %collective-permute-start.12) | collective-permute-done | bytes 524320 | tf_op jit(solution)/shard_map/ppermute | solution.py:448
  85.6 1.0 %across.1 = (f32[256,2048]{1,0:T(8,128)S(1)}, f32[8,256]{1,0:T(8,128)S(1)}) custom-call(bf16[256,3072]{1,0:T(8,128)(2,1)S(1)} %get-tuple-element.36.refs_0_.act_other, bf16[256,3072]{1,0:T(8,128)(2,1)S(1)} %get-tuple-element.39.refs_1_.act_own, f32[256,1024]{1,0:T(8,128)S(1)} %get-tuple-element.40.within_other, ...), custom_call_target="tpu_custom_call" | custom-call | flops 268435456 | tf_op jit(solution)/shard_map/across/pallas_call | solution.py:305
  86.7 1.8 %collective-permute-start.13 = (f32[8,256]{1,0:T(8,128)S(1)}, f32[8,256]{1,0:T(8,128)S(1)}, u32[]{:S(2)}, u32[]{:S(2)}) collective-permute-start(f32[8,256]{1,0:T(8,128)S(1)} %get-tuple-element.52.refs_0_), channel_id=1, source_target_pairs={{0,1},{1,2},{2,3},{3,0},{4,5},{5,6},{6,7},{7,4},{8,9},{9,10},{10,1... | collective-permute-start | bytes 24584 | tf_op jit(solution)/shard_map/ppermute | solution.py:357
  88.4 1.3 %collective-permute-start.14 = (f32[8,256]{1,0:T(8,128)S(1)}, f32[8,256]{1,0:T(8,128)S(1)}, u32[]{:S(2)}, u32[]{:S(2)}) collective-permute-start(f32[8,256]{1,0:T(8,128)S(1)} %get-tuple-element.52.refs_0_), channel_id=1, source_target_pairs={{0,2},{1,3},{2,0},{3,1},{4,6},{5,7},{6,4},{7,5},{8,10},{9,11},{10,... | collective-permute-start | bytes 24584 | tf_op jit(solution)/shard_map/ppermute | solution.py:357
  89.7 2.6 %collective-permute-start.15 = (f32[8,256]{1,0:T(8,128)S(1)}, f32[8,256]{1,0:T(8,128)S(1)}, u32[]{:S(2)}, u32[]{:S(2)}) collective-permute-start(f32[8,256]{1,0:T(8,128)S(1)} %get-tuple-element.52.refs_0_), channel_id=1, source_target_pairs={{0,3},{1,0},{2,1},{3,2},{4,7},{5,4},{6,5},{7,6},{8,11},{9,8},{10,9... | collective-permute-start | bytes 24584 | tf_op jit(solution)/shard_map/ppermute | solution.py:357
  92.4 0.0 collective-permute-done.13.refs_1_
  92.4 0.6 collective-permute-done.14.refs_2_
  93.0 0.8 collective-permute-done.15.refs_3_
  93.7 1.5 %normalize.1 = bf16[256,2048]{1,0:T(8,128)(2,1)} custom-call(f32[256,2048]{1,0:T(8,128)S(1)} %get-tuple-element.51.att_ref, f32[1,2048]{1,0:T(1,128)S(1)} %bitcast.1, f32[8,256]{1,0:T(8,128)S(1)} %get-tuple-element.52.refs_0_, f32[8,256]{1,0:T(8,128)S(1)} %collective-permute-done.13.refs_1_, f32[8,256]{1,0:T(8,128)S(1)} %collective-permute-done.14.refs_2_, ...), custom_call_target="tpu_custom_call" | custom-call | flops 1048576 | bytes 1048576 | tf_op jit(solution)/shard_map/normalize/pallas_call | solution.py:341
  (3 shorter events, 0.0 us)
Async XLA Ops:
  0.0 15.8 %collective-permute-start.5 = (bf16[1536,256]{1,0:T(8,128)(2,1)}, bf16[1536,256]{1,0:T(8,128)(2,1)S(1)}, u32[]{:S(2)}, u32[]{:S(2)}) collective-permute-start(bf16[1536,256]{1,0:T(8,128)(2,1)} %refs_0_.1), channel_id=1, source_target_pairs={{1,2},{2,1},{5,6},{6,5},{9,10},{10,9},{13,14},{14,13},{17,18},{18,... | collective-permute-start | bytes 2359304 | tf_op jit(solution)/shard_map/ppermute | solution.py:485
  0.7 23.3 %collective-permute-start = (bf16[1536,256]{1,0:T(8,128)(2,1)}, bf16[1536,256]{1,0:T(8,128)(2,1)S(1)}, u32[]{:S(2)}, u32[]{:S(2)}) collective-permute-start(bf16[1536,256]{1,0:T(8,128)(2,1)} %refs_0_.1), channel_id=1, source_target_pairs={{0,1},{1,0},{2,3},{3,2},{4,5},{5,4},{6,7},{7,6},{8,9},{9,8},{10,11... | collective-permute-start | bytes 2359304 | tf_op jit(solution)/shard_map/ppermute | solution.py:485
  6.6 1.2 %copy-start.1 = (bf16[1536,256]{1,0:T(8,128)(2,1)S(1)}, bf16[1536,256]{1,0:T(8,128)(2,1)}, u32[]{:S(2)}) copy-start(bf16[1536,256]{1,0:T(8,128)(2,1)} %refs_0_.1) | copy-start | bytes 2359300
  15.8 28.3 %collective-permute-start.6 = (bf16[1536,256]{1,0:T(8,128)(2,1)S(1)}, bf16[1536,256]{1,0:T(8,128)(2,1)S(1)}, u32[]{:S(2)}, u32[]{:S(2)}) collective-permute-start(bf16[1536,256]{1,0:T(8,128)(2,1)S(1)} %collective-permute-done.5.refs_0_), channel_id=1, source_target_pairs={{2,3},{1,0},{6,7},{5,4},{10,11},{9,8},{14,15},{13,12},{18,19},{17,... | collective-permute-start | bytes 2359304 | tf_op jit(solution)/shard_map/ppermute | solution.py:485
  24.1 9.5 %collective-permute-start.3 = (bf16[768,256]{1,0:T(8,128)(2,1)S(1)}, bf16[768,256]{1,0:T(8,128)(2,1)S(1)}, u32[]{:S(2)}, u32[]{:S(2)}) collective-permute-start(bf16[768,256]{1,0:T(8,128)(2,1)S(1)} %get-tuple-element.53), channel_id=1, source_target_pairs={{1,2},{2,1},{5,6},{6,5},{9,10},{10,9},{13,14},{14,13},{17,18},{18,... | collective-permute-start | bytes 1179656 | tf_op jit(solution)/shard_map/ppermute | solution.py:485
  24.8 10.1 %collective-permute-start.1 = (bf16[768,256]{1,0:T(8,128)(2,1)S(1)}, bf16[768,256]{1,0:T(8,128)(2,1)S(1)}, u32[]{:S(2)}, u32[]{:S(2)}) collective-permute-start(bf16[768,256]{1,0:T(8,128)(2,1)S(1)} %get-tuple-element.54), channel_id=1, source_target_pairs={{1,2},{2,1},{5,6},{6,5},{9,10},{10,9},{13,14},{14,13},{17,18},{18,... | collective-permute-start | bytes 1179656 | tf_op jit(solution)/shard_map/ppermute | solution.py:485
  33.6 18.9 %collective-permute-start.4 = (bf16[768,256]{1,0:T(8,128)(2,1)S(1)}, bf16[768,256]{1,0:T(8,128)(2,1)S(1)}, u32[]{:S(2)}, u32[]{:S(2)}) collective-permute-start(bf16[768,256]{1,0:T(8,128)(2,1)S(1)} %collective-permute-done.3.refs_0_), channel_id=1, source_target_pairs={{2,3},{1,0},{6,7},{5,4},{10,11},{9,8},{14,15},{13,12},{18,19},{17,... | collective-permute-start | bytes 1179656 | tf_op jit(solution)/shard_map/ppermute | solution.py:485
  34.9 24.2 %collective-permute-start.2 = (bf16[768,256]{1,0:T(8,128)(2,1)S(1)}, bf16[768,256]{1,0:T(8,128)(2,1)S(1)}, u32[]{:S(2)}, u32[]{:S(2)}) collective-permute-start(bf16[768,256]{1,0:T(8,128)(2,1)S(1)} %collective-permute-done.1.refs_0_), channel_id=1, source_target_pairs={{2,3},{1,0},{6,7},{5,4},{10,11},{9,8},{14,15},{13,12},{18,19},{17,... | collective-permute-start | bytes 1179656 | tf_op jit(solution)/shard_map/ppermute | solution.py:485
  63.5 2.3 %collective-permute-start.7 = (f32[8,128,128]{2,1,0:T(8,128)S(1)}, f32[8,128,128]{2,1,0:T(8,128)S(1)}, u32[]{:S(2)}, u32[]{:S(2)}) collective-permute-start(f32[8,128,128]{2,1,0:T(8,128)S(1)} %get-tuple-element.43), channel_id=1, source_target_pairs={{0,4},{4,0},{8,12},{12,8},{16,20},{20,16},{24,28},{28,24},{1,5},{5... | collective-permute-start | bytes 1572872 | tf_op jit(solution)/shard_map/ppermute | solution.py:429
  65.8 19.8 %copy-start = (f32[16,128,128]{2,1,0:T(8,128)S(1)}, f32[16,128,128]{2,1,0:T(8,128)}, u32[]{:S(2)}) copy-start(f32[16,128,128]{2,1,0:T(8,128)} %prior.1) | copy-start | bytes 3145732
  65.9 6.7 %collective-permute-start.8 = (bf16[4,128,128]{2,1,0:T(8,128)(2,1)S(1)}, bf16[4,128,128]{2,1,0:T(8,128)(2,1)S(1)}, u32[]{:S(2)}, u32[]{:S(2)}) collective-permute-start(bf16[4,128,128]{2,1,0:T(8,128)(2,1)S(1)} %get-tuple-element.44), channel_id=1, source_target_pairs={{0,8},{4,12},{8,0},{12,4},{16,24},{20,28},{24,16},{28,20},{1,9},{5... | collective-permute-start | bytes 393224 | tf_op jit(solution)/shard_map/ppermute | solution.py:439
  67.4 6.5 %collective-permute-start.9 = (bf16[4,128,128]{2,1,0:T(8,128)(2,1)S(1)}, bf16[4,128,128]{2,1,0:T(8,128)(2,1)S(1)}, u32[]{:S(2)}, u32[]{:S(2)}) collective-permute-start(bf16[4,128,128]{2,1,0:T(8,128)(2,1)S(1)} %get-tuple-element.45), channel_id=1, source_target_pairs={{0,16},{4,20},{8,24},{12,28},{1,17},{5,21},{9,25},{13,29},{2,18},{... | collective-permute-start | bytes 393224 | tf_op jit(solution)/shard_map/ppermute | solution.py:439
  71.1 22.7 %copy-start.2 = (f32[2048]{0:T(1024)S(1)}, f32[2048]{0:T(1024)}, u32[]{:S(2)}) copy-start(f32[2048]{0:T(1024)} %param.7) | copy-start | bytes 24580
  74.1 6.9 %collective-permute-start.10 = (bf16[4,128,128]{2,1,0:T(8,128)(2,1)S(1)}, bf16[4,128,128]{2,1,0:T(8,128)(2,1)S(1)}, u32[]{:S(2)}, u32[]{:S(2)}) collective-permute-start(bf16[4,128,128]{2,1,0:T(8,128)(2,1)S(1)} %get-tuple-element.47), channel_id=1, source_target_pairs={{0,16},{4,20},{8,24},{12,28},{1,17},{5,21},{9,25},{13,29},{2,18},{... | collective-permute-start | bytes 393224 | tf_op jit(solution)/shard_map/ppermute | solution.py:439
  78.5 5.0 %collective-permute-start.11 = (bf16[4,128,128]{2,1,0:T(8,128)(2,1)S(1)}, bf16[4,128,128]{2,1,0:T(8,128)(2,1)S(1)}, u32[]{:S(2)}, u32[]{:S(2)}) collective-permute-start(bf16[4,128,128]{2,1,0:T(8,128)(2,1)S(1)} %get-tuple-element.48), channel_id=1, source_target_pairs={{0,8},{4,12},{8,0},{12,4},{16,24},{20,28},{24,16},{28,20},{1,9},{5... | collective-permute-start | bytes 393224 | tf_op jit(solution)/shard_map/ppermute | solution.py:439
  83.6 2.0 %collective-permute-start.12 = (f32[8,128,128]{2,1,0:T(8,128)S(1)}, f32[8,128,128]{2,1,0:T(8,128)S(1)}, u32[]{:S(2)}, u32[]{:S(2)}) collective-permute-start(f32[8,128,128]{2,1,0:T(8,128)S(1)} %get-tuple-element.49), channel_id=1, source_target_pairs={{0,4},{4,0},{8,12},{12,8},{16,20},{20,16},{24,28},{28,24},{1,5},{5... | collective-permute-start | bytes 1572872 | tf_op jit(solution)/shard_map/ppermute | solution.py:448
  86.7 5.7 %collective-permute-start.13 = (f32[8,256]{1,0:T(8,128)S(1)}, f32[8,256]{1,0:T(8,128)S(1)}, u32[]{:S(2)}, u32[]{:S(2)}) collective-permute-start(f32[8,256]{1,0:T(8,128)S(1)} %get-tuple-element.52.refs_0_), channel_id=1, source_target_pairs={{0,1},{1,2},{2,3},{3,0},{4,5},{5,6},{6,7},{7,4},{8,9},{9,10},{10,1... | collective-permute-start | bytes 24584 | tf_op jit(solution)/shard_map/ppermute | solution.py:357
  88.4 4.5 %collective-permute-start.14 = (f32[8,256]{1,0:T(8,128)S(1)}, f32[8,256]{1,0:T(8,128)S(1)}, u32[]{:S(2)}, u32[]{:S(2)}) collective-permute-start(f32[8,256]{1,0:T(8,128)S(1)} %get-tuple-element.52.refs_0_), channel_id=1, source_target_pairs={{0,2},{1,3},{2,0},{3,1},{4,6},{5,7},{6,4},{7,5},{8,10},{9,11},{10,... | collective-permute-start | bytes 24584 | tf_op jit(solution)/shard_map/ppermute | solution.py:357
  89.7 4.0 %collective-permute-start.15 = (f32[8,256]{1,0:T(8,128)S(1)}, f32[8,256]{1,0:T(8,128)S(1)}, u32[]{:S(2)}, u32[]{:S(2)}) collective-permute-start(f32[8,256]{1,0:T(8,128)S(1)} %get-tuple-element.52.refs_0_), channel_id=1, source_target_pairs={{0,3},{1,0},{2,1},{3,2},{4,7},{5,4},{6,5},{7,6},{8,11},{9,8},{10,9... | collective-permute-start | bytes 24584 | tf_op jit(solution)/shard_map/ppermute | solution.py:357

commit v3 on v2

--- a/solution.py
+++ b/solution.py
@@ -9,7 +9,8 @@
 
 EPSILON = 1e-06
 PARTS = 3
-COLUMNS = 1536
+COLUMNS = 1024
+SLOTS = 3
 VMEM_EXTRA = 4 * 1024 * 1024
 
 F32 = jnp.float32
@@ -55,60 +56,97 @@
     return [pl.ds(at, width) for at in range(0, columns, width)]
 
 
-def project_kernel(counts, first, picks, weight_rows, *refs):
+def project_kernel(counts, first, picks, weight_rows, later_rows, *refs):
     refs = list(refs)
     choices = [[refs.pop(0) for _ in range(count)] for count in counts]
     weight = refs.pop(0)
     if not first:
         refs.pop(0)
-    total, done, raw, turned, held, sem, weight_sems = refs
-    done[...] = jnp.zeros_like(done)
-    rows, columns = held.shape
-    blocks = column_blocks(columns)
+    total = refs.pop(0)
+    slab, done = (refs.pop(0), refs.pop(0)) if later_rows else (None, None)
+    raw, turned, sem, *rest = refs
+    rows = raw.shape[0]
+    blocks = column_blocks(weight.shape[1])
 
     start_features(of_place(picks), choices, raw, sem)
-    at = pl.ds(pl.multiple_of(of_place(weight_rows), 16), rows)
-    copies = [
-        pltpu.make_async_copy(weight.at[at, block], held.at[:, block], weight_sems.at[b])
-        for b, block in enumerate(blocks)
-    ]
-    for copy in copies:
+    copies = []
+    slots = 0
+    if weight_rows:
+        held, weight_sems = rest
+        slots = held.shape[0]
+        at = pl.ds(pl.multiple_of(of_place(weight_rows), 16), rows)
+        for b, block in enumerate(blocks):
+            copies.append(
+                pltpu.make_async_copy(
+                    weight.at[at, block], held.at[b % slots], weight_sems.at[b]
+                )
+            )
+    if later_rows:
+        done[...] = jnp.zeros_like(done)
+        later = pl.ds(pl.multiple_of(of_place(later_rows), 16), slab.shape[0])
+        slab_copy = pltpu.make_async_copy(
+            weight.at[later, :], slab, weight_sems.at[len(blocks)]
+        )
+    for copy in copies[:slots]:
         copy.start()
     wait_features(raw, sem)
     turned[...] = raw[...].T
-    for copy, block in zip(copies, blocks):
-        copy.wait()
-        product = jnp.dot(turned[...], held[:, block], preferred_element_type=F32)
+    for b, block in enumerate(blocks):
+        if weight_rows:
+            copies[b].wait()
+            matrix = held[b % slots]
+        else:
+            matrix = weight[0:rows, block]
+        product = jnp.dot(turned[...], matrix, preferred_element_type=F32)
         if first:
             total[:, block] = product
         else:
             total[:, block] += product
-
-
-def project(choices, picks, weight_rows, weight, total):
+        if b + slots < len(copies):
+            copies[b + slots].start()
+        if later_rows and b + slots == len(copies) - 1 + (slots == len(copies)):
+            slab_copy.start()
+    if later_rows:
+        slab_copy.wait()
+
+
+def project(choices, picks, weight, total, weight_rows=None, later_rows=None, later=0):
     counts = [len(pieces) for pieces in choices]
     rows = sum(piece.shape[0] for piece in choices[0])
     tokens, columns = choices[0][0].shape[1], weight.shape[1]
     first = total is None
     flat = [piece for pieces in choices for piece in pieces]
     operands = flat + [weight] + ([] if first else [total])
+    out_shape = [pltpu.VMEM((tokens, columns), F32)]
+    if later_rows:
+        out_shape += [pltpu.VMEM((later, columns), BF16), pltpu.VMEM((8, 128), F32)]
+    scratch = [
+        pltpu.VMEM((rows, tokens), BF16),
+        pltpu.VMEM((tokens, rows), BF16),
+        pltpu.SemaphoreType.DMA,
+    ]
+    scratch_bytes = 4 * rows * tokens
+    if weight_rows:
+        blocks = column_blocks(columns)
+        slots = min(SLOTS, len(blocks))
+        scratch += [
+            pltpu.VMEM((slots, rows, blocks[0].size), BF16),
+            pltpu.SemaphoreType.DMA((len(blocks) + 1,)),
+        ]
+        scratch_bytes += 2 * slots * rows * blocks[0].size
     return pl.pallas_call(
-        functools.partial(project_kernel, counts, first, picks, weight_rows),
-        out_shape=(pltpu.VMEM((tokens, columns), F32), pltpu.VMEM((8, 128), F32)),
-        in_specs=[HBM if first else ANY] * len(flat) + [HBM] + ([] if first else [WHOLE]),
-        out_specs=(WHOLE, WHOLE),
-        scratch_shapes=[
-            pltpu.VMEM((rows, tokens), BF16),
-            pltpu.VMEM((tokens, rows), BF16),
-            pltpu.VMEM((rows, columns), BF16),
-            pltpu.SemaphoreType.DMA,
-            pltpu.SemaphoreType.DMA((len(column_blocks(columns)),)),
-        ],
+        functools.partial(project_kernel, counts, first, picks, weight_rows, later_rows),
+        out_shape=out_shape,
+        in_specs=[HBM if first else ANY] * len(flat)
+        + [HBM if weight_rows else WHOLE]
+        + ([] if first else [WHOLE]),
+        out_specs=[WHOLE] * len(out_shape),
+        scratch_shapes=scratch,
         input_output_aliases={} if first else {len(operands) - 1: 0},
-        compiler_params=params(2 * rows * (columns + 2 * tokens)),
+        compiler_params=params(scratch_bytes),
         cost_estimate=pl.CostEstimate(
             flops=2 * tokens * rows * columns,
-            bytes_accessed=rows * columns * 2 + rows * tokens * 2,
+            bytes_accessed=(rows + later) * columns * 2 + rows * tokens * 2,
             transcendentals=0,
         ),
         name="project",
@@ -119,16 +157,18 @@
     return next(g for g in (4, 2, 1) if half % g == 0)
 
 
-def activate_heads(first_column, width, turned, held, total, act_ref, state_ref, arrived):
+def activate_heads(side, width, turned, slab, total, act_ref, state_ref):
     half = state_ref.shape[0]
     group = PARTS * width
     at_once = heads_at_once(half)
     for h in range(0, half, at_once):
-        arrived(h // at_once)
         here = slice(h * group, (h + at_once) * group)
-        block = pl.ds(pl.multiple_of(first_column + h * group, group), at_once * group)
+        column = pl.multiple_of((side * half + h) * group, group)
+        block = pl.ds(column, at_once * group)
         projected = total[:, block] + jnp.dot(
-            turned[...], held[:, here], preferred_element_type=F32
+            turned[...],
+            slab[slab.shape[0] - turned.shape[1] :, block],
+            preferred_element_type=F32,
         )
         act = (projected / (1.0 + jnp.exp(-projected))).astype(BF16)
         act_ref[:, here] = act
@@ -142,53 +182,29 @@
             )
 
 
-def first_kernel(n_choices, width, picks, weight_rows, *refs):
-    choices = [[ref] for ref in refs[:n_choices]]
-    weight, total, turned, rest, act_ref, state_ref, raw, held, sem, weight_sems = refs[
-        n_choices:
-    ]
-    rows, columns = held.shape
-    block = heads_at_once(state_ref.shape[0]) * PARTS * width
-    core = lax.axis_index("context") % 2
-    start_features(of_place(picks), choices, raw, sem)
-    at = pl.ds(pl.multiple_of(of_place(weight_rows), 16), rows)
-    copies = []
-    for b in range(columns // block):
-        here = pl.ds(pl.multiple_of((1 - core) * columns + b * block, block), block)
-        there = held.at[:, pl.ds(b * block, block)]
-        copies.append(pltpu.make_async_copy(weight.at[at, here], there, weight_sems.at[b]))
-    here = pl.ds(pl.multiple_of(core * columns, block), columns)
-    rest_copy = pltpu.make_async_copy(weight.at[at, here], rest, weight_sems.at[len(copies)])
-    for copy in copies:
-        copy.start()
-    rest_copy.start()
-    wait_features(raw, sem)
-    turned[...] = raw[...].T
-    activate_heads(
-        (1 - core) * columns,
-        width,
-        turned,
-        held,
-        total,
-        act_ref,
-        state_ref,
-        lambda b: copies[b].wait(),
-    )
-    rest_copy.wait()
-
-
-def second_kernel(width, turned, held, total, act_ref, state_ref):
-    core = lax.axis_index("context") % 2
-    activate_heads(
-        core * held.shape[1], width, turned, held, total, act_ref, state_ref, lambda b: None
-    )
-
-
-def activate(choices, picks, weight_rows, weight, total, heads, width):
+def first_kernel(n_choices, width, picks, *refs):
+    choices = refs[:n_choices]
+    slab, total, turned, act_ref, state_ref = refs[n_choices:]
+    pick = of_place(picks)
+    for c, choice in enumerate(choices):
+
+        @pl.when(pick == c)
+        def _(choice=choice):
+            turned[...] = choice[...].T
+
+    side = 1 - lax.axis_index("context") % 2
+    activate_heads(side, width, turned, slab, total, act_ref, state_ref)
+
+
+def second_kernel(width, turned, slab, total, act_ref, state_ref):
+    side = lax.axis_index("context") % 2
+    activate_heads(side, width, turned, slab, total, act_ref, state_ref)
+
+
+def activate(choices, picks, slab, total, heads, width):
     rows, tokens = choices[0].shape
     half = heads // 2
     columns = half * PARTS * width
-    blocks = half // heads_at_once(half)
     outs = (
         pltpu.VMEM((tokens, columns), BF16),
         pltpu.VMEM((half, width, width), F32),
@@ -198,21 +214,15 @@
         bytes_accessed=rows * tokens * 2,
         transcendentals=tokens * columns,
     )
-    turned, rest, act_other, state_other = pl.pallas_call(
-        functools.partial(first_kernel, len(choices), width, picks, weight_rows),
-        out_shape=(pltpu.VMEM((tokens, rows), BF16), pltpu.VMEM((rows, columns), BF16)) + outs,
-        in_specs=[ANY] * len(choices) + [HBM, WHOLE],
-        out_specs=(WHOLE,) * 4,
-        scratch_shapes=[
-            pltpu.VMEM((rows, tokens), BF16),
-            pltpu.VMEM((rows, columns), BF16),
-            pltpu.SemaphoreType.DMA,
-            pltpu.SemaphoreType.DMA((blocks + 1,)),
-        ],
-        compiler_params=params(2 * rows * (columns + tokens)),
+    turned, act_other, state_other = pl.pallas_call(
+        functools.partial(first_kernel, len(choices), width, picks),
+        out_shape=(pltpu.VMEM((tokens, rows), BF16),) + outs,
+        in_specs=[WHOLE] * (len(choices) + 2),
+        out_specs=(WHOLE,) * 3,
+        compiler_params=params(0),
         cost_estimate=cost,
         name="activate",
-    )(*choices, weight, total)
+    )(*choices, slab, total)
     act_own, state_own = pl.pallas_call(
         functools.partial(second_kernel, width),
         out_shape=outs,
@@ -221,7 +231,7 @@
         compiler_params=params(0),
         cost_estimate=cost,
         name="activate",
-    )(turned, rest, total)
+    )(turned, slab, total)
     return act_other, state_other, act_own, state_own
 
 
@@ -387,8 +397,7 @@
         else:
             for ref in downs:
                 before = before + ref[h - cut].astype(F32)
-            message = total
-            if n_down and not final:
+            if not final:
                 message = before + jnp.where(has(bits[-1 - n_down]), 0.0, total)
         if final:
             for_mate, mine = refs[-2:]
@@ -429,21 +438,16 @@
     theirs = lax.ppermute(other_states, "context", swap)
     bits = [1 << b for b in range((chips - 1).bit_length())]
 
-    def send(x, bit, both):
-        pairs = [
-            (2 * i + c, 2 * (i ^ bit) + c)
-            for i in range(chips)
-            for c in range(2)
-            if both or not i & bit
-        ]
+    def send(x, bit):
+        pairs = [(2 * i + c, 2 * (i ^ bit) + c) for i in range(chips) for c in range(2)]
         return lax.ppermute(x, "context", pairs)
 
     ups, downs = [], []
     for step, (rise, fall) in enumerate(zip(bits, bits[::-1])):
         messages = meet(bits, own, theirs, ups, downs, after if step == 1 else [], False)
         if cut:
-            ups = ups + [send(messages[0], rise, step < len(bits) - 1)]
-        downs = downs + [send(messages[-1], fall, step > 0)]
+            ups = ups + [send(messages[0], rise)]
+        downs = downs + [send(messages[-1], fall)]
     for_mate, mine = meet(bits, own, theirs, ups, downs, [], True)
     return lax.ppermute(for_mate, "context", swap), mine
 
@@ -458,7 +462,10 @@
                 here = share + way * t
                 if 0 <= here < n and 0 <= here + way < n:
                     pairs[chain][t].append((here, here + way))
+                    if t == 1 and chain == 1:
+                        pairs[chain][t].append((here + way, here))
                     arrivals[here + way].append((t, chain, share))
+    pairs = [[sorted(set(p)) for p in chain] for chain in pairs]
     return pairs, arrivals
 
 
@@ -471,8 +478,16 @@
         return [x[:early], x[early:]]
 
     pairs, arrivals = hops(n_tensor)
-    starts = [i * share for i in range(n_tensor)]
-    total, done = project([[tokens_t]], [0] * n_tensor, starts, qkv_weight, None)
+    last = n_tensor - 2
+    total, slab, done = project(
+        [[tokens_t]],
+        [0] * n_tensor,
+        qkv_weight,
+        None,
+        [i * share for i in range(n_tensor)],
+        [there[last][2] * share for there in arrivals],
+        share,
+    )
     held = [[tokens_t], [tokens_t]]
     came = {}
     for t in range(n_tensor - 1):
@@ -486,19 +501,18 @@
                 came[t, chain] = held[chain]
 
     for m in range(n_tensor - 1):
-        keys = sorted({came_at[m][:2] for came_at in arrivals})
-        picks = [keys.index(came_at[m][:2]) for came_at in arrivals]
-        rows = [came_at[m][2] * share for came_at in arrivals]
+        keys = sorted({there[m][:2] for there in arrivals})
+        picks = [keys.index(there[m][:2]) for there in arrivals]
         choices = [came[key] for key in keys]
-        if m < n_tensor - 2:
-            total, _ = project(choices, picks, rows, qkv_weight, total)
+        if m < last:
+            rows = [there[m][2] * share for there in arrivals]
+            (total,) = project(choices, picks, qkv_weight, total, rows)
         else:
             choices = [c if len(c) == 2 else cut(c[0]) for c in choices]
-            total, _ = project([c[:1] for c in choices], picks, rows, qkv_weight, total)
-            rows = [row + early for row in rows]
-            other_act, other_states, own_act, own_states = activate(
-                [c[1] for c in choices], picks, rows, qkv_weight, total, heads, width
-            )
+            (total,) = project([c[:1] for c in choices], picks, slab, total)
+    other_act, other_states, own_act, own_states = activate(
+        [c[1] for c in choices], picks, slab, total, heads, width
+    )
     acts = (other_act, own_act)
     *withins, done = attend_within(*acts, width)
     other, own = earlier_states(other_states, own_states, [done], n_context)

time: 95.6 us -> 88.3 us (0.924)
  starting transfers between devices: 27.9 us -> 23.5 us
  waiting for transfers between devices: 25.6 us -> 22.2 us
    ppermute x7, waiting for transfers between devices: 16.5 us -> 10.4 us  [body(): lax.ppermute(x, 'tensor', pairs[chain][t])]
    ppermute x4, starting transfers between devices: 10.2 us -> 5.19 us  [send(): return lax.ppermute(x, 'context', pairs)]
    ppermute x7, starting transfers between devices: 11.8 us -> 14.3 us  [body(): lax.ppermute(x, 'tensor', pairs[chain][t])]
    pallas_call x4, Pallas kernels: 29.6 us -> 31.9 us  [project(): pl.pallas_call(functools.partial(project_kernel, counts, first, picks, we...]
    ppermute x3, starting transfers between devices: 5.72 us -> 3.86 us  [terms_over_tensor(): lax.ppermute(x, 'tensor', [(i, (i + d) % n) for i in range(n)])]
    pallas_call x1, Pallas kernels: 4.33 us -> 2.55 us  [activate(): pl.pallas_call(functools.partial(first_kernel, len(choices), width, picks...]
    ppermute x3, waiting for transfers between devices: 1.37 us -> 2.86 us  [terms_over_tensor(): lax.ppermute(x, 'tensor', [(i, (i + d) % n) for i in range(n)])]
    ppermute x4, waiting for transfers between devices: 5.82 us -> 7.03 us  [send(): return lax.ppermute(x, 'context', pairs)]
  transfers between devices with their start and end apart: 16 -> 16, of which waited for: 10 -> 10; matrix products, arithmetic and copies ran while one was open for 0% -> 0% of each run, Pallas kernels for 35% -> 40%
where the time goes in v3:
time: 88.3 us; the launch traced here: 88 us
  Pallas kernels  41 us (46%)
  starting transfers between devices  23.5 us (27%)
  waiting for transfers between devices  22.2 us (25%)
  local copies, waits for them, and re-layouts  1.23 us (1%)
    pallas_call x4, Pallas kernels, project(): pl.pallas_call(functools.partial(project_kernel, counts, first, picks, we...  31.9 us
    ppermute x7, starting transfers between devices, body(): lax.ppermute(x, 'tensor', pairs[chain][t])  14.3 us
    ppermute x7, waiting for transfers between devices, body(): lax.ppermute(x, 'tensor', pairs[chain][t])  10.4 us
    ppermute x4, waiting for transfers between devices, send(): return lax.ppermute(x, 'context', pairs)  7.03 us
    ppermute x4, starting transfers between devices, send(): return lax.ppermute(x, 'context', pairs)  5.19 us
    ppermute x3, starting transfers between devices, terms_over_tensor(): lax.ppermute(x, 'tensor', [(i, (i + d) % n) for i in range(n)])  3.86 us
    ppermute x3, waiting for transfers between devices, terms_over_tensor(): lax.ppermute(x, 'tensor', [(i, (i + d) % n) for i in range(n)])  2.86 us
    pallas_call x1, Pallas kernels, activate(): pl.pallas_call(functools.partial(first_kernel, len(choices), width, picks...  2.55 us
  transfers between devices with their start and end apart: 16, of which 10 were waited for; matrix products, arithmetic and copies ran while one was open for 0% of the time, Pallas kernels for 40%

profile of v3, /device:TPU:0, one launch (start us, length us, event | category | flops | bytes accessed | tf_op | source)
XLA Modules:
  0.0 88.0 jit_solution(8604440686176424534)
XLA Ops:
  0.0 0.7 collective-permute-start.5
  0.7 5.9 %collective-permute-start = (bf16[1536,256]{1,0:T(8,128)(2,1)}, bf16[1536,256]{1,0:T(8,128)(2,1)S(1)}, u32[]{:S(2)}, u32[]{:S(2)}) collective-permute-start(bf16[1536,256]{1,0:T(8,128)(2,1)} %refs_0_.1), channel_id=1, source_target_pairs={{0,1},{1,0},{2,3},{3,2},{4,5},{5,4},{6,7},{7,6},{8,9},{9,8},{10,11... | collective-permute-start | bytes 2359304 | tf_op jit(solution)/shard_map/ppermute | solution.py:500
  6.6 1.2 %copy-done.1 = bf16[1536,256]{1,0:T(8,128)(2,1)S(1)} copy-done((bf16[1536,256]{1,0:T(8,128)(2,1)S(1)}, bf16[1536,256]{1,0:T(8,128)(2,1)}, u32[]{:S(2)}) %copy-start.1) | copy-done | bytes 786456
  7.7 12.9 %project.4 = (f32[256,6144]{1,0:T(8,128)S(1)}, bf16[1536,6144]{1,0:T(8,128)(2,1)S(1)}, f32[8,128]{1,0:T(8,128)}) custom-call(bf16[1536,256]{1,0:T(8,128)(2,1)S(1)} %copy-done.1, bf16[6144,6144]{1,0:T(8,128)(2,1)} %refs_2_.1), custom_call_target="tpu_custom_call" | custom-call | flops 4831838208 | bytes 38535168 | tf_op jit(solution)/shard_map/project/pallas_call | solution.py:137
  20.6 0.0 collective-permute-done.5.refs_0_
  20.6 3.8 %collective-permute-start.6 = (bf16[1536,256]{1,0:T(8,128)(2,1)S(1)}, bf16[1536,256]{1,0:T(8,128)(2,1)S(1)}, u32[]{:S(2)}, u32[]{:S(2)}) collective-permute-start(bf16[1536,256]{1,0:T(8,128)(2,1)S(1)} %collective-permute-done.5.refs_0_), channel_id=1, source_target_pairs={{0,1},{1,0},{2,3},{3,2},{4,5},{5,4},{6,7},{7,6},{8,9},{9,8},{10,11... | collective-permute-start | bytes 2359304 | tf_op jit(solution)/shard_map/ppermute | solution.py:500
  24.4 0.0 collective-permute-done.refs_0_
  24.4 0.1 fusion
  24.5 0.7 collective-permute-start.3
  25.2 0.7 collective-permute-start.1
  25.8 8.0 %project.5.refs_3_ = f32[256,6144]{1,0:T(8,128)S(1)} custom-call(bf16[1536,256]{1,0:T(8,128)(2,1)S(1)} %collective-permute-done.refs_0_, bf16[6144,6144]{1,0:T(8,128)(2,1)} %refs_2_.1, f32[256,6144]{1,0:T(8,128)S(1)} %get-tuple-element.30.refs_2_), custom_call_target="tpu_custom_call", output_to_operand_aliasing={{}: (2, {})} | custom-call | flops 4831838208 | bytes 19660800 | tf_op jit(solution)/shard_map/project/pallas_call | solution.py:137
  33.8 0.0 collective-permute-done.3.refs_0_
  33.9 1.3 %collective-permute-start.4 = (bf16[768,256]{1,0:T(8,128)(2,1)S(1)}, bf16[768,256]{1,0:T(8,128)(2,1)S(1)}, u32[]{:S(2)}, u32[]{:S(2)}) collective-permute-start(bf16[768,256]{1,0:T(8,128)(2,1)S(1)} %collective-permute-done.3.refs_0_), channel_id=1, source_target_pairs={{1,0},{2,3},{5,4},{6,7},{9,8},{10,11},{13,12},{14,15},{17,16},{18,... | collective-permute-start | bytes 1179656 | tf_op jit(solution)/shard_map/ppermute | solution.py:500
  35.2 0.0 collective-permute-done.1.refs_0_
  35.2 1.3 %collective-permute-start.2 = (bf16[768,256]{1,0:T(8,128)(2,1)S(1)}, bf16[768,256]{1,0:T(8,128)(2,1)S(1)}, u32[]{:S(2)}, u32[]{:S(2)}) collective-permute-start(bf16[768,256]{1,0:T(8,128)(2,1)S(1)} %collective-permute-done.1.refs_0_), channel_id=1, source_target_pairs={{1,0},{2,3},{5,4},{6,7},{9,8},{10,11},{13,12},{14,15},{17,16},{18,... | collective-permute-start | bytes 1179656 | tf_op jit(solution)/shard_map/ppermute | solution.py:500
  36.5 5.7 %collective-permute-done.6.refs_1_ = bf16[1536,256]{1,0:T(8,128)(2,1)S(1)} collective-permute-done((bf16[1536,256]{1,0:T(8,128)(2,1)S(1)}, bf16[1536,256]{1,0:T(8,128)(2,1)S(1)}, u32[]{:S(2)}, u32[]{:S(2)}) %collective-permute-start.6) | collective-permute-done | bytes 786464 | tf_op jit(solution)/shard_map/ppermute | solution.py:500
  42.1 8.2 %project.6.refs_3_ = f32[256,6144]{1,0:T(8,128)S(1)} custom-call(bf16[1536,256]{1,0:T(8,128)(2,1)S(1)} %collective-permute-done.5.refs_0_, bf16[1536,256]{1,0:T(8,128)(2,1)S(1)} %collective-permute-done.6.refs_1_, bf16[6144,6144]{1,0:T(8,128)(2,1)} %refs_2_.1, f32[256,6144]{1,0:T(8,128)S(1)} %project.5.refs_3_), custom_call_target="tpu_custom_call", output_to_operand_aliasing={{}: (3, {})} | custom-call | flops 4831838208 | bytes 19660800 | tf_op jit(solution)/shard_map/project/pallas_call | solution.py:137
  50.3 0.8 collective-permute-done.4.refs_1_
  51.1 2.9 %project.7.refs_3_.total = f32[256,6144]{1,0:T(8,128)S(1)} custom-call(bf16[768,256]{1,0:T(8,128)(2,1)S(1)} %collective-permute-done.3.refs_0_, bf16[768,256]{1,0:T(8,128)(2,1)S(1)} %collective-permute-done.4.refs_1_, bf16[1536,6144]{1,0:T(8,128)(2,1)S(1)} %get-tuple-element.28.refs_2_.slab, ...), custom_call_target="tpu_custom_call", output_to_operand_aliasing={{}: (3, {})} | custom-call | flops 2415919104 | bytes 9830400 | tf_op jit(solution)/shard_map/project/pallas_call | solution.py:137
  54.0 3.9 %collective-permute-done.2.refs_1_ = bf16[768,256]{1,0:T(8,128)(2,1)S(1)} collective-permute-done((bf16[768,256]{1,0:T(8,128)(2,1)S(1)}, bf16[768,256]{1,0:T(8,128)(2,1)S(1)}, u32[]{:S(2)}, u32[]{:S(2)}) %collective-permute-start.2) | collective-permute-done | bytes 393248 | tf_op jit(solution)/shard_map/ppermute | solution.py:500
  57.9 2.6 %activate.2 = (bf16[256,768]{1,0:T(8,128)(2,1)S(1)}, bf16[256,3072]{1,0:T(8,128)(2,1)S(1)}, f32[8,128,128]{2,1,0:T(8,128)S(1)}) custom-call(bf16[768,256]{1,0:T(8,128)(2,1)S(1)} %collective-permute-done.1.refs_0_, bf16[768,256]{1,0:T(8,128)(2,1)S(1)} %collective-permute-done.2.refs_1_, bf16[1536,6144]{1,0:T(8,128)(2,1)S(1)} %get-tuple-element.28.refs_2_.slab, ...), custom_call_target="tpu_custom_call" | custom-call | flops 1275068416 | bytes 393216 | tf_op jit(solution)/shard_map/activate/pallas_call | solution.py:217
  60.5 0.1 collective-permute-start.7
  60.6 2.2 %activate.3 = (bf16[256,3072]{1,0:T(8,128)(2,1)S(1)}, f32[8,128,128]{2,1,0:T(8,128)S(1)}) custom-call(bf16[256,768]{1,0:T(8,128)(2,1)S(1)} %get-tuple-element.32.turned, bf16[1536,6144]{1,0:T(8,128)(2,1)S(1)} %get-tuple-element.28.refs_2_.slab, f32[256,6144]{1,0:T(8,128)S(1)} %project.7.refs_3_.total), custom_call_target="tpu_custom_call" | custom-call | flops 1275068416 | bytes 393216 | tf_op jit(solution)/shard_map/activate/pallas_call | solution.py:226
  62.8 0.0 copy-start
  62.8 0.0 collective-permute-done.7.refs_1_
  62.8 0.1 meet.3
  62.8 1.6 %collective-permute-start.8 = (bf16[4,128,128]{2,1,0:T(8,128)(2,1)S(1)}, bf16[4,128,128]{2,1,0:T(8,128)(2,1)S(1)}, u32[]{:S(2)}, u32[]{:S(2)}) collective-permute-start(bf16[4,128,128]{2,1,0:T(8,128)(2,1)S(1)} %get-tuple-element.38), channel_id=1, source_target_pairs={{0,8},{4,12},{8,0},{12,4},{16,24},{20,28},{24,16},{28,20},{1,9},{5... | collective-permute-start | bytes 393224 | tf_op jit(solution)/shard_map/ppermute | solution.py:443
  64.4 1.5 %collective-permute-start.9 = (bf16[4,128,128]{2,1,0:T(8,128)(2,1)S(1)}, bf16[4,128,128]{2,1,0:T(8,128)(2,1)S(1)}, u32[]{:S(2)}, u32[]{:S(2)}) collective-permute-start(bf16[4,128,128]{2,1,0:T(8,128)(2,1)S(1)} %get-tuple-element.39), channel_id=1, source_target_pairs={{0,16},{4,20},{8,24},{12,28},{16,0},{20,4},{24,8},{28,12},{1,17},{... | collective-permute-start | bytes 393224 | tf_op jit(solution)/shard_map/ppermute | solution.py:443
  65.9 1.5 %within.1 = (f32[256,1024]{1,0:T(8,128)S(1)}, f32[256,1024]{1,0:T(8,128)S(1)}, f32[8,128]{1,0:T(8,128)S(1)}) custom-call(bf16[256,3072]{1,0:T(8,128)(2,1)S(1)} %get-tuple-element.31.refs_0_.act_other, bf16[256,3072]{1,0:T(8,128)(2,1)S(1)} %get-tuple-element.33.refs_1_.act_own), custom_call_target="tpu_custom_call" | custom-call | flops 536870912 | bytes 3145728 | tf_op jit(solution)/shard_map/within/pallas_call | solution.py:262
  67.4 1.4 %collective-permute-done.8.refs_2_ = bf16[4,128,128]{2,1,0:T(8,128)(2,1)S(1)} collective-permute-done((bf16[4,128,128]{2,1,0:T(8,128)(2,1)S(1)}, bf16[4,128,128]{2,1,0:T(8,128)(2,1)S(1)}, u32[]{:S(2)}, u32[]{:S(2)}) %collective-permute-start.8) | collective-permute-done | bytes 131104 | tf_op jit(solution)/shard_map/ppermute | solution.py:443
  68.8 1.2 %collective-permute-done.9.refs_3_.refs_4_ = bf16[4,128,128]{2,1,0:T(8,128)(2,1)S(1)} collective-permute-done((bf16[4,128,128]{2,1,0:T(8,128)(2,1)S(1)}, bf16[4,128,128]{2,1,0:T(8,128)(2,1)S(1)}, u32[]{:S(2)}, u32[]{:S(2)}) %collective-permute-start.9) | collective-permute-done | bytes 131104 | tf_op jit(solution)/shard_map/ppermute | solution.py:443
  70.0 0.1 meet.4
  70.1 1.6 %collective-permute-start.10 = (bf16[4,128,128]{2,1,0:T(8,128)(2,1)S(1)}, bf16[4,128,128]{2,1,0:T(8,128)(2,1)S(1)}, u32[]{:S(2)}, u32[]{:S(2)}) collective-permute-start(bf16[4,128,128]{2,1,0:T(8,128)(2,1)S(1)} %get-tuple-element.41), channel_id=1, source_target_pairs={{0,16},{4,20},{8,24},{12,28},{16,0},{20,4},{24,8},{28,12},{1,17},{... | collective-permute-start | bytes 393224 | tf_op jit(solution)/shard_map/ppermute | solution.py:443
  71.7 0.5 collective-permute-start.11
  72.2 2.9 %collective-permute-done.10.refs_3_ = bf16[4,128,128]{2,1,0:T(8,128)(2,1)S(1)} collective-permute-done((bf16[4,128,128]{2,1,0:T(8,128)(2,1)S(1)}, bf16[4,128,128]{2,1,0:T(8,128)(2,1)S(1)}, u32[]{:S(2)}, u32[]{:S(2)}) %collective-permute-start.10) | collective-permute-done | bytes 131104 | tf_op jit(solution)/shard_map/ppermute | solution.py:443
  75.1 1.5 %collective-permute-done.11.refs_5_ = bf16[4,128,128]{2,1,0:T(8,128)(2,1)S(1)} collective-permute-done((bf16[4,128,128]{2,1,0:T(8,128)(2,1)S(1)}, bf16[4,128,128]{2,1,0:T(8,128)(2,1)S(1)}, u32[]{:S(2)}, u32[]{:S(2)}) %collective-permute-start.11) | collective-permute-done | bytes 131104 | tf_op jit(solution)/shard_map/ppermute | solution.py:443
  76.6 0.2 meet.5
  76.8 0.1 collective-permute-start.12
  76.9 1.9 %collective-permute-done.12.other = f32[8,128,128]{2,1,0:T(8,128)S(1)} collective-permute-done((f32[8,128,128]{2,1,0:T(8,128)S(1)}, f32[8,128,128]{2,1,0:T(8,128)S(1)}, u32[]{:S(2)}, u32[]{:S(2)}) %collective-permute-start.12) | collective-permute-done | bytes 524320 | tf_op jit(solution)/shard_map/ppermute | solution.py:452
  78.8 0.0 copy-done
  78.8 1.0 %across.1 = (f32[256,2048]{1,0:T(8,128)S(1)}, f32[8,256]{1,0:T(8,128)S(1)}) custom-call(bf16[256,3072]{1,0:T(8,128)(2,1)S(1)} %get-tuple-element.31.refs_0_.act_other, bf16[256,3072]{1,0:T(8,128)(2,1)S(1)} %get-tuple-element.33.refs_1_.act_own, f32[256,1024]{1,0:T(8,128)S(1)} %get-tuple-element.34.within_other, ...), custom_call_target="tpu_custom_call" | custom-call | flops 268435456 | tf_op jit(solution)/shard_map/across/pallas_call | solution.py:315
  79.8 0.4 collective-permute-start.13
  80.2 2.6 %collective-permute-start.14 = (f32[8,256]{1,0:T(8,128)S(1)}, f32[8,256]{1,0:T(8,128)S(1)}, u32[]{:S(2)}, u32[]{:S(2)}) collective-permute-start(f32[8,256]{1,0:T(8,128)S(1)} %get-tuple-element.46.refs_0_), channel_id=1, source_target_pairs={{0,2},{1,3},{2,0},{3,1},{4,6},{5,7},{6,4},{7,5},{8,10},{9,11},{10,... | collective-permute-start | bytes 24584 | tf_op jit(solution)/shard_map/ppermute | solution.py:367
  82.9 0.8 collective-permute-start.15
  83.6 1.6 %collective-permute-done.13.refs_1_ = f32[8,256]{1,0:T(8,128)S(1)} collective-permute-done((f32[8,256]{1,0:T(8,128)S(1)}, f32[8,256]{1,0:T(8,128)S(1)}, u32[]{:S(2)}, u32[]{:S(2)}) %collective-permute-start.13) | collective-permute-done | bytes 8224 | tf_op jit(solution)/shard_map/ppermute | solution.py:367
  85.3 0.0 collective-permute-done.14.refs_2_
  85.3 1.2 %collective-permute-done.15.refs_3_ = f32[8,256]{1,0:T(8,128)S(1)} collective-permute-done((f32[8,256]{1,0:T(8,128)S(1)}, f32[8,256]{1,0:T(8,128)S(1)}, u32[]{:S(2)}, u32[]{:S(2)}) %collective-permute-start.15) | collective-permute-done | bytes 8224 | tf_op jit(solution)/shard_map/ppermute | solution.py:367
  86.5 1.5 %normalize.1 = bf16[256,2048]{1,0:T(8,128)(2,1)} custom-call(f32[256,2048]{1,0:T(8,128)S(1)} %get-tuple-element.45.att_ref, f32[1,2048]{1,0:T(1,128)S(1)} %bitcast.1, f32[8,256]{1,0:T(8,128)S(1)} %get-tuple-element.46.refs_0_, f32[8,256]{1,0:T(8,128)S(1)} %collective-permute-done.13.refs_1_, f32[8,256]{1,0:T(8,128)S(1)} %collective-permute-done.14.refs_2_, ...), custom_call_target="tpu_custom_call" | custom-call | flops 1048576 | bytes 1048576 | tf_op jit(solution)/shard_map/normalize/pallas_call | solution.py:351
  (3 shorter events, 0.0 us)
Async XLA Ops:
  0.0 20.6 %collective-permute-start.5 = (bf16[1536,256]{1,0:T(8,128)(2,1)}, bf16[1536,256]{1,0:T(8,128)(2,1)S(1)}, u32[]{:S(2)}, u32[]{:S(2)}) collective-permute-start(bf16[1536,256]{1,0:T(8,128)(2,1)} %refs_0_.1), channel_id=1, source_target_pairs={{1,2},{2,1},{5,6},{6,5},{9,10},{10,9},{13,14},{14,13},{17,18},{18,... | collective-permute-start | bytes 2359304 | tf_op jit(solution)/shard_map/ppermute | solution.py:500
  0.7 23.7 %collective-permute-start = (bf16[1536,256]{1,0:T(8,128)(2,1)}, bf16[1536,256]{1,0:T(8,128)(2,1)S(1)}, u32[]{:S(2)}, u32[]{:S(2)}) collective-permute-start(bf16[1536,256]{1,0:T(8,128)(2,1)} %refs_0_.1), channel_id=1, source_target_pairs={{0,1},{1,0},{2,3},{3,2},{4,5},{5,4},{6,7},{7,6},{8,9},{9,8},{10,11... | collective-permute-start | bytes 2359304 | tf_op jit(solution)/shard_map/ppermute | solution.py:500
  6.6 1.2 %copy-start.1 = (bf16[1536,256]{1,0:T(8,128)(2,1)S(1)}, bf16[1536,256]{1,0:T(8,128)(2,1)}, u32[]{:S(2)}) copy-start(bf16[1536,256]{1,0:T(8,128)(2,1)} %refs_0_.1) | copy-start | bytes 2359300
  20.6 21.5 %collective-permute-start.6 = (bf16[1536,256]{1,0:T(8,128)(2,1)S(1)}, bf16[1536,256]{1,0:T(8,128)(2,1)S(1)}, u32[]{:S(2)}, u32[]{:S(2)}) collective-permute-start(bf16[1536,256]{1,0:T(8,128)(2,1)S(1)} %collective-permute-done.5.refs_0_), channel_id=1, source_target_pairs={{0,1},{1,0},{2,3},{3,2},{4,5},{5,4},{6,7},{7,6},{8,9},{9,8},{10,11... | collective-permute-start | bytes 2359304 | tf_op jit(solution)/shard_map/ppermute | solution.py:500
  24.5 9.4 %collective-permute-start.3 = (bf16[768,256]{1,0:T(8,128)(2,1)S(1)}, bf16[768,256]{1,0:T(8,128)(2,1)S(1)}, u32[]{:S(2)}, u32[]{:S(2)}) collective-permute-start(bf16[768,256]{1,0:T(8,128)(2,1)S(1)} %get-tuple-element.47), channel_id=1, source_target_pairs={{1,2},{2,1},{5,6},{6,5},{9,10},{10,9},{13,14},{14,13},{17,18},{18,... | collective-permute-start | bytes 1179656 | tf_op jit(solution)/shard_map/ppermute | solution.py:500
  25.2 10.0 %collective-permute-start.1 = (bf16[768,256]{1,0:T(8,128)(2,1)S(1)}, bf16[768,256]{1,0:T(8,128)(2,1)S(1)}, u32[]{:S(2)}, u32[]{:S(2)}) collective-permute-start(bf16[768,256]{1,0:T(8,128)(2,1)S(1)} %get-tuple-element.48), channel_id=1, source_target_pairs={{1,2},{2,1},{5,6},{6,5},{9,10},{10,9},{13,14},{14,13},{17,18},{18,... | collective-permute-start | bytes 1179656 | tf_op jit(solution)/shard_map/ppermute | solution.py:500
  33.9 17.2 %collective-permute-start.4 = (bf16[768,256]{1,0:T(8,128)(2,1)S(1)}, bf16[768,256]{1,0:T(8,128)(2,1)S(1)}, u32[]{:S(2)}, u32[]{:S(2)}) collective-permute-start(bf16[768,256]{1,0:T(8,128)(2,1)S(1)} %collective-permute-done.3.refs_0_), channel_id=1, source_target_pairs={{1,0},{2,3},{5,4},{6,7},{9,8},{10,11},{13,12},{14,15},{17,16},{18,... | collective-permute-start | bytes 1179656 | tf_op jit(solution)/shard_map/ppermute | solution.py:500
  35.2 22.7 %collective-permute-start.2 = (bf16[768,256]{1,0:T(8,128)(2,1)S(1)}, bf16[768,256]{1,0:T(8,128)(2,1)S(1)}, u32[]{:S(2)}, u32[]{:S(2)}) collective-permute-start(bf16[768,256]{1,0:T(8,128)(2,1)S(1)} %collective-permute-done.1.refs_0_), channel_id=1, source_target_pairs={{1,0},{2,3},{5,4},{6,7},{9,8},{10,11},{13,12},{14,15},{17,16},{18,... | collective-permute-start | bytes 1179656 | tf_op jit(solution)/shard_map/ppermute | solution.py:500
  60.5 2.3 %collective-permute-start.7 = (f32[8,128,128]{2,1,0:T(8,128)S(1)}, f32[8,128,128]{2,1,0:T(8,128)S(1)}, u32[]{:S(2)}, u32[]{:S(2)}) collective-permute-start(f32[8,128,128]{2,1,0:T(8,128)S(1)} %get-tuple-element.37), channel_id=1, source_target_pairs={{0,4},{4,0},{8,12},{12,8},{16,20},{20,16},{24,28},{28,24},{1,5},{5... | collective-permute-start | bytes 1572872 | tf_op jit(solution)/shard_map/ppermute | solution.py:438
  62.8 16.0 %copy-start = (f32[16,128,128]{2,1,0:T(8,128)S(1)}, f32[16,128,128]{2,1,0:T(8,128)}, u32[]{:S(2)}) copy-start(f32[16,128,128]{2,1,0:T(8,128)} %prior.1) | copy-start | bytes 3145732
  62.8 5.9 %collective-permute-start.8 = (bf16[4,128,128]{2,1,0:T(8,128)(2,1)S(1)}, bf16[4,128,128]{2,1,0:T(8,128)(2,1)S(1)}, u32[]{:S(2)}, u32[]{:S(2)}) collective-permute-start(bf16[4,128,128]{2,1,0:T(8,128)(2,1)S(1)} %get-tuple-element.38), channel_id=1, source_target_pairs={{0,8},{4,12},{8,0},{12,4},{16,24},{20,28},{24,16},{28,20},{1,9},{5... | collective-permute-start | bytes 393224 | tf_op jit(solution)/shard_map/ppermute | solution.py:443
  64.4 5.6 %collective-permute-start.9 = (bf16[4,128,128]{2,1,0:T(8,128)(2,1)S(1)}, bf16[4,128,128]{2,1,0:T(8,128)(2,1)S(1)}, u32[]{:S(2)}, u32[]{:S(2)}) collective-permute-start(bf16[4,128,128]{2,1,0:T(8,128)(2,1)S(1)} %get-tuple-element.39), channel_id=1, source_target_pairs={{0,16},{4,20},{8,24},{12,28},{16,0},{20,4},{24,8},{28,12},{1,17},{... | collective-permute-start | bytes 393224 | tf_op jit(solution)/shard_map/ppermute | solution.py:443
  65.9 20.6 %copy-start.2 = (f32[2048]{0:T(1024)S(1)}, f32[2048]{0:T(1024)}, u32[]{:S(2)}) copy-start(f32[2048]{0:T(1024)} %param.7) | copy-start | bytes 24580
  70.1 5.0 %collective-permute-start.10 = (bf16[4,128,128]{2,1,0:T(8,128)(2,1)S(1)}, bf16[4,128,128]{2,1,0:T(8,128)(2,1)S(1)}, u32[]{:S(2)}, u32[]{:S(2)}) collective-permute-start(bf16[4,128,128]{2,1,0:T(8,128)(2,1)S(1)} %get-tuple-element.41), channel_id=1, source_target_pairs={{0,16},{4,20},{8,24},{12,28},{16,0},{20,4},{24,8},{28,12},{1,17},{... | collective-permute-start | bytes 393224 | tf_op jit(solution)/shard_map/ppermute | solution.py:443
  71.7 5.0 %collective-permute-start.11 = (bf16[4,128,128]{2,1,0:T(8,128)(2,1)S(1)}, bf16[4,128,128]{2,1,0:T(8,128)(2,1)S(1)}, u32[]{:S(2)}, u32[]{:S(2)}) collective-permute-start(bf16[4,128,128]{2,1,0:T(8,128)(2,1)S(1)} %get-tuple-element.42), channel_id=1, source_target_pairs={{0,8},{4,12},{8,0},{12,4},{16,24},{20,28},{24,16},{28,20},{1,9},{5... | collective-permute-start | bytes 393224 | tf_op jit(solution)/shard_map/ppermute | solution.py:443
  76.8 2.0 %collective-permute-start.12 = (f32[8,128,128]{2,1,0:T(8,128)S(1)}, f32[8,128,128]{2,1,0:T(8,128)S(1)}, u32[]{:S(2)}, u32[]{:S(2)}) collective-permute-start(f32[8,128,128]{2,1,0:T(8,128)S(1)} %get-tuple-element.43), channel_id=1, source_target_pairs={{0,4},{4,0},{8,12},{12,8},{16,20},{20,16},{24,28},{28,24},{1,5},{5... | collective-permute-start | bytes 1572872 | tf_op jit(solution)/shard_map/ppermute | solution.py:452
  79.8 5.5 %collective-permute-start.13 = (f32[8,256]{1,0:T(8,128)S(1)}, f32[8,256]{1,0:T(8,128)S(1)}, u32[]{:S(2)}, u32[]{:S(2)}) collective-permute-start(f32[8,256]{1,0:T(8,128)S(1)} %get-tuple-element.46.refs_0_), channel_id=1, source_target_pairs={{0,1},{1,2},{2,3},{3,0},{4,5},{5,6},{6,7},{7,4},{8,9},{9,10},{10,1... | collective-permute-start | bytes 24584 | tf_op jit(solution)/shard_map/ppermute | solution.py:367
  80.2 5.1 %collective-permute-start.14 = (f32[8,256]{1,0:T(8,128)S(1)}, f32[8,256]{1,0:T(8,128)S(1)}, u32[]{:S(2)}, u32[]{:S(2)}) collective-permute-start(f32[8,256]{1,0:T(8,128)S(1)} %get-tuple-element.46.refs_0_), channel_id=1, source_target_pairs={{0,2},{1,3},{2,0},{3,1},{4,6},{5,7},{6,4},{7,5},{8,10},{9,11},{10,... | collective-permute-start | bytes 24584 | tf_op jit(solution)/shard_map/ppermute | solution.py:367
  82.9 3.7 %collective-permute-start.15 = (f32[8,256]{1,0:T(8,128)S(1)}, f32[8,256]{1,0:T(8,128)S(1)}, u32[]{:S(2)}, u32[]{:S(2)}) collective-permute-start(f32[8,256]{1,0:T(8,128)S(1)} %get-tuple-element.46.refs_0_), channel_id=1, source_target_pairs={{0,3},{1,0},{2,1},{3,2},{4,7},{5,4},{6,5},{7,6},{8,11},{9,8},{10,9... | collective-permute-start | bytes 24584 | tf_op jit(solution)/shard_map/ppermute | solution.py:367

commit v4 on v3

v4 whole, which is shorter than its diff:
```python
import functools

import jax
import jax.numpy as jnp
from jax import lax
from jax.experimental import pallas as pl
from jax.experimental.pallas import tpu as pltpu
from jax.sharding import PartitionSpec as P

EPSILON = 1e-06
PARTS = 3
COLUMNS = 1024
SLOT_BYTES = 10 * 1024 * 1024
VMEM_EXTRA = 4 * 1024 * 1024

F32 = jnp.float32
BF16 = jnp.bfloat16


def params(scratch):
    return pltpu.CompilerParams(vmem_limit_bytes=scratch + VMEM_EXTRA)


HBM = pl.BlockSpec(memory_space=pltpu.HBM)
WHOLE = pl.BlockSpec(memory_space=pltpu.VMEM)
ANY = pl.BlockSpec(memory_space=pl.ANY)


def start_features(pick, choices, raw, sem):
    for c, pieces in enumerate(choices):

        @pl.when(pick == c)
        def _(pieces=pieces):
            at = 0
            for piece in pieces:
                there = raw.at[pl.ds(at, piece.shape[0])]
                pltpu.make_async_copy(piece, there, sem).start()
                at += piece.shape[0]


def wait_features(raw, sem):
    pltpu.make_async_copy(raw, raw, sem).wait()


def of_place(values):
    place = lax.axis_index("tensor")
    found = jnp.int32(values[0])
    for i, value in enumerate(values[1:], 1):
        if value != values[0]:
            found = jnp.where(place == i, jnp.int32(value), found)
    return found


def column_blocks(columns):
    width = COLUMNS if columns % COLUMNS == 0 else columns
    return [pl.ds(at, width) for at in range(0, columns, width)]


def project_kernel(counts, first, picks, weight_rows, next_rows, slab_rows, *refs):
    refs = list(refs)
    choices = [[refs.pop(0) for _ in range(count)] for count in counts]
    weight = refs.pop(0)
    ready = None
    if not first:
        ready, _, _ = refs.pop(0), refs.pop(0), refs.pop(0)
    total, done = refs.pop(0), refs.pop(0)
    next_block = refs.pop(0) if next_rows else None
    slab = refs.pop(0) if slab_rows else None
    raw, turned, held, sem, weight_sems = refs
    done[...] = jnp.zeros_like(done)
    rows = raw.shape[0]
    slots = held.shape[0]
    blocks = column_blocks(weight.shape[1])

    start_features(of_place(picks), choices, raw, sem)
    at = pl.ds(pl.multiple_of(of_place(weight_rows), 16), rows)
    streamed = blocks if first else blocks[1:]
    copies = [
        pltpu.make_async_copy(weight.at[at, block], held.at[b % slots], weight_sems.at[b])
        for b, block in enumerate(streamed)
    ]
    if next_rows:
        at = pl.ds(pl.multiple_of(of_place(next_rows), 16), next_block.shape[0])
        copies.append(
            pltpu.make_async_copy(
                weight.at[at, blocks[0]], next_block, weight_sems.at[len(streamed)]
            )
        )
    if slab_rows:
        at = pl.ds(pl.multiple_of(of_place(slab_rows), 16), slab.shape[0])
        copies.append(
            pltpu.make_async_copy(weight.at[at, :], slab, weight_sems.at[len(copies)])
        )
    for copy in copies[:slots]:
        copy.start()
    wait_features(raw, sem)
    turned[...] = raw[...].T
    for b, block in enumerate(blocks):
        b = b if first else b - 1
        if b < 0:
            matrix = ready[...]
        else:
            copies[b].wait()
            matrix = held[b % slots]
        product = jnp.dot(turned[...], matrix, preferred_element_type=F32)
        if first:
            total[:, block] = product
        else:
            total[:, block] += product
        if 0 <= b < len(copies) - slots:
            copies[b + slots].start()
    for copy in copies[len(streamed) :]:
        copy.wait()


def project(
    choices,
    picks,
    weight,
    weight_rows,
    ready,
    total,
    after,
    next_rows=None,
    next_count=0,
    slab_rows=None,
    slab_count=0,
):
    counts = [len(pieces) for pieces in choices]
    rows = sum(piece.shape[0] for piece in choices[0])
    tokens, columns = choices[0][0].shape[1], weight.shape[1]
    first = total is None
    flat = [piece for pieces in choices for piece in pieces]
    operands = flat + [weight] + ([] if first else [ready, after, total])
    blocks = column_blocks(columns)
    block = blocks[0].size
    slots = max(1, min(SLOT_BYTES // (2 * rows * block), len(blocks)))
    out_shape = [pltpu.VMEM((tokens, columns), F32), pltpu.VMEM((8, 128), F32)]
    if next_rows:
        out_shape.append(pltpu.VMEM((next_count, block), BF16))
    if slab_rows:
        out_shape.append(pltpu.VMEM((slab_count, columns), BF16))
    return pl.pallas_call(
        functools.partial(
            project_kernel, counts, first, picks, weight_rows, next_rows, slab_rows
        ),
        out_shape=out_shape,
        in_specs=[ANY] * len(flat) + [HBM] + ([] if first else [WHOLE, ANY, WHOLE]),
        out_specs=[WHOLE] * len(out_shape),
        scratch_shapes=[
            pltpu.VMEM((rows, tokens), BF16),
            pltpu.VMEM((tokens, rows), BF16),
            pltpu.VMEM((slots, rows, block), BF16),
            pltpu.SemaphoreType.DMA,
            pltpu.SemaphoreType.DMA((len(blocks) + 2,)),
        ],
        input_output_aliases={} if first else {len(operands) - 1: 0},
        compiler_params=params(2 * rows * (2 * tokens + slots * block)),
        cost_estimate=pl.CostEstimate(
            flops=2 * tokens * rows * columns,
            bytes_accessed=rows * columns * 2 + rows * tokens * 2,
            transcendentals=0,
        ),
        name="project",
    )(*operands)


def gate_kernel(*refs):
    pass


def gate(x, after):
    return pl.pallas_call(
        gate_kernel,
        out_shape=jax.ShapeDtypeStruct(x.shape, x.dtype),
        in_specs=[ANY, ANY],
        out_specs=ANY,
        input_output_aliases={0: 0},
        compiler_params=params(0),
        name="gate",
    )(x, after)


def cut_kernel(x, *refs):
    *_, upper, lower, sems = refs
    rows = upper.shape[0]
    copies = [
        pltpu.make_async_copy(x.at[pl.ds(0, rows)], upper, sems.at[0]),
        pltpu.make_async_copy(x.at[pl.ds(rows, lower.shape[0])], lower, sems.at[1]),
    ]
    for copy in copies:
        copy.start()
    for copy in copies:
        copy.wait()


def cut_in_two(x, rows, after=()):
    sizes = (rows, x.shape[0] - rows)
    return list(
        pl.pallas_call(
            cut_kernel,
            out_shape=[pltpu.VMEM((size, x.shape[1]), x.dtype) for size in sizes],
            in_specs=[ANY if after else HBM] + [ANY] * len(after),
            out_specs=[WHOLE] * 2,
            scratch_shapes=[pltpu.SemaphoreType.DMA((2,))],
            compiler_params=params(0),
            name="cut",
        )(x, *after)
    )


def heads_at_once(half):
    return next(g for g in (4, 2, 1) if half % g == 0)


def activate_heads(side, width, turned, slab, total, act_ref, state_ref):
    half = state_ref.shape[0]
    group = PARTS * width
    at_once = heads_at_once(half)
    for h in range(0, half, at_once):
        here = slice(h * group, (h + at_once) * group)
        column = pl.multiple_of((side * half + h) * group, group)
        block = pl.ds(column, at_once * group)
        projected = total[:, block] + jnp.dot(
            turned[...],
            slab[slab.shape[0] - turned.shape[1] :, block],
            preferred_element_type=F32,
        )
        act = (projected / (1.0 + jnp.exp(-projected))).astype(BF16)
        act_ref[:, here] = act
        for g in range(at_once):
            at = g * group
            state_ref[h + g] = lax.dot_general(
                act[:, at + width : at + 2 * width],
                act[:, at + 2 * width : at + group],
                (((0,), (0,)), ((), ())),
                preferred_element_type=F32,
            )


def first_kernel(n_choices, width, picks, *refs):
    choices = refs[:n_choices]
    slab, total, turned, act_ref, state_ref = refs[n_choices:]
    pick = of_place(picks)
    for c, choice in enumerate(choices):

        @pl.when(pick == c)
        def _(choice=choice):
            turned[...] = choice[...].T

    side = 1 - lax.axis_index("context") % 2
    activate_heads(side, width, turned, slab, total, act_ref, state_ref)


def second_kernel(width, turned, slab, total, act_ref, state_ref):
    side = lax.axis_index("context") % 2
    activate_heads(side, width, turned, slab, total, act_ref, state_ref)


def activate(choices, picks, slab, total, heads, width):
    rows, tokens = choices[0].shape
    half = heads // 2
    columns = half * PARTS * width
    outs = (
        pltpu.VMEM((tokens, columns), BF16),
        pltpu.VMEM((half, width, width), F32),
    )
    cost = pl.CostEstimate(
        flops=2 * tokens * rows * columns + 2 * half * tokens * width * width,
        bytes_accessed=rows * tokens * 2,
        transcendentals=tokens * columns,
    )
    turned, act_other, state_other = pl.pallas_call(
        functools.partial(first_kernel, len(choices), width, picks),
        out_shape=(pltpu.VMEM((tokens, rows), BF16),) + outs,
        in_specs=[WHOLE] * (len(choices) + 2),
        out_specs=(WHOLE,) * 3,
        compiler_params=params(0),
        cost_estimate=cost,
        name="activate",
    )(*choices, slab, total)
    act_own, state_own = pl.pallas_call(
        functools.partial(second_kernel, width),
        out_shape=outs,
        in_specs=[WHOLE] * 3,
        out_specs=(WHOLE,) * 2,
        compiler_params=params(0),
        cost_estimate=cost,
        name="activate",
    )(turned, slab, total)
    return act_other, state_other, act_own, state_own


def within_kernel(width, *refs):
    tokens, columns = refs[0].shape
    causal = lax.broadcasted_iota(jnp.int32, (tokens, tokens), 0) >= lax.broadcasted_iota(
        jnp.int32, (tokens, tokens), 1
    )
    refs[4][...] = jnp.zeros_like(refs[4])
    for act_ref, within_ref in ((refs[0], refs[2]), (refs[1], refs[3])):
        for h in range(columns // (PARTS * width)):
            at = h * PARTS * width
            queries = act_ref[:, at : at + width]
            keys = act_ref[:, at + width : at + 2 * width]
            values = act_ref[:, at + 2 * width : at + 3 * width]
            scores = lax.dot_general(
                queries, keys, (((1,), (1,)), ((), ())), preferred_element_type=F32
            )
            scores = jnp.where(causal, scores, 0.0).astype(BF16)
            within_ref[:, h * width : (h + 1) * width] = jnp.dot(
                scores, values, preferred_element_type=F32
            )


def attend_within(act_other, act_own, width):
    tokens, columns = act_own.shape
    heads = columns // (PARTS * width)
    return pl.pallas_call(
        functools.partial(within_kernel, width),
        out_shape=(pltpu.VMEM((tokens, heads * width), F32),) * 2 + (pltpu.VMEM((8, 128), F32),),
        in_specs=[WHOLE] * 2,
        out_specs=(WHOLE,) * 3,
        compiler_params=params(0),
        cost_estimate=pl.CostEstimate(
            flops=8 * heads * tokens * tokens * width,
            bytes_accessed=tokens * columns * 4,
            transcendentals=0,
        ),
        name="within",
    )(act_other, act_own)


def across_kernel(own_side, n_groups, act, within, prior, *refs):
    groups = refs[:n_groups]
    *squares_in, att_ref, square_ref = refs[n_groups:]
    places = [(ref, h) for ref in groups for h in range(ref.shape[0])]
    half, width = len(places), prior.shape[1]
    core = lax.axis_index("context") % 2
    side = core if own_side else 1 - core
    squares = None
    for h, (earlier, place) in enumerate(places):
        carried = prior[side * half + h] + earlier[place]
        upper = carried.astype(BF16)
        lower = (carried - upper.astype(F32)).astype(BF16)
        at = h * PARTS * width
        queries = act[:, at : at + width]
        here = slice(h * width, (h + 1) * width)
        attended = within[:, here] + jnp.dot(
            jnp.concatenate([queries, queries], axis=1),
            jnp.concatenate([upper, lower], axis=0),
            preferred_element_type=F32,
        )
        att_ref[:, here] = attended
        square = attended * attended
        squares = square if squares is None else squares + square
    total = lax.dot_general(
        jnp.ones((8, width), F32),
        squares,
        (((1,), (1,)), ((), ())),
        preferred_element_type=F32,
        precision=lax.Precision.HIGHEST,
    )
    for ref in squares_in:
        total += ref[...]
    square_ref[...] = total


def attend_across(own_side, act, within, prior, earlier, squares):
    tokens = act.shape[0]
    half, width = prior.shape[0] // 2, prior.shape[1]
    operands = [act, within, prior] + earlier + squares
    return pl.pallas_call(
        functools.partial(across_kernel, own_side, len(earlier)),
        out_shape=(
            pltpu.VMEM((tokens, half * width), F32),
            pltpu.VMEM((8, tokens), F32),
        ),
        in_specs=[WHOLE] * len(operands),
        out_specs=(WHOLE, WHOLE),
        compiler_params=params(0),
        cost_estimate=pl.CostEstimate(
            flops=4 * half * tokens * width * width, bytes_accessed=0, transcendentals=0
        ),
        name="across",
    )(*operands)


def norm_kernel(features, att_other, att_own, gain_ref, *refs):
    *square_refs, out_ref, held, sems = refs
    core = lax.axis_index("context") % 2
    squares = sum(ref[...] for ref in square_refs[1:]) + square_refs[0][...]
    ones = jnp.ones((squares.shape[0], 128), F32)
    mean_sq = lax.dot_general(
        squares * (1.0 / squares.shape[0] / features),
        ones,
        (((0,), (0,)), ((), ())),
        preferred_element_type=F32,
        precision=lax.Precision.HIGHEST,
    )
    inverse = lax.rsqrt(mean_sq + EPSILON)
    columns = held.shape[2]
    parts = att_own.shape[1] // columns
    copies = []
    for side, att in ((1 - core, att_other), (core, att_own)):
        for part in range(parts):
            slot = len(copies)
            first = pl.multiple_of((side * parts + part) * columns, columns)
            for at in range(0, columns, 128):
                gain = gain_ref[:, pl.ds(pl.multiple_of(first + at, 128), 128)]
                here = slice(part * columns + at, part * columns + at + 128)
                held[slot, :, at : at + 128] = (att[:, here] * inverse * gain).astype(BF16)
            copies.append(
                pltpu.make_async_copy(
                    held.at[slot], out_ref.at[:, pl.ds(first, columns)], sems.at[slot]
                )
            )
            copies[-1].start()
    for copy in copies:
        copy.wait()


def normalize(att_other, att_own, squares, gain, features):
    tokens, half = att_own.shape
    columns = half // 2 if half % 256 == 0 else half
    count = 2 * half // columns
    return pl.pallas_call(
        functools.partial(norm_kernel, features),
        out_shape=jax.ShapeDtypeStruct((tokens, 2 * half), BF16),
        in_specs=[WHOLE] * (3 + len(squares)),
        out_specs=HBM,
        scratch_shapes=[
            pltpu.VMEM((count, tokens, columns), BF16),
            pltpu.SemaphoreType.DMA((count,)),
        ],
        compiler_params=params(4 * tokens * half),
        cost_estimate=pl.CostEstimate(
            flops=4 * tokens * half, bytes_accessed=4 * tokens * half, transcendentals=0
        ),
        name="normalize",
    )(att_other, att_own, gain[None, :], *squares)


def terms_over_tensor(x, n):
    if n <= 4:
        return [x] + [
            lax.ppermute(x, "tensor", [(i, (i + d) % n) for i in range(n)]) for d in range(1, n)
        ]
    if n & (n - 1):
        return [lax.psum(x, "tensor")]
    bit = 1
    while bit * 2 < n:
        x = x + lax.ppermute(x, "tensor", [(i, i ^ bit) for i in range(n)])
        bit *= 2
    return [x, lax.ppermute(x, "tensor", [(i, i ^ bit) for i in range(n)])]


def meet_kernel(bits, n_got, first, final, *refs):
    own, theirs, gots = refs[0], refs[1], refs[2 : 2 + n_got]
    index = lax.axis_index("context")
    core, chip = index % 2, index // 2
    rising = core == 0

    def has(bit):
        return chip // bit % 2 == 1

    for h in range(refs[-1].shape[0]):
        own_part, their_part = own[first + h], theirs[first + h]
        total = own_part + their_part
        reached = total
        before = jnp.zeros_like(total)
        for bit, ref in zip(bits, gots):
            got = ref[h].astype(F32)
            earlier = jnp.logical_or(core == 1, has(bit))
            before = before + jnp.where(earlier, got, 0.0)
            reached = reached + got
        if final:
            for_mate, mine = refs[-2:]
            for_mate[h] = before + jnp.where(rising, own_part, 0.0)
            mine[h] = before + jnp.where(rising, 0.0, their_part)
        else:
            falling = before + jnp.where(has(bits[-1 - n_got]), 0.0, total)
            refs[-1][h] = jnp.where(rising, reached, falling).astype(BF16)


def meet(bits, own, theirs, gots, after, first, count, final):
    _, width, _ = own.shape
    if final:
        out_shape = [pltpu.VMEM((count, width, width), F32)] * 2
    else:
        out_shape = [pltpu.VMEM((count, width, width), BF16)]
    operands = [own, theirs] + gots + after
    return pl.pallas_call(
        functools.partial(meet_kernel, bits, len(gots), first, final),
        out_shape=out_shape,
        in_specs=[WHOLE] * len(operands),
        out_specs=[WHOLE] * len(out_shape),
        compiler_params=params(0),
        cost_estimate=pl.CostEstimate(
            flops=4 * count * width * width, bytes_accessed=0, transcendentals=0
        ),
        name="meet",
    )(*operands)


def earlier_states(other_states, own, after, n):
    chips, half = n // 2, own.shape[0]
    swap = [(i, i ^ 1) for i in range(n)]
    theirs = lax.ppermute(other_states, "context", swap)
    bits = [1 << b for b in range((chips - 1).bit_length())]
    groups = [(0, half // 2), (half // 2, half - half // 2)]
    groups = [group for group in groups if group[1]]
    gots = [[] for _ in groups]
    for step, (rise, fall) in enumerate(zip(bits, bits[::-1])):
        pairs = [
            (2 * i + c, 2 * (i ^ bit) + c)
            for i in range(chips)
            for c, bit in enumerate((rise, fall))
        ]
        for g, group in enumerate(groups):
            waits = after if step == 1 and g == 0 else []
            (message,) = meet(bits, own, theirs, gots[g], waits, *group, False)
            gots[g] = gots[g] + [lax.ppermute(message, "context", pairs)]
    others, mine = [], []
    for g, group in enumerate(groups):
        for_mate, kept = meet(bits, own, theirs, gots[g], [], *group, True)
        others.append(lax.ppermute(for_mate, "context", swap))
        mine.append(kept)
    return others, mine


def hops(n):
    pairs = [[[] for _ in range(n - 1)] for _ in range(2)]
    arrivals = [[] for _ in range(n)]
    for t in range(n - 1):
        for chain in range(2):
            for share in range(n):
                way = 1 if share % 2 == chain else -1
                here = share + way * t
                if 0 <= here < n and 0 <= here + way < n:
                    pairs[chain][t].append((here, here + way))
                    if t == 1 and chain == 1:
                        pairs[chain][t].append((here + way, here))
                    arrivals[here + way].append((t, chain, share))
    pairs = [[sorted(set(p)) for p in chain] for chain in pairs]
    return pairs, arrivals


def body(n_tensor, n_context, tokens_t, qkv_weight, prior_state, norm_gain):
    share = tokens_t.shape[0]
    heads, width, _ = prior_state.shape
    early = share // 2

    pairs, arrivals = hops(n_tensor)
    last = n_tensor - 2
    pieces = cut_in_two(tokens_t, early)
    held = [[tokens_t], pieces]
    came = {}

    steps = [(-1, None), (0, None)] + [(1, 0), (1, 1)] + [(m, None) for m in range(2, last)]
    steps = [step for step in steps if step[0] < last] + [(last, 0)]

    def rows_of(m, piece):
        starts = [there[m][2] if m >= 0 else i for i, there in enumerate(arrivals)]
        return [start * share + (early if piece == 1 else 0) for start in starts]

    def count_of(piece):
        return {None: share, 0: early, 1: share - early}[piece]

    def run(number, ready, total, after):
        m, piece = steps[number]
        following = []
        if number + 1 < len(steps):
            following = [rows_of(*steps[number + 1]), count_of(steps[number + 1][1])]
            if number == 0:
                following += [rows_of(last, 1), share - early]
        choices, picks = [pieces], [0] * n_tensor
        if m >= 0:
            keys = sorted({there[m][:2] for there in arrivals})
            picks = [keys.index(there[m][:2]) for there in arrivals]
            choices = [came[key] if piece is None else [came[key][piece]] for key in keys]
        return project(
            choices, picks, qkv_weight, rows_of(m, piece), ready, total, after, *following
        )

    total, done, ready, slab = run(0, None, None, None)
    number = 1
    for t in range(n_tensor - 1):
        for chain in range(2):
            if pairs[chain][t]:
                held[chain] = [lax.ppermute(x, "tensor", pairs[chain][t]) for x in held[chain]]
                came[t, chain] = held[chain]
        if t == 0:
            if (0, 1) in came:
                held[1][0] = done = gate(held[1][0], done)
            held[0] = came[0, 0] = cut_in_two(held[0][0], early, [done])
            if (0, 1) in came:
                held[1][1] = gate(held[1][1], held[0][0])
        gates = [0, 1] if t == 1 and t < last else []
        while number < len(steps) - 1 and 1 <= t >= steps[number][0]:
            total, done, ready = run(number, ready, total, done)
            number += 1
            if gates:
                j = gates.pop(0)
                held[0][j] = done = gate(held[0][j], done)

    total, _ = run(number, ready, total, done)
    keys = sorted({there[last][:2] for there in arrivals})
    picks = [keys.index(there[last][:2]) for there in arrivals]
    choices = [came[key] for key in keys]
    other_act, other_states, own_act, own_states = activate(
        [c[1] for c in choices], picks, slab, total, heads, width
    )
    other_within, own_within, done = attend_within(other_act, own_act, width)
    other, own = earlier_states(other_states, own_states, [done], n_context)
    own_att, squares = attend_across(True, own_act, own_within, prior_state, own, [])
    other_att, squares = attend_across(
        False, other_act, other_within, prior_state, other, [squares]
    )
    squares = terms_over_tensor(squares, n_tensor)
    return normalize(other_att, own_att, squares, norm_gain, n_tensor * heads * width)


def solution(mesh):
    n_tensor, n_context = mesh.shape["tensor"], mesh.shape["context"]
    in_specs = (P("tensor", "context"), P(None, "tensor"), P("tensor", None, None), P("tensor"))
    return jax.shard_map(
        functools.partial(body, n_tensor, n_context),
        mesh=mesh,
        in_specs=in_specs,
        out_specs=P("context", "tensor"),
        check_vma=False,
    )
```

time: 88.3 us -> 85.4 us (0.967)
  waiting for transfers between devices: 22.2 us -> 14.8 us
  starting transfers between devices: 23.5 us -> 26.1 us
  Pallas kernels: 41 us -> 42.6 us
    ppermute x7 -> x9, waiting for transfers between devices: 10.4 us -> 4.49 us  [body(): lax.ppermute(x, 'tensor', pairs[chain][t])]
    ppermute x5 -> x6, waiting for transfers between devices: 8.93 us -> 5.45 us  [the longest x4 4.71 us: earlier_states(): gots[g] = gots[g] + [lax.ppermute(message, 'context', pairs)]]
    ppermute x7 -> x9, starting transfers between devices: 14.3 us -> 17.4 us  [body(): lax.ppermute(x, 'tensor', pairs[chain][t])]
    ppermute x3, waiting for transfers between devices: 2.86 us -> 4.88 us  [terms_over_tensor(): lax.ppermute(x, 'tensor', [(i, (i + d) % n) for i in range(n)])]
    pallas_call x4 -> x14, Pallas kernels: 1.3 us -> 2.73 us  [the longest x2 1.51 us: attend_across(): pl.pallas_call(functools.partial(across_kernel, own_side, len(earlier)),...]
    pallas_call x4 -> x5, Pallas kernels: 31.9 us -> 32.3 us  [project(): pl.pallas_call(functools.partial(project_kernel, counts, first, picks, we...]
    ppermute x5 -> x6, starting transfers between devices: 5.26 us -> 5.38 us  [the longest x4 5.24 us: earlier_states(): gots[g] = gots[g] + [lax.ppermute(message, 'context', pairs)]]
  transfers between devices with their start and end apart: 16 -> 19, of which waited for: 10 -> 9; matrix products, arithmetic and copies ran while one was open for 0% -> 0% of each run, Pallas kernels for 40% -> 45%
where the time goes in v4:
time: 85.4 us; the launch traced here: 85.2 us
  Pallas kernels  42.6 us (50%)
  starting transfers between devices  26.1 us (31%)
  waiting for transfers between devices  14.8 us (17%)
  local copies, waits for them, and re-layouts  1.18 us (1%)
    pallas_call x5, Pallas kernels, project(): pl.pallas_call(functools.partial(project_kernel, counts, first, picks, we...  32.3 us
    ppermute x9, starting transfers between devices, body(): lax.ppermute(x, 'tensor', pairs[chain][t])  17.4 us
    ppermute x4, starting transfers between devices, earlier_states(): gots[g] = gots[g] + [lax.ppermute(message, 'context', pairs)]  5.24 us
    ppermute x3, waiting for transfers between devices, terms_over_tensor(): lax.ppermute(x, 'tensor', [(i, (i + d) % n) for i in range(n)])  4.88 us
    ppermute x4, waiting for transfers between devices, earlier_states(): gots[g] = gots[g] + [lax.ppermute(message, 'context', pairs)]  4.71 us
    ppermute x9, waiting for transfers between devices, body(): lax.ppermute(x, 'tensor', pairs[chain][t])  4.49 us
    ppermute x3, starting transfers between devices, terms_over_tensor(): lax.ppermute(x, 'tensor', [(i, (i + d) % n) for i in range(n)])  3.24 us
    pallas_call x1, Pallas kernels, activate(): pl.pallas_call(functools.partial(first_kernel, len(choices), width, picks...  2.36 us
  transfers between devices with their start and end apart: 19, of which 9 were waited for; matrix products, arithmetic and copies ran while one was open for 0% of the time, Pallas kernels for 45%

profile of v4, /device:TPU:0, one launch (start us, length us, event | category | flops | bytes accessed | tf_op | source)
XLA Modules:
  0.0 85.2 jit_solution(17479873026356558466)
XLA Ops:
  0.0 3.0 %collective-permute-start = (bf16[1536,256]{1,0:T(8,128)(2,1)}, bf16[1536,256]{1,0:T(8,128)(2,1)S(1)}, u32[]{:S(2)}, u32[]{:S(2)}) collective-permute-start(bf16[1536,256]{1,0:T(8,128)(2,1)} %x.1), channel_id=1, source_target_pairs={{0,1},{1,0},{2,3},{3,2},{4,5},{5,4},{6,7},{7,6},{8,9},{9,8},{10,11... | collective-permute-start | bytes 2359304 | tf_op jit(solution)/shard_map/ppermute | solution.py:590
  3.0 1.2 %copy-done.1 = bf16[1536,256]{1,0:T(8,128)(2,1)S(1)} copy-done((bf16[1536,256]{1,0:T(8,128)(2,1)S(1)}, bf16[1536,256]{1,0:T(8,128)(2,1)}, u32[]{:S(2)}) %copy-start.1) | copy-done | bytes 786456
  4.2 0.4 cut.2
  4.6 0.7 collective-permute-start.1
  5.3 0.7 collective-permute-start.7
  6.0 10.8 %project.5 = (f32[256,6144]{1,0:T(8,128)S(1)}, f32[8,128]{1,0:T(8,128)S(1)}, bf16[1536,1024]{1,0:T(8,128)(2,1)S(1)}, bf16[768,6144]{1,0:T(8,128)(2,1)S(1)}) custom-call(bf16[768,256]{1,0:T(8,128)(2,1)S(1)} %get-tuple-element.39.refs_0_, bf16[768,256]{1,0:T(8,128)(2,1)S(1)} %get-tuple-element.40.refs_1_, bf16[6144,6144]{1,0:T(8,128)(2,1)} %refs_2_.9), custom_call_target="tpu_custom_call" | custom-call | flops 4831838208 | bytes 19660800 | tf_op jit(solution)/shard_map/project/pallas_call | solution.py:143
  16.8 5.7 %collective-permute-start.3 = (bf16[768,256]{1,0:T(8,128)(2,1)S(1)}, bf16[768,256]{1,0:T(8,128)(2,1)S(1)}, u32[]{:S(2)}, u32[]{:S(2)}) collective-permute-start(bf16[768,256]{1,0:T(8,128)(2,1)S(1)} %gate.4.refs_0_.refs_4_), channel_id=1, source_target_pairs={{0,1},{1,0},{2,3},{3,2},{4,5},{5,4},{6,7},{7,6},{8,9},{9,8},{10,11... | collective-permute-start | bytes 1179656 | tf_op jit(solution)/shard_map/ppermute | solution.py:590
  22.5 0.4 cut.3
  22.9 0.7 collective-permute-start.4
  23.6 3.4 %collective-permute-start.8 = (bf16[768,256]{1,0:T(8,128)(2,1)S(1)}, bf16[768,256]{1,0:T(8,128)(2,1)S(1)}, u32[]{:S(2)}, u32[]{:S(2)}) collective-permute-start(bf16[768,256]{1,0:T(8,128)(2,1)S(1)} %gate.7.refs_0_), channel_id=1, source_target_pairs={{0,1},{1,0},{2,3},{3,2},{4,5},{5,4},{6,7},{7,6},{8,9},{9,8},{10,11... | collective-permute-start | bytes 1179656 | tf_op jit(solution)/shard_map/ppermute | solution.py:590
  27.0 0.7 collective-permute-start.2
  27.7 7.4 %project.6 = (f32[256,6144]{1,0:T(8,128)S(1)}, f32[8,128]{1,0:T(8,128)S(1)}, bf16[768,1024]{1,0:T(8,128)(2,1)S(1)}) custom-call(bf16[768,256]{1,0:T(8,128)(2,1)S(1)} %get-tuple-element.43.refs_0_.refs_1_, bf16[768,256]{1,0:T(8,128)(2,1)S(1)} %get-tuple-element.42.refs_1_, bf16[6144,6144]{1,0:T(8,128)(2,1)} %refs_2_.9, ...), custom_call_target="tpu_custom_call", output_to_operand_aliasing={{0}: (5, {})} | custom-call | flops 4831838208 | bytes 19660800 | tf_op jit(solution)/shard_map/project/pallas_call | solution.py:143
  35.1 1.3 %collective-permute-start.6 = (bf16[768,256]{1,0:T(8,128)(2,1)S(1)}, bf16[768,256]{1,0:T(8,128)(2,1)S(1)}, u32[]{:S(2)}, u32[]{:S(2)}) collective-permute-start(bf16[768,256]{1,0:T(8,128)(2,1)S(1)} %gate.5.refs_4_.refs_0_), channel_id=1, source_target_pairs={{1,0},{2,3},{5,4},{6,7},{9,8},{10,11},{13,12},{14,15},{17,16},{18,... | collective-permute-start | bytes 1179656 | tf_op jit(solution)/shard_map/ppermute | solution.py:590
  36.4 4.6 %project.7 = (f32[256,6144]{1,0:T(8,128)S(1)}, f32[8,128]{1,0:T(8,128)S(1)}, bf16[768,1024]{1,0:T(8,128)(2,1)S(1)}) custom-call(bf16[768,256]{1,0:T(8,128)(2,1)S(1)} %gate.4.refs_0_.refs_4_, bf16[768,256]{1,0:T(8,128)(2,1)S(1)} %collective-permute-done.3.refs_1_, bf16[6144,6144]{1,0:T(8,128)(2,1)} %refs_2_.9, ...), custom_call_target="tpu_custom_call", output_to_operand_aliasing={{0}: (5, {})} | custom-call | flops 2415919104 | bytes 9830400 | tf_op jit(solution)/shard_map/project/pallas_call | solution.py:143
  41.1 1.3 %collective-permute-start.5 = (bf16[768,256]{1,0:T(8,128)(2,1)S(1)}, bf16[768,256]{1,0:T(8,128)(2,1)S(1)}, u32[]{:S(2)}, u32[]{:S(2)}) collective-permute-start(bf16[768,256]{1,0:T(8,128)(2,1)S(1)} %gate.6.refs_4_.refs_0_), channel_id=1, source_target_pairs={{1,0},{2,3},{5,4},{6,7},{9,8},{10,11},{13,12},{14,15},{17,16},{18,... | collective-permute-start | bytes 1179656 | tf_op jit(solution)/shard_map/ppermute | solution.py:590
  42.4 4.8 %project.8 = (f32[256,6144]{1,0:T(8,128)S(1)}, f32[8,128]{1,0:T(8,128)S(1)}, bf16[768,1024]{1,0:T(8,128)(2,1)S(1)}) custom-call(bf16[768,256]{1,0:T(8,128)(2,1)S(1)} %gate.7.refs_0_, bf16[768,256]{1,0:T(8,128)(2,1)S(1)} %collective-permute-done.8.refs_1_, bf16[6144,6144]{1,0:T(8,128)(2,1)} %refs_2_.9, ...), custom_call_target="tpu_custom_call", output_to_operand_aliasing={{0}: (5, {})} | custom-call | flops 2415919104 | bytes 9830400 | tf_op jit(solution)/shard_map/project/pallas_call | solution.py:143
  47.2 2.1 %collective-permute-done.6.refs_1_ = bf16[768,256]{1,0:T(8,128)(2,1)S(1)} collective-permute-done((bf16[768,256]{1,0:T(8,128)(2,1)S(1)}, bf16[768,256]{1,0:T(8,128)(2,1)S(1)}, u32[]{:S(2)}, u32[]{:S(2)}) %collective-permute-start.6) | collective-permute-done | bytes 393248 | tf_op jit(solution)/shard_map/ppermute | solution.py:590
  49.4 4.6 %project.9 = (f32[256,6144]{1,0:T(8,128)S(1)}, f32[8,128]{1,0:T(8,128)}) custom-call(bf16[768,256]{1,0:T(8,128)(2,1)S(1)} %gate.5.refs_4_.refs_0_, bf16[768,256]{1,0:T(8,128)(2,1)S(1)} %collective-permute-done.6.refs_1_, bf16[6144,6144]{1,0:T(8,128)(2,1)} %refs_2_.9, ...), custom_call_target="tpu_custom_call", output_to_operand_aliasing={{0}: (5, {})} | custom-call | flops 2415919104 | bytes 9830400 | tf_op jit(solution)/shard_map/project/pallas_call | solution.py:143
  54.0 2.3 %collective-permute-done.5.refs_1_ = bf16[768,256]{1,0:T(8,128)(2,1)S(1)} collective-permute-done((bf16[768,256]{1,0:T(8,128)(2,1)S(1)}, bf16[768,256]{1,0:T(8,128)(2,1)S(1)}, u32[]{:S(2)}, u32[]{:S(2)}) %collective-permute-start.5) | collective-permute-done | bytes 393248 | tf_op jit(solution)/shard_map/ppermute | solution.py:590
  56.3 2.4 %activate.2 = (bf16[256,768]{1,0:T(8,128)(2,1)S(1)}, bf16[256,3072]{1,0:T(8,128)(2,1)S(1)}, f32[8,128,128]{2,1,0:T(8,128)S(1)}) custom-call(bf16[768,256]{1,0:T(8,128)(2,1)S(1)} %gate.6.refs_4_.refs_0_, bf16[768,256]{1,0:T(8,128)(2,1)S(1)} %collective-permute-done.5.refs_1_, bf16[768,6144]{1,0:T(8,128)(2,1)S(1)} %get-tuple-element.50.refs_2_.slab, ...), custom_call_target="tpu_custom_call" | custom-call | flops 1275068416 | bytes 393216 | tf_op jit(solution)/shard_map/activate/pallas_call | solution.py:273
  58.7 0.1 collective-permute-start.9
  58.8 2.2 %activate.3 = (bf16[256,3072]{1,0:T(8,128)(2,1)S(1)}, f32[8,128,128]{2,1,0:T(8,128)S(1)}) custom-call(bf16[256,768]{1,0:T(8,128)(2,1)S(1)} %get-tuple-element.58.turned, bf16[768,6144]{1,0:T(8,128)(2,1)S(1)} %get-tuple-element.50.refs_2_.slab, f32[256,6144]{1,0:T(8,128)S(1)} %get-tuple-element.56.refs_3_.total), custom_call_target="tpu_custom_call" | custom-call | flops 1275068416 | bytes 393216 | tf_op jit(solution)/shard_map/activate/pallas_call | solution.py:282
  61.0 0.0 copy-start
  61.1 0.1 meet.9
  61.1 1.6 %collective-permute-start.13 = (bf16[4,128,128]{2,1,0:T(8,128)(2,1)S(1)}, bf16[4,128,128]{2,1,0:T(8,128)(2,1)S(1)}, u32[]{:S(2)}, u32[]{:S(2)}) collective-permute-start(bf16[4,128,128]{2,1,0:T(8,128)(2,1)S(1)} %meet.9), channel_id=1, source_target_pairs={{0,8},{4,20},{8,0},{12,28},{16,24},{20,4},{24,16},{28,12},{1,9},{5... | collective-permute-start | bytes 393224 | tf_op jit(solution)/shard_map/ppermute | solution.py:522
  62.7 0.6 collective-permute-start.10
  63.3 1.5 %within.1 = (f32[256,1024]{1,0:T(8,128)S(1)}, f32[256,1024]{1,0:T(8,128)S(1)}, f32[8,128]{1,0:T(8,128)S(1)}) custom-call(bf16[256,3072]{1,0:T(8,128)(2,1)S(1)} %get-tuple-element.57.refs_0_.act, bf16[256,3072]{1,0:T(8,128)(2,1)S(1)} %get-tuple-element.59.refs_1_.act), custom_call_target="tpu_custom_call" | custom-call | flops 536870912 | bytes 3145728 | tf_op jit(solution)/shard_map/within/pallas_call | solution.py:318
  64.8 1.3 %collective-permute-done.13.refs_2_ = bf16[4,128,128]{2,1,0:T(8,128)(2,1)S(1)} collective-permute-done((bf16[4,128,128]{2,1,0:T(8,128)(2,1)S(1)}, bf16[4,128,128]{2,1,0:T(8,128)(2,1)S(1)}, u32[]{:S(2)}, u32[]{:S(2)}) %collective-permute-start.13) | collective-permute-done | bytes 131104 | tf_op jit(solution)/shard_map/ppermute | solution.py:522
  66.2 0.1 meet.10
  66.2 0.0 copy-start.2
  66.3 1.6 %collective-permute-start.14 = (bf16[4,128,128]{2,1,0:T(8,128)(2,1)S(1)}, bf16[4,128,128]{2,1,0:T(8,128)(2,1)S(1)}, u32[]{:S(2)}, u32[]{:S(2)}) collective-permute-start(bf16[4,128,128]{2,1,0:T(8,128)(2,1)S(1)} %meet.10), channel_id=1, source_target_pairs={{0,16},{4,12},{8,24},{12,4},{16,0},{20,28},{24,8},{28,20},{1,17},{... | collective-permute-start | bytes 393224 | tf_op jit(solution)/shard_map/ppermute | solution.py:522
  67.8 0.1 meet.7
  67.9 1.5 %collective-permute-start.11 = (bf16[4,128,128]{2,1,0:T(8,128)(2,1)S(1)}, bf16[4,128,128]{2,1,0:T(8,128)(2,1)S(1)}, u32[]{:S(2)}, u32[]{:S(2)}) collective-permute-start(bf16[4,128,128]{2,1,0:T(8,128)(2,1)S(1)} %meet.7), channel_id=1, source_target_pairs={{0,16},{4,12},{8,24},{12,4},{16,0},{20,28},{24,8},{28,20},{1,17},{... | collective-permute-start | bytes 393224 | tf_op jit(solution)/shard_map/ppermute | solution.py:522
  69.4 1.9 %collective-permute-done.14.refs_3_ = bf16[4,128,128]{2,1,0:T(8,128)(2,1)S(1)} collective-permute-done((bf16[4,128,128]{2,1,0:T(8,128)(2,1)S(1)}, bf16[4,128,128]{2,1,0:T(8,128)(2,1)S(1)}, u32[]{:S(2)}, u32[]{:S(2)}) %collective-permute-start.14) | collective-permute-done | bytes 131104 | tf_op jit(solution)/shard_map/ppermute | solution.py:522
  71.3 0.1 meet.11
  71.4 0.1 collective-permute-start.15
  71.4 1.5 %collective-permute-done.11.refs_3_ = bf16[4,128,128]{2,1,0:T(8,128)(2,1)S(1)} collective-permute-done((bf16[4,128,128]{2,1,0:T(8,128)(2,1)S(1)}, bf16[4,128,128]{2,1,0:T(8,128)(2,1)S(1)}, u32[]{:S(2)}, u32[]{:S(2)}) %collective-permute-start.11) | collective-permute-done | bytes 131104 | tf_op jit(solution)/shard_map/ppermute | solution.py:522
  73.0 0.1 meet.8
  73.0 0.1 collective-permute-start.12
  73.1 0.8 across.2
  73.9 0.7 collective-permute-done.12.refs_0_
  74.6 0.7 across.3
  75.4 2.7 %collective-permute-start.18 = (f32[8,256]{1,0:T(8,128)S(1)}, f32[8,256]{1,0:T(8,128)S(1)}, u32[]{:S(2)}, u32[]{:S(2)}) collective-permute-start(f32[8,256]{1,0:T(8,128)S(1)} %get-tuple-element.72.refs_0_), channel_id=1, source_target_pairs={{0,3},{1,0},{2,1},{3,2},{4,7},{5,4},{6,5},{7,6},{8,11},{9,8},{10,9... | collective-permute-start | bytes 24584 | tf_op jit(solution)/shard_map/ppermute | solution.py:446
  78.1 0.6 collective-permute-start.16
  78.6 0.8 collective-permute-done.18.refs_3_
  79.4 3.2 %collective-permute-done.17.refs_2_ = f32[8,256]{1,0:T(8,128)S(1)} collective-permute-done((f32[8,256]{1,0:T(8,128)S(1)}, f32[8,256]{1,0:T(8,128)S(1)}, u32[]{:S(2)}, u32[]{:S(2)}) %collective-permute-start.17) | collective-permute-done | bytes 8224 | tf_op jit(solution)/shard_map/ppermute | solution.py:446
  82.6 0.9 %collective-permute-done.16.refs_1_ = f32[8,256]{1,0:T(8,128)S(1)} collective-permute-done((f32[8,256]{1,0:T(8,128)S(1)}, f32[8,256]{1,0:T(8,128)S(1)}, u32[]{:S(2)}, u32[]{:S(2)}) %collective-permute-start.16) | collective-permute-done | bytes 8224 | tf_op jit(solution)/shard_map/ppermute | solution.py:446
  83.5 1.5 %normalize.1 = bf16[256,2048]{1,0:T(8,128)(2,1)} custom-call(f32[256,1024]{1,0:T(8,128)S(1)} %get-tuple-element.70.att_other, f32[256,1024]{1,0:T(8,128)S(1)} %get-tuple-element.71.att_own, f32[1,2048]{1,0:T(1,128)S(1)} %bitcast.1, f32[8,256]{1,0:T(8,128)S(1)} %get-tuple-element.72.refs_0_, f32[8,256]{1,0:T(8,128)S(1)} %collective-permute-done.16.refs_1_, ...), custom_call_target="tpu_custom_call" | custom-call | flops 1048576 | bytes 1048576 | tf_op jit(solution)/shard_map/normalize/pallas_call | solution.py:426
  (19 shorter events, 0.1 us)
Async XLA Ops:
  0.0 22.5 %collective-permute-start = (bf16[1536,256]{1,0:T(8,128)(2,1)}, bf16[1536,256]{1,0:T(8,128)(2,1)S(1)}, u32[]{:S(2)}, u32[]{:S(2)}) collective-permute-start(bf16[1536,256]{1,0:T(8,128)(2,1)} %x.1), channel_id=1, source_target_pairs={{0,1},{1,0},{2,3},{3,2},{4,5},{5,4},{6,7},{7,6},{8,9},{9,8},{10,11... | collective-permute-start | bytes 2359304 | tf_op jit(solution)/shard_map/ppermute | solution.py:590
  3.0 1.2 %copy-start.1 = (bf16[1536,256]{1,0:T(8,128)(2,1)S(1)}, bf16[1536,256]{1,0:T(8,128)(2,1)}, u32[]{:S(2)}) copy-start(bf16[1536,256]{1,0:T(8,128)(2,1)} %x.1) | copy-start | bytes 2359300
  4.6 12.2 %collective-permute-start.1 = (bf16[768,256]{1,0:T(8,128)(2,1)S(1)}, bf16[768,256]{1,0:T(8,128)(2,1)S(1)}, u32[]{:S(2)}, u32[]{:S(2)}) collective-permute-start(bf16[768,256]{1,0:T(8,128)(2,1)S(1)} %get-tuple-element.39.refs_0_), channel_id=1, source_target_pairs={{1,2},{2,1},{5,6},{6,5},{9,10},{10,9},{13,14},{14,13},{17,18},{18,... | collective-permute-start | bytes 1179656 | tf_op jit(solution)/shard_map/ppermute | solution.py:590
  5.3 18.3 %collective-permute-start.7 = (bf16[768,256]{1,0:T(8,128)(2,1)S(1)}, bf16[768,256]{1,0:T(8,128)(2,1)S(1)}, u32[]{:S(2)}, u32[]{:S(2)}) collective-permute-start(bf16[768,256]{1,0:T(8,128)(2,1)S(1)} %get-tuple-element.40.refs_1_), channel_id=1, source_target_pairs={{1,2},{2,1},{5,6},{6,5},{9,10},{10,9},{13,14},{14,13},{17,18},{18,... | collective-permute-start | bytes 1179656 | tf_op jit(solution)/shard_map/ppermute | solution.py:590
  16.8 19.6 %collective-permute-start.3 = (bf16[768,256]{1,0:T(8,128)(2,1)S(1)}, bf16[768,256]{1,0:T(8,128)(2,1)S(1)}, u32[]{:S(2)}, u32[]{:S(2)}) collective-permute-start(bf16[768,256]{1,0:T(8,128)(2,1)S(1)} %gate.4.refs_0_.refs_4_), channel_id=1, source_target_pairs={{0,1},{1,0},{2,3},{3,2},{4,5},{5,4},{6,7},{7,6},{8,9},{9,8},{10,11... | collective-permute-start | bytes 1179656 | tf_op jit(solution)/shard_map/ppermute | solution.py:590
  22.9 12.2 %collective-permute-start.4 = (bf16[768,256]{1,0:T(8,128)(2,1)S(1)}, bf16[768,256]{1,0:T(8,128)(2,1)S(1)}, u32[]{:S(2)}, u32[]{:S(2)}) collective-permute-start(bf16[768,256]{1,0:T(8,128)(2,1)S(1)} %get-tuple-element.43.refs_0_.refs_1_), channel_id=1, source_target_pairs={{1,2},{2,1},{5,6},{6,5},{9,10},{10,9},{13,14},{14,13},{17,18},{18,... | collective-permute-start | bytes 1179656 | tf_op jit(solution)/shard_map/ppermute | solution.py:590
  23.6 18.8 %collective-permute-start.8 = (bf16[768,256]{1,0:T(8,128)(2,1)S(1)}, bf16[768,256]{1,0:T(8,128)(2,1)S(1)}, u32[]{:S(2)}, u32[]{:S(2)}) collective-permute-start(bf16[768,256]{1,0:T(8,128)(2,1)S(1)} %gate.7.refs_0_), channel_id=1, source_target_pairs={{0,1},{1,0},{2,3},{3,2},{4,5},{5,4},{6,7},{7,6},{8,9},{9,8},{10,11... | collective-permute-start | bytes 1179656 | tf_op jit(solution)/shard_map/ppermute | solution.py:590
  27.0 14.0 %collective-permute-start.2 = (bf16[768,256]{1,0:T(8,128)(2,1)S(1)}, bf16[768,256]{1,0:T(8,128)(2,1)S(1)}, u32[]{:S(2)}, u32[]{:S(2)}) collective-permute-start(bf16[768,256]{1,0:T(8,128)(2,1)S(1)} %get-tuple-element.42.refs_1_), channel_id=1, source_target_pairs={{1,2},{2,1},{5,6},{6,5},{9,10},{10,9},{13,14},{14,13},{17,18},{18,... | collective-permute-start | bytes 1179656 | tf_op jit(solution)/shard_map/ppermute | solution.py:590
  35.1 14.3 %collective-permute-start.6 = (bf16[768,256]{1,0:T(8,128)(2,1)S(1)}, bf16[768,256]{1,0:T(8,128)(2,1)S(1)}, u32[]{:S(2)}, u32[]{:S(2)}) collective-permute-start(bf16[768,256]{1,0:T(8,128)(2,1)S(1)} %gate.5.refs_4_.refs_0_), channel_id=1, source_target_pairs={{1,0},{2,3},{5,4},{6,7},{9,8},{10,11},{13,12},{14,15},{17,16},{18,... | collective-permute-start | bytes 1179656 | tf_op jit(solution)/shard_map/ppermute | solution.py:590
  41.1 15.2 %collective-permute-start.5 = (bf16[768,256]{1,0:T(8,128)(2,1)S(1)}, bf16[768,256]{1,0:T(8,128)(2,1)S(1)}, u32[]{:S(2)}, u32[]{:S(2)}) collective-permute-start(bf16[768,256]{1,0:T(8,128)(2,1)S(1)} %gate.6.refs_4_.refs_0_), channel_id=1, source_target_pairs={{1,0},{2,3},{5,4},{6,7},{9,8},{10,11},{13,12},{14,15},{17,16},{18,... | collective-permute-start | bytes 1179656 | tf_op jit(solution)/shard_map/ppermute | solution.py:590
  58.7 2.3 %collective-permute-start.9 = (f32[8,128,128]{2,1,0:T(8,128)S(1)}, f32[8,128,128]{2,1,0:T(8,128)S(1)}, u32[]{:S(2)}, u32[]{:S(2)}) collective-permute-start(f32[8,128,128]{2,1,0:T(8,128)S(1)} %get-tuple-element.62), channel_id=1, source_target_pairs={{0,4},{4,0},{8,12},{12,8},{16,20},{20,16},{24,28},{28,24},{1,5},{5... | collective-permute-start | bytes 1572872 | tf_op jit(solution)/shard_map/ppermute | solution.py:508
  61.0 12.1 %copy-start = (f32[16,128,128]{2,1,0:T(8,128)S(1)}, f32[16,128,128]{2,1,0:T(8,128)}, u32[]{:S(2)}) copy-start(f32[16,128,128]{2,1,0:T(8,128)} %prior.3) | copy-start | bytes 3145732
  61.1 5.0 %collective-permute-start.13 = (bf16[4,128,128]{2,1,0:T(8,128)(2,1)S(1)}, bf16[4,128,128]{2,1,0:T(8,128)(2,1)S(1)}, u32[]{:S(2)}, u32[]{:S(2)}) collective-permute-start(bf16[4,128,128]{2,1,0:T(8,128)(2,1)S(1)} %meet.9), channel_id=1, source_target_pairs={{0,8},{4,20},{8,0},{12,28},{16,24},{20,4},{24,16},{28,12},{1,9},{5... | collective-permute-start | bytes 393224 | tf_op jit(solution)/shard_map/ppermute | solution.py:522
  62.7 5.1 %collective-permute-start.10 = (bf16[4,128,128]{2,1,0:T(8,128)(2,1)S(1)}, bf16[4,128,128]{2,1,0:T(8,128)(2,1)S(1)}, u32[]{:S(2)}, u32[]{:S(2)}) collective-permute-start(bf16[4,128,128]{2,1,0:T(8,128)(2,1)S(1)} %meet.6), channel_id=1, source_target_pairs={{0,8},{4,20},{8,0},{12,28},{16,24},{20,4},{24,16},{28,12},{1,9},{5... | collective-permute-start | bytes 393224 | tf_op jit(solution)/shard_map/ppermute | solution.py:522
  66.2 17.3 %copy-start.2 = (f32[2048]{0:T(1024)S(1)}, f32[2048]{0:T(1024)}, u32[]{:S(2)}) copy-start(f32[2048]{0:T(1024)} %param.7) | copy-start | bytes 24580
  66.3 5.0 %collective-permute-start.14 = (bf16[4,128,128]{2,1,0:T(8,128)(2,1)S(1)}, bf16[4,128,128]{2,1,0:T(8,128)(2,1)S(1)}, u32[]{:S(2)}, u32[]{:S(2)}) collective-permute-start(bf16[4,128,128]{2,1,0:T(8,128)(2,1)S(1)} %meet.10), channel_id=1, source_target_pairs={{0,16},{4,12},{8,24},{12,4},{16,0},{20,28},{24,8},{28,20},{1,17},{... | collective-permute-start | bytes 393224 | tf_op jit(solution)/shard_map/ppermute | solution.py:522
  67.9 5.0 %collective-permute-start.11 = (bf16[4,128,128]{2,1,0:T(8,128)(2,1)S(1)}, bf16[4,128,128]{2,1,0:T(8,128)(2,1)S(1)}, u32[]{:S(2)}, u32[]{:S(2)}) collective-permute-start(bf16[4,128,128]{2,1,0:T(8,128)(2,1)S(1)} %meet.7), channel_id=1, source_target_pairs={{0,16},{4,12},{8,24},{12,4},{16,0},{20,28},{24,8},{28,20},{1,17},{... | collective-permute-start | bytes 393224 | tf_op jit(solution)/shard_map/ppermute | solution.py:522
  71.4 2.5 %collective-permute-start.15 = (f32[4,128,128]{2,1,0:T(8,128)S(1)}, f32[4,128,128]{2,1,0:T(8,128)S(1)}, u32[]{:S(2)}, u32[]{:S(2)}) collective-permute-start(f32[4,128,128]{2,1,0:T(8,128)S(1)} %get-tuple-element.65), channel_id=1, source_target_pairs={{0,4},{4,0},{8,12},{12,8},{16,20},{20,16},{24,28},{28,24},{1,5},{5... | collective-permute-start | bytes 786440 | tf_op jit(solution)/shard_map/ppermute | solution.py:526
  73.0 1.6 %collective-permute-start.12 = (f32[4,128,128]{2,1,0:T(8,128)S(1)}, f32[4,128,128]{2,1,0:T(8,128)S(1)}, u32[]{:S(2)}, u32[]{:S(2)}) collective-permute-start(f32[4,128,128]{2,1,0:T(8,128)S(1)} %get-tuple-element.64), channel_id=1, source_target_pairs={{0,4},{4,0},{8,12},{12,8},{16,20},{20,16},{24,28},{28,24},{1,5},{5... | collective-permute-start | bytes 786440 | tf_op jit(solution)/shard_map/ppermute | solution.py:526
  75.4 4.0 %collective-permute-start.18 = (f32[8,256]{1,0:T(8,128)S(1)}, f32[8,256]{1,0:T(8,128)S(1)}, u32[]{:S(2)}, u32[]{:S(2)}) collective-permute-start(f32[8,256]{1,0:T(8,128)S(1)} %get-tuple-element.72.refs_0_), channel_id=1, source_target_pairs={{0,3},{1,0},{2,1},{3,2},{4,7},{5,4},{6,5},{7,6},{8,11},{9,8},{10,9... | collective-permute-start | bytes 24584 | tf_op jit(solution)/shard_map/ppermute | solution.py:446
  78.1 4.5 %collective-permute-start.17 = (f32[8,256]{1,0:T(8,128)S(1)}, f32[8,256]{1,0:T(8,128)S(1)}, u32[]{:S(2)}, u32[]{:S(2)}) collective-permute-start(f32[8,256]{1,0:T(8,128)S(1)} %get-tuple-element.72.refs_0_), channel_id=1, source_target_pairs={{0,2},{1,3},{2,0},{3,1},{4,6},{5,7},{6,4},{7,5},{8,10},{9,11},{10,... | collective-permute-start | bytes 24584 | tf_op jit(solution)/shard_map/ppermute | solution.py:446
  78.1 5.4 %collective-permute-start.16 = (f32[8,256]{1,0:T(8,128)S(1)}, f32[8,256]{1,0:T(8,128)S(1)}, u32[]{:S(2)}, u32[]{:S(2)}) collective-permute-start(f32[8,256]{1,0:T(8,128)S(1)} %get-tuple-element.72.refs_0_), channel_id=1, source_target_pairs={{0,1},{1,2},{2,3},{3,0},{4,5},{5,6},{6,7},{7,4},{8,9},{9,10},{10,1... | collective-permute-start | bytes 24584 | tf_op jit(solution)/shard_map/ppermute | solution.py:446

commit v5 on v4

--- a/solution.py
+++ b/solution.py
@@ -389,15 +389,8 @@
     *square_refs, out_ref, held, sems = refs
     core = lax.axis_index("context") % 2
     squares = sum(ref[...] for ref in square_refs[1:]) + square_refs[0][...]
-    ones = jnp.ones((squares.shape[0], 128), F32)
-    mean_sq = lax.dot_general(
-        squares * (1.0 / squares.shape[0] / features),
-        ones,
-        (((0,), (0,)), ((), ())),
-        preferred_element_type=F32,
-        precision=lax.Precision.HIGHEST,
-    )
-    inverse = lax.rsqrt(mean_sq + EPSILON)
+    inverse = lax.rsqrt(squares[:1] * (1.0 / features) + EPSILON)
+    inverse = jnp.broadcast_to(inverse, (128, squares.shape[1])).T
     columns = held.shape[2]
     parts = att_own.shape[1] // columns
     copies = []
@@ -441,12 +434,12 @@
 
 
 def terms_over_tensor(x, n):
+    if n & (n - 1):
+        return [lax.psum(x, "tensor")]
     if n <= 4:
         return [x] + [
-            lax.ppermute(x, "tensor", [(i, (i + d) % n) for i in range(n)]) for d in range(1, n)
+            lax.ppermute(x, "tensor", [(i, i ^ d) for i in range(n)]) for d in range(1, n)
         ]
-    if n & (n - 1):
-        return [lax.psum(x, "tensor")]
     bit = 1
     while bit * 2 < n:
         x = x + lax.ppermute(x, "tensor", [(i, i ^ bit) for i in range(n)])

time: 85.4 us -> 84.3 us (0.987)
  waiting for transfers between devices: 14.8 us -> 12.7 us
  starting transfers between devices: 26.1 us -> 27.3 us
    ppermute x3, waiting for transfers between devices: 4.88 us -> 2.8 us  [terms_over_tensor(): lax.ppermute(x, 'tensor', [(i, i ^ d) for i in range(n)])]
    ppermute x3, starting transfers between devices: 3.24 us -> 4.42 us  [terms_over_tensor(): lax.ppermute(x, 'tensor', [(i, i ^ d) for i in range(n)])]
  transfers between devices with their start and end apart: 19 -> 19, of which waited for: 9 -> 8; matrix products, arithmetic and copies ran while one was open for 0% -> 0% of each run, Pallas kernels for 45% -> 45%
where the time goes in v5:
time: 84.3 us; the launch traced here: 84.1 us
  Pallas kernels  42.3 us (50%)
  starting transfers between devices  27.3 us (32%)
  waiting for transfers between devices  12.7 us (15%)
  local copies, waits for them, and re-layouts  1.18 us (1%)
    pallas_call x5, Pallas kernels, project(): pl.pallas_call(functools.partial(project_kernel, counts, first, picks, we...  32.3 us
    ppermute x9, starting transfers between devices, body(): lax.ppermute(x, 'tensor', pairs[chain][t])  17.4 us
    ppermute x4, starting transfers between devices, earlier_states(): gots[g] = gots[g] + [lax.ppermute(message, 'context', pairs)]  5.24 us
    ppermute x4, waiting for transfers between devices, earlier_states(): gots[g] = gots[g] + [lax.ppermute(message, 'context', pairs)]  4.71 us
    ppermute x9, waiting for transfers between devices, body(): lax.ppermute(x, 'tensor', pairs[chain][t])  4.49 us
    ppermute x3, starting transfers between devices, terms_over_tensor(): lax.ppermute(x, 'tensor', [(i, i ^ d) for i in range(n)])  4.42 us
    ppermute x3, waiting for transfers between devices, terms_over_tensor(): lax.ppermute(x, 'tensor', [(i, i ^ d) for i in range(n)])  2.8 us
    pallas_call x1, Pallas kernels, activate(): pl.pallas_call(functools.partial(first_kernel, len(choices), width, picks...  2.36 us
  transfers between devices with their start and end apart: 19, of which 8 were waited for; matrix products, arithmetic and copies ran while one was open for 0% of the time, Pallas kernels for 45%

profile of v5, /device:TPU:0, one launch (start us, length us, event | category | flops | bytes accessed | tf_op | source)
XLA Modules:
  0.0 84.1 jit_solution(15650698164179388383)
XLA Ops:
  0.0 3.0 %collective-permute-start = (bf16[1536,256]{1,0:T(8,128)(2,1)}, bf16[1536,256]{1,0:T(8,128)(2,1)S(1)}, u32[]{:S(2)}, u32[]{:S(2)}) collective-permute-start(bf16[1536,256]{1,0:T(8,128)(2,1)} %x.1), channel_id=1, source_target_pairs={{0,1},{1,0},{2,3},{3,2},{4,5},{5,4},{6,7},{7,6},{8,9},{9,8},{10,11... | collective-permute-start | bytes 2359304 | tf_op jit(solution)/shard_map/ppermute | solution.py:583
  3.0 1.2 %copy-done.1 = bf16[1536,256]{1,0:T(8,128)(2,1)S(1)} copy-done((bf16[1536,256]{1,0:T(8,128)(2,1)S(1)}, bf16[1536,256]{1,0:T(8,128)(2,1)}, u32[]{:S(2)}) %copy-start.1) | copy-done | bytes 786456
  4.2 0.4 cut.2
  4.6 0.7 collective-permute-start.1
  5.3 0.7 collective-permute-start.7
  6.0 10.8 %project.5 = (f32[256,6144]{1,0:T(8,128)S(1)}, f32[8,128]{1,0:T(8,128)S(1)}, bf16[1536,1024]{1,0:T(8,128)(2,1)S(1)}, bf16[768,6144]{1,0:T(8,128)(2,1)S(1)}) custom-call(bf16[768,256]{1,0:T(8,128)(2,1)S(1)} %get-tuple-element.39.refs_0_, bf16[768,256]{1,0:T(8,128)(2,1)S(1)} %get-tuple-element.40.refs_1_, bf16[6144,6144]{1,0:T(8,128)(2,1)} %refs_2_.9), custom_call_target="tpu_custom_call" | custom-call | flops 4831838208 | bytes 19660800 | tf_op jit(solution)/shard_map/project/pallas_call | solution.py:143
  16.8 0.0 collective-permute-done.1.refs_0_
  16.8 5.7 %collective-permute-start.3 = (bf16[768,256]{1,0:T(8,128)(2,1)S(1)}, bf16[768,256]{1,0:T(8,128)(2,1)S(1)}, u32[]{:S(2)}, u32[]{:S(2)}) collective-permute-start(bf16[768,256]{1,0:T(8,128)(2,1)S(1)} %gate.4.refs_0_.refs_4_), channel_id=1, source_target_pairs={{0,1},{1,0},{2,3},{3,2},{4,5},{5,4},{6,7},{7,6},{8,9},{9,8},{10,11... | collective-permute-start | bytes 1179656 | tf_op jit(solution)/shard_map/ppermute | solution.py:583
  22.5 0.4 cut.3
  22.9 0.7 collective-permute-start.4
  23.6 3.4 %collective-permute-start.8 = (bf16[768,256]{1,0:T(8,128)(2,1)S(1)}, bf16[768,256]{1,0:T(8,128)(2,1)S(1)}, u32[]{:S(2)}, u32[]{:S(2)}) collective-permute-start(bf16[768,256]{1,0:T(8,128)(2,1)S(1)} %gate.7.refs_0_), channel_id=1, source_target_pairs={{0,1},{1,0},{2,3},{3,2},{4,5},{5,4},{6,7},{7,6},{8,9},{9,8},{10,11... | collective-permute-start | bytes 1179656 | tf_op jit(solution)/shard_map/ppermute | solution.py:583
  27.0 0.7 collective-permute-start.2
  27.7 7.4 %project.6 = (f32[256,6144]{1,0:T(8,128)S(1)}, f32[8,128]{1,0:T(8,128)S(1)}, bf16[768,1024]{1,0:T(8,128)(2,1)S(1)}) custom-call(bf16[768,256]{1,0:T(8,128)(2,1)S(1)} %get-tuple-element.43.refs_0_.refs_1_, bf16[768,256]{1,0:T(8,128)(2,1)S(1)} %get-tuple-element.42.refs_1_, bf16[6144,6144]{1,0:T(8,128)(2,1)} %refs_2_.9, ...), custom_call_target="tpu_custom_call", output_to_operand_aliasing={{0}: (5, {})} | custom-call | flops 4831838208 | bytes 19660800 | tf_op jit(solution)/shard_map/project/pallas_call | solution.py:143
  35.1 1.3 %collective-permute-start.6 = (bf16[768,256]{1,0:T(8,128)(2,1)S(1)}, bf16[768,256]{1,0:T(8,128)(2,1)S(1)}, u32[]{:S(2)}, u32[]{:S(2)}) collective-permute-start(bf16[768,256]{1,0:T(8,128)(2,1)S(1)} %gate.5.refs_4_.refs_0_), channel_id=1, source_target_pairs={{1,0},{2,3},{5,4},{6,7},{9,8},{10,11},{13,12},{14,15},{17,16},{18,... | collective-permute-start | bytes 1179656 | tf_op jit(solution)/shard_map/ppermute | solution.py:583
  36.4 4.6 %project.7 = (f32[256,6144]{1,0:T(8,128)S(1)}, f32[8,128]{1,0:T(8,128)S(1)}, bf16[768,1024]{1,0:T(8,128)(2,1)S(1)}) custom-call(bf16[768,256]{1,0:T(8,128)(2,1)S(1)} %gate.4.refs_0_.refs_4_, bf16[768,256]{1,0:T(8,128)(2,1)S(1)} %collective-permute-done.3.refs_1_, bf16[6144,6144]{1,0:T(8,128)(2,1)} %refs_2_.9, ...), custom_call_target="tpu_custom_call", output_to_operand_aliasing={{0}: (5, {})} | custom-call | flops 2415919104 | bytes 9830400 | tf_op jit(solution)/shard_map/project/pallas_call | solution.py:143
  41.1 1.3 %collective-permute-start.5 = (bf16[768,256]{1,0:T(8,128)(2,1)S(1)}, bf16[768,256]{1,0:T(8,128)(2,1)S(1)}, u32[]{:S(2)}, u32[]{:S(2)}) collective-permute-start(bf16[768,256]{1,0:T(8,128)(2,1)S(1)} %gate.6.refs_4_.refs_0_), channel_id=1, source_target_pairs={{1,0},{2,3},{5,4},{6,7},{9,8},{10,11},{13,12},{14,15},{17,16},{18,... | collective-permute-start | bytes 1179656 | tf_op jit(solution)/shard_map/ppermute | solution.py:583
  42.4 4.8 %project.8 = (f32[256,6144]{1,0:T(8,128)S(1)}, f32[8,128]{1,0:T(8,128)S(1)}, bf16[768,1024]{1,0:T(8,128)(2,1)S(1)}) custom-call(bf16[768,256]{1,0:T(8,128)(2,1)S(1)} %gate.7.refs_0_, bf16[768,256]{1,0:T(8,128)(2,1)S(1)} %collective-permute-done.8.refs_1_, bf16[6144,6144]{1,0:T(8,128)(2,1)} %refs_2_.9, ...), custom_call_target="tpu_custom_call", output_to_operand_aliasing={{0}: (5, {})} | custom-call | flops 2415919104 | bytes 9830400 | tf_op jit(solution)/shard_map/project/pallas_call | solution.py:143
  47.2 2.1 %collective-permute-done.6.refs_1_ = bf16[768,256]{1,0:T(8,128)(2,1)S(1)} collective-permute-done((bf16[768,256]{1,0:T(8,128)(2,1)S(1)}, bf16[768,256]{1,0:T(8,128)(2,1)S(1)}, u32[]{:S(2)}, u32[]{:S(2)}) %collective-permute-start.6) | collective-permute-done | bytes 393248 | tf_op jit(solution)/shard_map/ppermute | solution.py:583
  49.4 4.6 %project.9 = (f32[256,6144]{1,0:T(8,128)S(1)}, f32[8,128]{1,0:T(8,128)}) custom-call(bf16[768,256]{1,0:T(8,128)(2,1)S(1)} %gate.5.refs_4_.refs_0_, bf16[768,256]{1,0:T(8,128)(2,1)S(1)} %collective-permute-done.6.refs_1_, bf16[6144,6144]{1,0:T(8,128)(2,1)} %refs_2_.9, ...), custom_call_target="tpu_custom_call", output_to_operand_aliasing={{0}: (5, {})} | custom-call | flops 2415919104 | bytes 9830400 | tf_op jit(solution)/shard_map/project/pallas_call | solution.py:143
  54.0 2.3 %collective-permute-done.5.refs_1_ = bf16[768,256]{1,0:T(8,128)(2,1)S(1)} collective-permute-done((bf16[768,256]{1,0:T(8,128)(2,1)S(1)}, bf16[768,256]{1,0:T(8,128)(2,1)S(1)}, u32[]{:S(2)}, u32[]{:S(2)}) %collective-permute-start.5) | collective-permute-done | bytes 393248 | tf_op jit(solution)/shard_map/ppermute | solution.py:583
  56.3 2.4 %activate.2 = (bf16[256,768]{1,0:T(8,128)(2,1)S(1)}, bf16[256,3072]{1,0:T(8,128)(2,1)S(1)}, f32[8,128,128]{2,1,0:T(8,128)S(1)}) custom-call(bf16[768,256]{1,0:T(8,128)(2,1)S(1)} %gate.6.refs_4_.refs_0_, bf16[768,256]{1,0:T(8,128)(2,1)S(1)} %collective-permute-done.5.refs_1_, bf16[768,6144]{1,0:T(8,128)(2,1)S(1)} %get-tuple-element.50.refs_2_.slab, ...), custom_call_target="tpu_custom_call" | custom-call | flops 1275068416 | bytes 393216 | tf_op jit(solution)/shard_map/activate/pallas_call | solution.py:273
  58.7 0.1 collective-permute-start.9
  58.8 2.2 %activate.3 = (bf16[256,3072]{1,0:T(8,128)(2,1)S(1)}, f32[8,128,128]{2,1,0:T(8,128)S(1)}) custom-call(bf16[256,768]{1,0:T(8,128)(2,1)S(1)} %get-tuple-element.58.turned, bf16[768,6144]{1,0:T(8,128)(2,1)S(1)} %get-tuple-element.50.refs_2_.slab, f32[256,6144]{1,0:T(8,128)S(1)} %get-tuple-element.56.refs_3_.total), custom_call_target="tpu_custom_call" | custom-call | flops 1275068416 | bytes 393216 | tf_op jit(solution)/shard_map/activate/pallas_call | solution.py:282
  61.0 0.0 copy-start
  61.1 0.1 meet.9
  61.1 1.6 %collective-permute-start.13 = (bf16[4,128,128]{2,1,0:T(8,128)(2,1)S(1)}, bf16[4,128,128]{2,1,0:T(8,128)(2,1)S(1)}, u32[]{:S(2)}, u32[]{:S(2)}) collective-permute-start(bf16[4,128,128]{2,1,0:T(8,128)(2,1)S(1)} %meet.9), channel_id=1, source_target_pairs={{0,8},{4,20},{8,0},{12,28},{16,24},{20,4},{24,16},{28,12},{1,9},{5... | collective-permute-start | bytes 393224 | tf_op jit(solution)/shard_map/ppermute | solution.py:515
  62.7 0.6 collective-permute-start.10
  63.3 1.5 %within.1 = (f32[256,1024]{1,0:T(8,128)S(1)}, f32[256,1024]{1,0:T(8,128)S(1)}, f32[8,128]{1,0:T(8,128)S(1)}) custom-call(bf16[256,3072]{1,0:T(8,128)(2,1)S(1)} %get-tuple-element.57.refs_0_.act, bf16[256,3072]{1,0:T(8,128)(2,1)S(1)} %get-tuple-element.59.refs_1_.act), custom_call_target="tpu_custom_call" | custom-call | flops 536870912 | bytes 3145728 | tf_op jit(solution)/shard_map/within/pallas_call | solution.py:318
  64.8 1.3 %collective-permute-done.13.refs_2_ = bf16[4,128,128]{2,1,0:T(8,128)(2,1)S(1)} collective-permute-done((bf16[4,128,128]{2,1,0:T(8,128)(2,1)S(1)}, bf16[4,128,128]{2,1,0:T(8,128)(2,1)S(1)}, u32[]{:S(2)}, u32[]{:S(2)}) %collective-permute-start.13) | collective-permute-done | bytes 131104 | tf_op jit(solution)/shard_map/ppermute | solution.py:515
  66.2 0.1 meet.10
  66.2 0.0 copy-start.2
  66.3 1.6 %collective-permute-start.14 = (bf16[4,128,128]{2,1,0:T(8,128)(2,1)S(1)}, bf16[4,128,128]{2,1,0:T(8,128)(2,1)S(1)}, u32[]{:S(2)}, u32[]{:S(2)}) collective-permute-start(bf16[4,128,128]{2,1,0:T(8,128)(2,1)S(1)} %meet.10), channel_id=1, source_target_pairs={{0,16},{4,12},{8,24},{12,4},{16,0},{20,28},{24,8},{28,20},{1,17},{... | collective-permute-start | bytes 393224 | tf_op jit(solution)/shard_map/ppermute | solution.py:515
  67.8 0.1 meet.7
  67.9 1.5 %collective-permute-start.11 = (bf16[4,128,128]{2,1,0:T(8,128)(2,1)S(1)}, bf16[4,128,128]{2,1,0:T(8,128)(2,1)S(1)}, u32[]{:S(2)}, u32[]{:S(2)}) collective-permute-start(bf16[4,128,128]{2,1,0:T(8,128)(2,1)S(1)} %meet.7), channel_id=1, source_target_pairs={{0,16},{4,12},{8,24},{12,4},{16,0},{20,28},{24,8},{28,20},{1,17},{... | collective-permute-start | bytes 393224 | tf_op jit(solution)/shard_map/ppermute | solution.py:515
  69.4 1.9 %collective-permute-done.14.refs_3_ = bf16[4,128,128]{2,1,0:T(8,128)(2,1)S(1)} collective-permute-done((bf16[4,128,128]{2,1,0:T(8,128)(2,1)S(1)}, bf16[4,128,128]{2,1,0:T(8,128)(2,1)S(1)}, u32[]{:S(2)}, u32[]{:S(2)}) %collective-permute-start.14) | collective-permute-done | bytes 131104 | tf_op jit(solution)/shard_map/ppermute | solution.py:515
  71.3 0.1 meet.11
  71.4 0.1 collective-permute-start.15
  71.4 1.5 %collective-permute-done.11.refs_3_ = bf16[4,128,128]{2,1,0:T(8,128)(2,1)S(1)} collective-permute-done((bf16[4,128,128]{2,1,0:T(8,128)(2,1)S(1)}, bf16[4,128,128]{2,1,0:T(8,128)(2,1)S(1)}, u32[]{:S(2)}, u32[]{:S(2)}) %collective-permute-start.11) | collective-permute-done | bytes 131104 | tf_op jit(solution)/shard_map/ppermute | solution.py:515
  73.0 0.1 meet.8
  73.0 0.1 collective-permute-start.12
  73.1 0.8 across.2
  73.9 0.7 collective-permute-done.12.refs_0_
  74.6 0.7 across.3
  75.4 2.7 %collective-permute-start.18 = (f32[8,256]{1,0:T(8,128)S(1)}, f32[8,256]{1,0:T(8,128)S(1)}, u32[]{:S(2)}, u32[]{:S(2)}) collective-permute-start(f32[8,256]{1,0:T(8,128)S(1)} %get-tuple-element.72.refs_0_), channel_id=1, source_target_pairs={{0,3},{1,2},{2,1},{3,0},{4,7},{5,6},{6,5},{7,4},{8,11},{9,10},{10,... | collective-permute-start | bytes 24584 | tf_op jit(solution)/shard_map/ppermute | solution.py:441
  78.1 1.7 %collective-permute-start.16 = (f32[8,256]{1,0:T(8,128)S(1)}, f32[8,256]{1,0:T(8,128)S(1)}, u32[]{:S(2)}, u32[]{:S(2)}) collective-permute-start(f32[8,256]{1,0:T(8,128)S(1)} %get-tuple-element.72.refs_0_), channel_id=1, source_target_pairs={{0,1},{1,0},{2,3},{3,2},{4,5},{5,4},{6,7},{7,6},{8,9},{9,8},{10,11... | collective-permute-start | bytes 24584 | tf_op jit(solution)/shard_map/ppermute | solution.py:441
  79.8 1.1 %collective-permute-done.18.refs_3_ = f32[8,256]{1,0:T(8,128)S(1)} collective-permute-done((f32[8,256]{1,0:T(8,128)S(1)}, f32[8,256]{1,0:T(8,128)S(1)}, u32[]{:S(2)}, u32[]{:S(2)}) %collective-permute-start.18) | collective-permute-done | bytes 8224 | tf_op jit(solution)/shard_map/ppermute | solution.py:441
  80.9 1.7 %collective-permute-done.17.refs_2_ = f32[8,256]{1,0:T(8,128)S(1)} collective-permute-done((f32[8,256]{1,0:T(8,128)S(1)}, f32[8,256]{1,0:T(8,128)S(1)}, u32[]{:S(2)}, u32[]{:S(2)}) %collective-permute-start.17) | collective-permute-done | bytes 8224 | tf_op jit(solution)/shard_map/ppermute | solution.py:441
  82.6 1.3 %normalize.1 = bf16[256,2048]{1,0:T(8,128)(2,1)} custom-call(f32[256,1024]{1,0:T(8,128)S(1)} %get-tuple-element.70.att_other, f32[256,1024]{1,0:T(8,128)S(1)} %get-tuple-element.71.att_own, f32[1,2048]{1,0:T(1,128)S(1)} %bitcast.1, f32[8,256]{1,0:T(8,128)S(1)} %get-tuple-element.72.refs_0_, f32[8,256]{1,0:T(8,128)S(1)} %collective-permute-done.16.refs_1_, ...), custom_call_target="tpu_custom_call" | custom-call | flops 1048576 | bytes 1048576 | tf_op jit(solution)/shard_map/normalize/pallas_call | solution.py:419
  (19 shorter events, 0.1 us)
Async XLA Ops:
  0.0 22.5 %collective-permute-start = (bf16[1536,256]{1,0:T(8,128)(2,1)}, bf16[1536,256]{1,0:T(8,128)(2,1)S(1)}, u32[]{:S(2)}, u32[]{:S(2)}) collective-permute-start(bf16[1536,256]{1,0:T(8,128)(2,1)} %x.1), channel_id=1, source_target_pairs={{0,1},{1,0},{2,3},{3,2},{4,5},{5,4},{6,7},{7,6},{8,9},{9,8},{10,11... | collective-permute-start | bytes 2359304 | tf_op jit(solution)/shard_map/ppermute | solution.py:583
  3.0 1.2 %copy-start.1 = (bf16[1536,256]{1,0:T(8,128)(2,1)S(1)}, bf16[1536,256]{1,0:T(8,128)(2,1)}, u32[]{:S(2)}) copy-start(bf16[1536,256]{1,0:T(8,128)(2,1)} %x.1) | copy-start | bytes 2359300
  4.6 12.2 %collective-permute-start.1 = (bf16[768,256]{1,0:T(8,128)(2,1)S(1)}, bf16[768,256]{1,0:T(8,128)(2,1)S(1)}, u32[]{:S(2)}, u32[]{:S(2)}) collective-permute-start(bf16[768,256]{1,0:T(8,128)(2,1)S(1)} %get-tuple-element.39.refs_0_), channel_id=1, source_target_pairs={{1,2},{2,1},{5,6},{6,5},{9,10},{10,9},{13,14},{14,13},{17,18},{18,... | collective-permute-start | bytes 1179656 | tf_op jit(solution)/shard_map/ppermute | solution.py:583
  5.3 18.3 %collective-permute-start.7 = (bf16[768,256]{1,0:T(8,128)(2,1)S(1)}, bf16[768,256]{1,0:T(8,128)(2,1)S(1)}, u32[]{:S(2)}, u32[]{:S(2)}) collective-permute-start(bf16[768,256]{1,0:T(8,128)(2,1)S(1)} %get-tuple-element.40.refs_1_), channel_id=1, source_target_pairs={{1,2},{2,1},{5,6},{6,5},{9,10},{10,9},{13,14},{14,13},{17,18},{18,... | collective-permute-start | bytes 1179656 | tf_op jit(solution)/shard_map/ppermute | solution.py:583
  16.8 19.6 %collective-permute-start.3 = (bf16[768,256]{1,0:T(8,128)(2,1)S(1)}, bf16[768,256]{1,0:T(8,128)(2,1)S(1)}, u32[]{:S(2)}, u32[]{:S(2)}) collective-permute-start(bf16[768,256]{1,0:T(8,128)(2,1)S(1)} %gate.4.refs_0_.refs_4_), channel_id=1, source_target_pairs={{0,1},{1,0},{2,3},{3,2},{4,5},{5,4},{6,7},{7,6},{8,9},{9,8},{10,11... | collective-permute-start | bytes 1179656 | tf_op jit(solution)/shard_map/ppermute | solution.py:583
  22.9 12.2 %collective-permute-start.4 = (bf16[768,256]{1,0:T(8,128)(2,1)S(1)}, bf16[768,256]{1,0:T(8,128)(2,1)S(1)}, u32[]{:S(2)}, u32[]{:S(2)}) collective-permute-start(bf16[768,256]{1,0:T(8,128)(2,1)S(1)} %get-tuple-element.43.refs_0_.refs_1_), channel_id=1, source_target_pairs={{1,2},{2,1},{5,6},{6,5},{9,10},{10,9},{13,14},{14,13},{17,18},{18,... | collective-permute-start | bytes 1179656 | tf_op jit(solution)/shard_map/ppermute | solution.py:583
  23.6 18.8 %collective-permute-start.8 = (bf16[768,256]{1,0:T(8,128)(2,1)S(1)}, bf16[768,256]{1,0:T(8,128)(2,1)S(1)}, u32[]{:S(2)}, u32[]{:S(2)}) collective-permute-start(bf16[768,256]{1,0:T(8,128)(2,1)S(1)} %gate.7.refs_0_), channel_id=1, source_target_pairs={{0,1},{1,0},{2,3},{3,2},{4,5},{5,4},{6,7},{7,6},{8,9},{9,8},{10,11... | collective-permute-start | bytes 1179656 | tf_op jit(solution)/shard_map/ppermute | solution.py:583
  27.0 14.0 %collective-permute-start.2 = (bf16[768,256]{1,0:T(8,128)(2,1)S(1)}, bf16[768,256]{1,0:T(8,128)(2,1)S(1)}, u32[]{:S(2)}, u32[]{:S(2)}) collective-permute-start(bf16[768,256]{1,0:T(8,128)(2,1)S(1)} %get-tuple-element.42.refs_1_), channel_id=1, source_target_pairs={{1,2},{2,1},{5,6},{6,5},{9,10},{10,9},{13,14},{14,13},{17,18},{18,... | collective-permute-start | bytes 1179656 | tf_op jit(solution)/shard_map/ppermute | solution.py:583
  35.1 14.3 %collective-permute-start.6 = (bf16[768,256]{1,0:T(8,128)(2,1)S(1)}, bf16[768,256]{1,0:T(8,128)(2,1)S(1)}, u32[]{:S(2)}, u32[]{:S(2)}) collective-permute-start(bf16[768,256]{1,0:T(8,128)(2,1)S(1)} %gate.5.refs_4_.refs_0_), channel_id=1, source_target_pairs={{1,0},{2,3},{5,4},{6,7},{9,8},{10,11},{13,12},{14,15},{17,16},{18,... | collective-permute-start | bytes 1179656 | tf_op jit(solution)/shard_map/ppermute | solution.py:583
  41.1 15.2 %collective-permute-start.5 = (bf16[768,256]{1,0:T(8,128)(2,1)S(1)}, bf16[768,256]{1,0:T(8,128)(2,1)S(1)}, u32[]{:S(2)}, u32[]{:S(2)}) collective-permute-start(bf16[768,256]{1,0:T(8,128)(2,1)S(1)} %gate.6.refs_4_.refs_0_), channel_id=1, source_target_pairs={{1,0},{2,3},{5,4},{6,7},{9,8},{10,11},{13,12},{14,15},{17,16},{18,... | collective-permute-start | bytes 1179656 | tf_op jit(solution)/shard_map/ppermute | solution.py:583
  58.7 2.3 %collective-permute-start.9 = (f32[8,128,128]{2,1,0:T(8,128)S(1)}, f32[8,128,128]{2,1,0:T(8,128)S(1)}, u32[]{:S(2)}, u32[]{:S(2)}) collective-permute-start(f32[8,128,128]{2,1,0:T(8,128)S(1)} %get-tuple-element.62), channel_id=1, source_target_pairs={{0,4},{4,0},{8,12},{12,8},{16,20},{20,16},{24,28},{28,24},{1,5},{5... | collective-permute-start | bytes 1572872 | tf_op jit(solution)/shard_map/ppermute | solution.py:501
  61.0 12.1 %copy-start = (f32[16,128,128]{2,1,0:T(8,128)S(1)}, f32[16,128,128]{2,1,0:T(8,128)}, u32[]{:S(2)}) copy-start(f32[16,128,128]{2,1,0:T(8,128)} %prior.3) | copy-start | bytes 3145732
  61.1 5.0 %collective-permute-start.13 = (bf16[4,128,128]{2,1,0:T(8,128)(2,1)S(1)}, bf16[4,128,128]{2,1,0:T(8,128)(2,1)S(1)}, u32[]{:S(2)}, u32[]{:S(2)}) collective-permute-start(bf16[4,128,128]{2,1,0:T(8,128)(2,1)S(1)} %meet.9), channel_id=1, source_target_pairs={{0,8},{4,20},{8,0},{12,28},{16,24},{20,4},{24,16},{28,12},{1,9},{5... | collective-permute-start | bytes 393224 | tf_op jit(solution)/shard_map/ppermute | solution.py:515
  62.7 5.1 %collective-permute-start.10 = (bf16[4,128,128]{2,1,0:T(8,128)(2,1)S(1)}, bf16[4,128,128]{2,1,0:T(8,128)(2,1)S(1)}, u32[]{:S(2)}, u32[]{:S(2)}) collective-permute-start(bf16[4,128,128]{2,1,0:T(8,128)(2,1)S(1)} %meet.6), channel_id=1, source_target_pairs={{0,8},{4,20},{8,0},{12,28},{16,24},{20,4},{24,16},{28,12},{1,9},{5... | collective-permute-start | bytes 393224 | tf_op jit(solution)/shard_map/ppermute | solution.py:515
  66.2 16.4 %copy-start.2 = (f32[2048]{0:T(1024)S(1)}, f32[2048]{0:T(1024)}, u32[]{:S(2)}) copy-start(f32[2048]{0:T(1024)} %param.7) | copy-start | bytes 24580
  66.3 5.0 %collective-permute-start.14 = (bf16[4,128,128]{2,1,0:T(8,128)(2,1)S(1)}, bf16[4,128,128]{2,1,0:T(8,128)(2,1)S(1)}, u32[]{:S(2)}, u32[]{:S(2)}) collective-permute-start(bf16[4,128,128]{2,1,0:T(8,128)(2,1)S(1)} %meet.10), channel_id=1, source_target_pairs={{0,16},{4,12},{8,24},{12,4},{16,0},{20,28},{24,8},{28,20},{1,17},{... | collective-permute-start | bytes 393224 | tf_op jit(solution)/shard_map/ppermute | solution.py:515
  67.9 5.0 %collective-permute-start.11 = (bf16[4,128,128]{2,1,0:T(8,128)(2,1)S(1)}, bf16[4,128,128]{2,1,0:T(8,128)(2,1)S(1)}, u32[]{:S(2)}, u32[]{:S(2)}) collective-permute-start(bf16[4,128,128]{2,1,0:T(8,128)(2,1)S(1)} %meet.7), channel_id=1, source_target_pairs={{0,16},{4,12},{8,24},{12,4},{16,0},{20,28},{24,8},{28,20},{1,17},{... | collective-permute-start | bytes 393224 | tf_op jit(solution)/shard_map/ppermute | solution.py:515
  71.4 2.5 %collective-permute-start.15 = (f32[4,128,128]{2,1,0:T(8,128)S(1)}, f32[4,128,128]{2,1,0:T(8,128)S(1)}, u32[]{:S(2)}, u32[]{:S(2)}) collective-permute-start(f32[4,128,128]{2,1,0:T(8,128)S(1)} %get-tuple-element.65), channel_id=1, source_target_pairs={{0,4},{4,0},{8,12},{12,8},{16,20},{20,16},{24,28},{28,24},{1,5},{5... | collective-permute-start | bytes 786440 | tf_op jit(solution)/shard_map/ppermute | solution.py:519
  73.0 1.6 %collective-permute-start.12 = (f32[4,128,128]{2,1,0:T(8,128)S(1)}, f32[4,128,128]{2,1,0:T(8,128)S(1)}, u32[]{:S(2)}, u32[]{:S(2)}) collective-permute-start(f32[4,128,128]{2,1,0:T(8,128)S(1)} %get-tuple-element.64), channel_id=1, source_target_pairs={{0,4},{4,0},{8,12},{12,8},{16,20},{20,16},{24,28},{28,24},{1,5},{5... | collective-permute-start | bytes 786440 | tf_op jit(solution)/shard_map/ppermute | solution.py:519
  75.4 5.5 %collective-permute-start.18 = (f32[8,256]{1,0:T(8,128)S(1)}, f32[8,256]{1,0:T(8,128)S(1)}, u32[]{:S(2)}, u32[]{:S(2)}) collective-permute-start(f32[8,256]{1,0:T(8,128)S(1)} %get-tuple-element.72.refs_0_), channel_id=1, source_target_pairs={{0,3},{1,2},{2,1},{3,0},{4,7},{5,6},{6,5},{7,4},{8,11},{9,10},{10,... | collective-permute-start | bytes 24584 | tf_op jit(solution)/shard_map/ppermute | solution.py:441
  78.1 4.5 %collective-permute-start.17 = (f32[8,256]{1,0:T(8,128)S(1)}, f32[8,256]{1,0:T(8,128)S(1)}, u32[]{:S(2)}, u32[]{:S(2)}) collective-permute-start(f32[8,256]{1,0:T(8,128)S(1)} %get-tuple-element.72.refs_0_), channel_id=1, source_target_pairs={{0,2},{1,3},{2,0},{3,1},{4,6},{5,7},{6,4},{7,5},{8,10},{9,11},{10,... | collective-permute-start | bytes 24584 | tf_op jit(solution)/shard_map/ppermute | solution.py:441
  78.1 4.5 %collective-permute-start.16 = (f32[8,256]{1,0:T(8,128)S(1)}, f32[8,256]{1,0:T(8,128)S(1)}, u32[]{:S(2)}, u32[]{:S(2)}) collective-permute-start(f32[8,256]{1,0:T(8,128)S(1)} %get-tuple-element.72.refs_0_), channel_id=1, source_target_pairs={{0,1},{1,0},{2,3},{3,2},{4,5},{5,4},{6,7},{7,6},{8,9},{9,8},{10,11... | collective-permute-start | bytes 24584 | tf_op jit(solution)/shard_map/ppermute | solution.py:441

commit v6 on v5

--- a/solution.py
+++ b/solution.py
@@ -24,22 +24,6 @@
 HBM = pl.BlockSpec(memory_space=pltpu.HBM)
 WHOLE = pl.BlockSpec(memory_space=pltpu.VMEM)
 ANY = pl.BlockSpec(memory_space=pl.ANY)
-
-
-def start_features(pick, choices, raw, sem):
-    for c, pieces in enumerate(choices):
-
-        @pl.when(pick == c)
-        def _(pieces=pieces):
-            at = 0
-            for piece in pieces:
-                there = raw.at[pl.ds(at, piece.shape[0])]
-                pltpu.make_async_copy(piece, there, sem).start()
-                at += piece.shape[0]
-
-
-def wait_features(raw, sem):
-    pltpu.make_async_copy(raw, raw, sem).wait()
 
 
 def of_place(values):
@@ -54,6 +38,21 @@
 def column_blocks(columns):
     width = COLUMNS if columns % COLUMNS == 0 else columns
     return [pl.ds(at, width) for at in range(0, columns, width)]
+
+
+def turn_features(pick, choices, turned):
+    for c, pieces in enumerate(choices):
+
+        def turn(pieces=pieces):
+            at = 0
+            for piece in pieces:
+                turned[:, at : at + piece.shape[0]] = piece[...].T
+                at += piece.shape[0]
+
+        if len(choices) == 1:
+            turn()
+        else:
+            pl.when(pick == c)(turn)
 
 
 def project_kernel(counts, first, picks, weight_rows, next_rows, slab_rows, *refs):
@@ -66,13 +65,12 @@
     total, done = refs.pop(0), refs.pop(0)
     next_block = refs.pop(0) if next_rows else None
     slab = refs.pop(0) if slab_rows else None
-    raw, turned, held, sem, weight_sems = refs
+    turned, held, weight_sems = refs
     done[...] = jnp.zeros_like(done)
-    rows = raw.shape[0]
+    rows = turned.shape[1]
     slots = held.shape[0]
     blocks = column_blocks(weight.shape[1])
 
-    start_features(of_place(picks), choices, raw, sem)
     at = pl.ds(pl.multiple_of(of_place(weight_rows), 16), rows)
     streamed = blocks if first else blocks[1:]
     copies = [
@@ -93,8 +91,7 @@
         )
     for copy in copies[:slots]:
         copy.start()
-    wait_features(raw, sem)
-    turned[...] = raw[...].T
+    turn_features(of_place(picks), choices, turned)
     for b, block in enumerate(blocks):
         b = b if first else b - 1
         if b < 0:
@@ -145,17 +142,15 @@
             project_kernel, counts, first, picks, weight_rows, next_rows, slab_rows
         ),
         out_shape=out_shape,
-        in_specs=[ANY] * len(flat) + [HBM] + ([] if first else [WHOLE, ANY, WHOLE]),
+        in_specs=[WHOLE] * len(flat) + [HBM] + ([] if first else [WHOLE, ANY, WHOLE]),
         out_specs=[WHOLE] * len(out_shape),
         scratch_shapes=[
-            pltpu.VMEM((rows, tokens), BF16),
             pltpu.VMEM((tokens, rows), BF16),
             pltpu.VMEM((slots, rows, block), BF16),
-            pltpu.SemaphoreType.DMA,
             pltpu.SemaphoreType.DMA((len(blocks) + 2,)),
         ],
         input_output_aliases={} if first else {len(operands) - 1: 0},
-        compiler_params=params(2 * rows * (2 * tokens + slots * block)),
+        compiler_params=params(2 * rows * (tokens + slots * block)),
         cost_estimate=pl.CostEstimate(
             flops=2 * tokens * rows * columns,
             bytes_accessed=rows * columns * 2 + rows * tokens * 2,
@@ -241,13 +236,7 @@
 def first_kernel(n_choices, width, picks, *refs):
     choices = refs[:n_choices]
     slab, total, turned, act_ref, state_ref = refs[n_choices:]
-    pick = of_place(picks)
-    for c, choice in enumerate(choices):
-
-        @pl.when(pick == c)
-        def _(choice=choice):
-            turned[...] = choice[...].T
-
+    turn_features(of_place(picks), [[choice] for choice in choices], turned)
     side = 1 - lax.axis_index("context") % 2
     activate_heads(side, width, turned, slab, total, act_ref, state_ref)
 
@@ -438,7 +427,7 @@
         return [lax.psum(x, "tensor")]
     if n <= 4:
         return [x] + [
-            lax.ppermute(x, "tensor", [(i, i ^ d) for i in range(n)]) for d in range(1, n)
+            lax.ppermute(x, "tensor", [(i, i ^ d) for i in range(n)]) for d in range(n - 1, 0, -1)
         ]
     bit = 1
     while bit * 2 < n:
@@ -531,8 +520,6 @@
                 here = share + way * t
                 if 0 <= here < n and 0 <= here + way < n:
                     pairs[chain][t].append((here, here + way))
-                    if t == 1 and chain == 1:
-                        pairs[chain][t].append((here + way, here))
                     arrivals[here + way].append((t, chain, share))
     pairs = [[sorted(set(p)) for p in chain] for chain in pairs]
     return pairs, arrivals
@@ -551,6 +538,7 @@
 
     steps = [(-1, None), (0, None)] + [(1, 0), (1, 1)] + [(m, None) for m in range(2, last)]
     steps = [step for step in steps if step[0] < last] + [(last, 0)]
+    slab_at = len(steps) - 2
 
     def rows_of(m, piece):
         starts = [there[m][2] if m >= 0 else i for i, there in enumerate(arrivals)]
@@ -564,7 +552,7 @@
         following = []
         if number + 1 < len(steps):
             following = [rows_of(*steps[number + 1]), count_of(steps[number + 1][1])]
-            if number == 0:
+            if number == slab_at:
                 following += [rows_of(last, 1), share - early]
         choices, picks = [pieces], [0] * n_tensor
         if m >= 0:
@@ -575,7 +563,7 @@
             choices, picks, qkv_weight, rows_of(m, piece), ready, total, after, *following
         )
 
-    total, done, ready, slab = run(0, None, None, None)
+    total, done, ready, *slab = run(0, None, None, None)
     number = 1
     for t in range(n_tensor - 1):
         for chain in range(2):
@@ -590,7 +578,8 @@
                 held[1][1] = gate(held[1][1], held[0][0])
         gates = [0, 1] if t == 1 and t < last else []
         while number < len(steps) - 1 and 1 <= t >= steps[number][0]:
-            total, done, ready = run(number, ready, total, done)
+            total, done, ready, *more = run(number, ready, total, done)
+            slab += more
             number += 1
             if gates:
                 j = gates.pop(0)
@@ -601,7 +590,7 @@
     picks = [keys.index(there[last][:2]) for there in arrivals]
     choices = [came[key] for key in keys]
     other_act, other_states, own_act, own_states = activate(
-        [c[1] for c in choices], picks, slab, total, heads, width
+        [c[1] for c in choices], picks, slab[0], total, heads, width
     )
     other_within, own_within, done = attend_within(other_act, own_act, width)
     other, own = earlier_states(other_states, own_states, [done], n_context)

time: 84.3 us -> 83.6 us (level)
  waiting for transfers between devices: 12.7 us -> 19.3 us
  starting transfers between devices: 27.3 us -> 20.8 us
    ppermute x9, starting transfers between devices: 17.4 us -> 10.9 us  [body(): lax.ppermute(x, 'tensor', pairs[chain][t])]
    ppermute x9, waiting for transfers between devices: 4.49 us -> 10.8 us  [body(): lax.ppermute(x, 'tensor', pairs[chain][t])]
  transfers between devices with their start and end apart: 19 -> 19, of which waited for: 8 -> 9; matrix products, arithmetic and copies ran while one was open for 0% -> 0% of each run, Pallas kernels for 45% -> 45%
where the time goes in v6:
time: 83.6 us; the launch traced here: 83.3 us
  Pallas kernels  41.5 us (50%)
  starting transfers between devices  20.8 us (25%)
  waiting for transfers between devices  19.3 us (23%)
  local copies, waits for them, and re-layouts  1.18 us (1%)
    pallas_call x5, Pallas kernels, project(): pl.pallas_call(functools.partial(project_kernel, counts, first, picks, we...  31.5 us
    ppermute x9, starting transfers between devices, body(): lax.ppermute(x, 'tensor', pairs[chain][t])  10.9 us
    ppermute x9, waiting for transfers between devices, body(): lax.ppermute(x, 'tensor', pairs[chain][t])  10.8 us
    ppermute x4, starting transfers between devices, earlier_states(): gots[g] = gots[g] + [lax.ppermute(message, 'context', pairs)]  5.26 us
    ppermute x4, waiting for transfers between devices, earlier_states(): gots[g] = gots[g] + [lax.ppermute(message, 'context', pairs)]  4.69 us
    ppermute x3, starting transfers between devices, terms_over_tensor(): lax.ppermute(x, 'tensor', [(i, i ^ d) for i in range(n)])  4.42 us
    ppermute x3, waiting for transfers between devices, terms_over_tensor(): lax.ppermute(x, 'tensor', [(i, i ^ d) for i in range(n)])  3.04 us
    pallas_call x1, Pallas kernels, activate(): pl.pallas_call(functools.partial(first_kernel, len(choices), width, picks...  2.36 us
  transfers between devices with their start and end apart: 19, of which 9 were waited for; matrix products, arithmetic and copies ran while one was open for 0% of the time, Pallas kernels for 45%

profile of v6, /device:TPU:0, one launch (start us, length us, event | category | flops | bytes accessed | tf_op | source)
XLA Modules:
  0.0 83.3 jit_solution(16325774534046025211)
XLA Ops:
  0.0 3.0 %collective-permute-start = (bf16[1536,256]{1,0:T(8,128)(2,1)}, bf16[1536,256]{1,0:T(8,128)(2,1)S(1)}, u32[]{:S(2)}, u32[]{:S(2)}) collective-permute-start(bf16[1536,256]{1,0:T(8,128)(2,1)} %x.1), channel_id=1, source_target_pairs={{0,1},{1,0},{2,3},{3,2},{4,5},{5,4},{6,7},{7,6},{8,9},{9,8},{10,11... | collective-permute-start | bytes 2359304 | tf_op jit(solution)/shard_map/ppermute | solution.py:571
  3.0 1.2 %copy-done.1 = bf16[1536,256]{1,0:T(8,128)(2,1)S(1)} copy-done((bf16[1536,256]{1,0:T(8,128)(2,1)S(1)}, bf16[1536,256]{1,0:T(8,128)(2,1)}, u32[]{:S(2)}) %copy-start.1) | copy-done | bytes 786456
  4.2 0.4 cut.2
  4.6 0.7 collective-permute-start.1
  5.3 0.7 collective-permute-start.6
  6.0 7.9 %project.5 = (f32[256,6144]{1,0:T(8,128)S(1)}, f32[8,128]{1,0:T(8,128)S(1)}, bf16[1536,1024]{1,0:T(8,128)(2,1)S(1)}) custom-call(bf16[768,256]{1,0:T(8,128)(2,1)S(1)} %get-tuple-element.39.refs_0_, bf16[768,256]{1,0:T(8,128)(2,1)S(1)} %get-tuple-element.40.refs_1_, bf16[6144,6144]{1,0:T(8,128)(2,1)} %refs_2_.9), custom_call_target="tpu_custom_call" | custom-call | flops 4831838208 | bytes 19660800 | tf_op jit(solution)/shard_map/project/pallas_call | solution.py:140
  14.0 1.3 %collective-permute-start.3 = (bf16[768,256]{1,0:T(8,128)(2,1)S(1)}, bf16[768,256]{1,0:T(8,128)(2,1)S(1)}, u32[]{:S(2)}, u32[]{:S(2)}) collective-permute-start(bf16[768,256]{1,0:T(8,128)(2,1)S(1)} %gate.4.refs_0_.refs_4_), channel_id=1, source_target_pairs={{1,0},{2,3},{5,4},{6,7},{9,8},{10,11},{13,12},{14,15},{17,16},{18,... | collective-permute-start | bytes 1179656 | tf_op jit(solution)/shard_map/ppermute | solution.py:571
  15.3 5.5 %collective-permute-done.x = bf16[1536,256]{1,0:T(8,128)(2,1)S(1)} collective-permute-done((bf16[1536,256]{1,0:T(8,128)(2,1)}, bf16[1536,256]{1,0:T(8,128)(2,1)S(1)}, u32[]{:S(2)}, u32[]{:S(2)}) %collective-permute-start) | collective-permute-done | bytes 786464 | tf_op jit(solution)/shard_map/ppermute | solution.py:571
  20.8 0.4 cut.3
  21.2 0.7 collective-permute-start.4
  21.9 0.7 collective-permute-start.2
  22.6 1.3 %collective-permute-start.7 = (bf16[768,256]{1,0:T(8,128)(2,1)S(1)}, bf16[768,256]{1,0:T(8,128)(2,1)S(1)}, u32[]{:S(2)}, u32[]{:S(2)}) collective-permute-start(bf16[768,256]{1,0:T(8,128)(2,1)S(1)} %gate.7.refs_0_), channel_id=1, source_target_pairs={{1,0},{2,3},{5,4},{6,7},{9,8},{10,11},{13,12},{14,15},{17,16},{18,... | collective-permute-start | bytes 1179656 | tf_op jit(solution)/shard_map/ppermute | solution.py:571
  23.9 7.9 %project.6 = (f32[256,6144]{1,0:T(8,128)S(1)}, f32[8,128]{1,0:T(8,128)S(1)}, bf16[768,1024]{1,0:T(8,128)(2,1)S(1)}) custom-call(bf16[768,256]{1,0:T(8,128)(2,1)S(1)} %get-tuple-element.43.refs_0_.refs_1_, bf16[768,256]{1,0:T(8,128)(2,1)S(1)} %get-tuple-element.42.refs_1_, bf16[6144,6144]{1,0:T(8,128)(2,1)} %refs_2_.9, ...), custom_call_target="tpu_custom_call", output_to_operand_aliasing={{0}: (5, {})} | custom-call | flops 4831838208 | bytes 19660800 | tf_op jit(solution)/shard_map/project/pallas_call | solution.py:140
  31.8 1.3 %collective-permute-start.8 = (bf16[768,256]{1,0:T(8,128)(2,1)S(1)}, bf16[768,256]{1,0:T(8,128)(2,1)S(1)}, u32[]{:S(2)}, u32[]{:S(2)}) collective-permute-start(bf16[768,256]{1,0:T(8,128)(2,1)S(1)} %gate.5.refs_4_.refs_0_), channel_id=1, source_target_pairs={{1,0},{2,3},{5,4},{6,7},{9,8},{10,11},{13,12},{14,15},{17,16},{18,... | collective-permute-start | bytes 1179656 | tf_op jit(solution)/shard_map/ppermute | solution.py:571
  33.1 4.4 %project.7 = (f32[256,6144]{1,0:T(8,128)S(1)}, f32[8,128]{1,0:T(8,128)S(1)}, bf16[768,1024]{1,0:T(8,128)(2,1)S(1)}) custom-call(bf16[768,256]{1,0:T(8,128)(2,1)S(1)} %gate.4.refs_0_.refs_4_, bf16[768,256]{1,0:T(8,128)(2,1)S(1)} %collective-permute-done.3.refs_1_, bf16[6144,6144]{1,0:T(8,128)(2,1)} %refs_2_.9, ...), custom_call_target="tpu_custom_call", output_to_operand_aliasing={{0}: (5, {})} | custom-call | flops 2415919104 | bytes 9830400 | tf_op jit(solution)/shard_map/project/pallas_call | solution.py:140
  37.5 1.3 %collective-permute-start.5 = (bf16[768,256]{1,0:T(8,128)(2,1)S(1)}, bf16[768,256]{1,0:T(8,128)(2,1)S(1)}, u32[]{:S(2)}, u32[]{:S(2)}) collective-permute-start(bf16[768,256]{1,0:T(8,128)(2,1)S(1)} %gate.6.refs_4_.refs_0_), channel_id=1, source_target_pairs={{1,0},{2,3},{5,4},{6,7},{9,8},{10,11},{13,12},{14,15},{17,16},{18,... | collective-permute-start | bytes 1179656 | tf_op jit(solution)/shard_map/ppermute | solution.py:571
  38.8 6.8 %project.8 = (f32[256,6144]{1,0:T(8,128)S(1)}, f32[8,128]{1,0:T(8,128)S(1)}, bf16[768,1024]{1,0:T(8,128)(2,1)S(1)}, bf16[768,6144]{1,0:T(8,128)(2,1)S(1)}) custom-call(bf16[768,256]{1,0:T(8,128)(2,1)S(1)} %gate.7.refs_0_, bf16[768,256]{1,0:T(8,128)(2,1)S(1)} %collective-permute-done.7.refs_1_, ...), custom_call_target="tpu_custom_call", output_to_operand_aliasing={{0}: (5, {})} | custom-call | flops 2415919104 | bytes 9830400 | tf_op jit(solution)/shard_map/project/pallas_call | solution.py:140
  45.7 3.6 %collective-permute-done.8.refs_1_ = bf16[768,256]{1,0:T(8,128)(2,1)S(1)} collective-permute-done((bf16[768,256]{1,0:T(8,128)(2,1)S(1)}, bf16[768,256]{1,0:T(8,128)(2,1)S(1)}, u32[]{:S(2)}, u32[]{:S(2)}) %collective-permute-start.8) | collective-permute-done | bytes 393248 | tf_op jit(solution)/shard_map/ppermute | solution.py:571
  49.3 4.4 %project.9 = (f32[256,6144]{1,0:T(8,128)S(1)}, f32[8,128]{1,0:T(8,128)}) custom-call(bf16[768,256]{1,0:T(8,128)(2,1)S(1)} %gate.5.refs_4_.refs_0_, bf16[768,256]{1,0:T(8,128)(2,1)S(1)} %collective-permute-done.8.refs_1_, bf16[6144,6144]{1,0:T(8,128)(2,1)} %refs_2_.9, ...), custom_call_target="tpu_custom_call", output_to_operand_aliasing={{0}: (5, {})} | custom-call | flops 2415919104 | bytes 9830400 | tf_op jit(solution)/shard_map/project/pallas_call | solution.py:140
  53.7 1.6 %collective-permute-done.5.refs_1_ = bf16[768,256]{1,0:T(8,128)(2,1)S(1)} collective-permute-done((bf16[768,256]{1,0:T(8,128)(2,1)S(1)}, bf16[768,256]{1,0:T(8,128)(2,1)S(1)}, u32[]{:S(2)}, u32[]{:S(2)}) %collective-permute-start.5) | collective-permute-done | bytes 393248 | tf_op jit(solution)/shard_map/ppermute | solution.py:571
  55.4 2.4 %activate.2 = (bf16[256,768]{1,0:T(8,128)(2,1)S(1)}, bf16[256,3072]{1,0:T(8,128)(2,1)S(1)}, f32[8,128,128]{2,1,0:T(8,128)S(1)}) custom-call(bf16[768,256]{1,0:T(8,128)(2,1)S(1)} %gate.6.refs_4_.refs_0_, bf16[768,256]{1,0:T(8,128)(2,1)S(1)} %collective-permute-done.5.refs_1_, bf16[768,6144]{1,0:T(8,128)(2,1)S(1)} %get-tuple-element.52.refs_2_.slab, ...), custom_call_target="tpu_custom_call" | custom-call | flops 1275068416 | bytes 393216 | tf_op jit(solution)/shard_map/activate/pallas_call | solution.py:262
  57.8 0.1 collective-permute-start.9
  57.8 2.2 %activate.3 = (bf16[256,3072]{1,0:T(8,128)(2,1)S(1)}, f32[8,128,128]{2,1,0:T(8,128)S(1)}) custom-call(bf16[256,768]{1,0:T(8,128)(2,1)S(1)} %get-tuple-element.58.turned, bf16[768,6144]{1,0:T(8,128)(2,1)S(1)} %get-tuple-element.52.refs_2_.slab, f32[256,6144]{1,0:T(8,128)S(1)} %get-tuple-element.56.refs_3_.total), custom_call_target="tpu_custom_call" | custom-call | flops 1275068416 | bytes 393216 | tf_op jit(solution)/shard_map/activate/pallas_call | solution.py:271
  60.1 0.0 copy-start
  60.1 0.1 meet.9
  60.2 1.6 %collective-permute-start.13 = (bf16[4,128,128]{2,1,0:T(8,128)(2,1)S(1)}, bf16[4,128,128]{2,1,0:T(8,128)(2,1)S(1)}, u32[]{:S(2)}, u32[]{:S(2)}) collective-permute-start(bf16[4,128,128]{2,1,0:T(8,128)(2,1)S(1)} %meet.9), channel_id=1, source_target_pairs={{0,8},{4,20},{8,0},{12,28},{16,24},{20,4},{24,16},{28,12},{1,9},{5... | collective-permute-start | bytes 393224 | tf_op jit(solution)/shard_map/ppermute | solution.py:504
  61.8 0.6 collective-permute-start.10
  62.4 1.5 %within.1 = (f32[256,1024]{1,0:T(8,128)S(1)}, f32[256,1024]{1,0:T(8,128)S(1)}, f32[8,128]{1,0:T(8,128)S(1)}) custom-call(bf16[256,3072]{1,0:T(8,128)(2,1)S(1)} %get-tuple-element.57.refs_0_.act, bf16[256,3072]{1,0:T(8,128)(2,1)S(1)} %get-tuple-element.59.refs_1_.act), custom_call_target="tpu_custom_call" | custom-call | flops 536870912 | bytes 3145728 | tf_op jit(solution)/shard_map/within/pallas_call | solution.py:307
  63.9 1.3 %collective-permute-done.13.refs_2_ = bf16[4,128,128]{2,1,0:T(8,128)(2,1)S(1)} collective-permute-done((bf16[4,128,128]{2,1,0:T(8,128)(2,1)S(1)}, bf16[4,128,128]{2,1,0:T(8,128)(2,1)S(1)}, u32[]{:S(2)}, u32[]{:S(2)}) %collective-permute-start.13) | collective-permute-done | bytes 131104 | tf_op jit(solution)/shard_map/ppermute | solution.py:504
  65.2 0.1 meet.10
  65.3 0.0 copy-start.2
  65.3 1.6 %collective-permute-start.14 = (bf16[4,128,128]{2,1,0:T(8,128)(2,1)S(1)}, bf16[4,128,128]{2,1,0:T(8,128)(2,1)S(1)}, u32[]{:S(2)}, u32[]{:S(2)}) collective-permute-start(bf16[4,128,128]{2,1,0:T(8,128)(2,1)S(1)} %meet.10), channel_id=1, source_target_pairs={{0,16},{4,12},{8,24},{12,4},{16,0},{20,28},{24,8},{28,20},{1,17},{... | collective-permute-start | bytes 393224 | tf_op jit(solution)/shard_map/ppermute | solution.py:504
  66.9 0.1 meet.7
  67.0 1.5 %collective-permute-start.11 = (bf16[4,128,128]{2,1,0:T(8,128)(2,1)S(1)}, bf16[4,128,128]{2,1,0:T(8,128)(2,1)S(1)}, u32[]{:S(2)}, u32[]{:S(2)}) collective-permute-start(bf16[4,128,128]{2,1,0:T(8,128)(2,1)S(1)} %meet.7), channel_id=1, source_target_pairs={{0,16},{4,12},{8,24},{12,4},{16,0},{20,28},{24,8},{28,20},{1,17},{... | collective-permute-start | bytes 393224 | tf_op jit(solution)/shard_map/ppermute | solution.py:504
  68.5 1.8 %collective-permute-done.14.refs_3_ = bf16[4,128,128]{2,1,0:T(8,128)(2,1)S(1)} collective-permute-done((bf16[4,128,128]{2,1,0:T(8,128)(2,1)S(1)}, bf16[4,128,128]{2,1,0:T(8,128)(2,1)S(1)}, u32[]{:S(2)}, u32[]{:S(2)}) %collective-permute-start.14) | collective-permute-done | bytes 131104 | tf_op jit(solution)/shard_map/ppermute | solution.py:504
  70.3 0.1 meet.11
  70.4 0.1 collective-permute-start.15
  70.5 1.5 %collective-permute-done.11.refs_3_ = bf16[4,128,128]{2,1,0:T(8,128)(2,1)S(1)} collective-permute-done((bf16[4,128,128]{2,1,0:T(8,128)(2,1)S(1)}, bf16[4,128,128]{2,1,0:T(8,128)(2,1)S(1)}, u32[]{:S(2)}, u32[]{:S(2)}) %collective-permute-start.11) | collective-permute-done | bytes 131104 | tf_op jit(solution)/shard_map/ppermute | solution.py:504
  72.0 0.1 meet.8
  72.1 0.1 collective-permute-start.12
  72.2 0.7 across.2
  72.9 0.8 collective-permute-done.12.refs_0_
  73.7 0.7 across.3
  74.4 2.9 %collective-permute-start.16 = (f32[8,256]{1,0:T(8,128)S(1)}, f32[8,256]{1,0:T(8,128)S(1)}, u32[]{:S(2)}, u32[]{:S(2)}) collective-permute-start(f32[8,256]{1,0:T(8,128)S(1)} %get-tuple-element.72.refs_0_), channel_id=1, source_target_pairs={{0,3},{1,2},{2,1},{3,0},{4,7},{5,6},{6,5},{7,4},{8,11},{9,10},{10,... | collective-permute-start | bytes 24584 | tf_op jit(solution)/shard_map/ppermute | solution.py:430
  77.3 1.5 %collective-permute-start.18 = (f32[8,256]{1,0:T(8,128)S(1)}, f32[8,256]{1,0:T(8,128)S(1)}, u32[]{:S(2)}, u32[]{:S(2)}) collective-permute-start(f32[8,256]{1,0:T(8,128)S(1)} %get-tuple-element.72.refs_0_), channel_id=1, source_target_pairs={{0,1},{1,0},{2,3},{3,2},{4,5},{5,4},{6,7},{7,6},{8,9},{9,8},{10,11... | collective-permute-start | bytes 24584 | tf_op jit(solution)/shard_map/ppermute | solution.py:430
  78.8 1.1 %collective-permute-done.16.refs_1_ = f32[8,256]{1,0:T(8,128)S(1)} collective-permute-done((f32[8,256]{1,0:T(8,128)S(1)}, f32[8,256]{1,0:T(8,128)S(1)}, u32[]{:S(2)}, u32[]{:S(2)}) %collective-permute-start.16) | collective-permute-done | bytes 8224 | tf_op jit(solution)/shard_map/ppermute | solution.py:430
  80.0 1.9 %collective-permute-done.17.refs_2_ = f32[8,256]{1,0:T(8,128)S(1)} collective-permute-done((f32[8,256]{1,0:T(8,128)S(1)}, f32[8,256]{1,0:T(8,128)S(1)}, u32[]{:S(2)}, u32[]{:S(2)}) %collective-permute-start.17) | collective-permute-done | bytes 8224 | tf_op jit(solution)/shard_map/ppermute | solution.py:430
  81.9 1.3 %normalize.1 = bf16[256,2048]{1,0:T(8,128)(2,1)} custom-call(f32[256,1024]{1,0:T(8,128)S(1)} %get-tuple-element.70.att_other, f32[256,1024]{1,0:T(8,128)S(1)} %get-tuple-element.71.att_own, f32[1,2048]{1,0:T(1,128)S(1)} %bitcast.1, f32[8,256]{1,0:T(8,128)S(1)} %get-tuple-element.72.refs_0_, f32[8,256]{1,0:T(8,128)S(1)} %collective-permute-done.16.refs_1_, ...), custom_call_target="tpu_custom_call" | custom-call | flops 1048576 | bytes 1048576 | tf_op jit(solution)/shard_map/normalize/pallas_call | solution.py:408
  (19 shorter events, 0.1 us)
Async XLA Ops:
  0.0 20.8 %collective-permute-start = (bf16[1536,256]{1,0:T(8,128)(2,1)}, bf16[1536,256]{1,0:T(8,128)(2,1)S(1)}, u32[]{:S(2)}, u32[]{:S(2)}) collective-permute-start(bf16[1536,256]{1,0:T(8,128)(2,1)} %x.1), channel_id=1, source_target_pairs={{0,1},{1,0},{2,3},{3,2},{4,5},{5,4},{6,7},{7,6},{8,9},{9,8},{10,11... | collective-permute-start | bytes 2359304 | tf_op jit(solution)/shard_map/ppermute | solution.py:571
  3.0 1.2 %copy-start.1 = (bf16[1536,256]{1,0:T(8,128)(2,1)S(1)}, bf16[1536,256]{1,0:T(8,128)(2,1)}, u32[]{:S(2)}) copy-start(bf16[1536,256]{1,0:T(8,128)(2,1)} %x.1) | copy-start | bytes 2359300
  4.6 9.3 %collective-permute-start.1 = (bf16[768,256]{1,0:T(8,128)(2,1)S(1)}, bf16[768,256]{1,0:T(8,128)(2,1)S(1)}, u32[]{:S(2)}, u32[]{:S(2)}) collective-permute-start(bf16[768,256]{1,0:T(8,128)(2,1)S(1)} %get-tuple-element.39.refs_0_), channel_id=1, source_target_pairs={{1,2},{2,1},{5,6},{6,5},{9,10},{10,9},{13,14},{14,13},{17,18},{18,... | collective-permute-start | bytes 1179656 | tf_op jit(solution)/shard_map/ppermute | solution.py:571
  5.3 17.3 %collective-permute-start.6 = (bf16[768,256]{1,0:T(8,128)(2,1)S(1)}, bf16[768,256]{1,0:T(8,128)(2,1)S(1)}, u32[]{:S(2)}, u32[]{:S(2)}) collective-permute-start(bf16[768,256]{1,0:T(8,128)(2,1)S(1)} %get-tuple-element.40.refs_1_), channel_id=1, source_target_pairs={{1,2},{2,1},{5,6},{6,5},{9,10},{10,9},{13,14},{14,13},{17,18},{18,... | collective-permute-start | bytes 1179656 | tf_op jit(solution)/shard_map/ppermute | solution.py:571
  14.0 19.1 %collective-permute-start.3 = (bf16[768,256]{1,0:T(8,128)(2,1)S(1)}, bf16[768,256]{1,0:T(8,128)(2,1)S(1)}, u32[]{:S(2)}, u32[]{:S(2)}) collective-permute-start(bf16[768,256]{1,0:T(8,128)(2,1)S(1)} %gate.4.refs_0_.refs_4_), channel_id=1, source_target_pairs={{1,0},{2,3},{5,4},{6,7},{9,8},{10,11},{13,12},{14,15},{17,16},{18,... | collective-permute-start | bytes 1179656 | tf_op jit(solution)/shard_map/ppermute | solution.py:571
  21.2 10.6 %collective-permute-start.4 = (bf16[768,256]{1,0:T(8,128)(2,1)S(1)}, bf16[768,256]{1,0:T(8,128)(2,1)S(1)}, u32[]{:S(2)}, u32[]{:S(2)}) collective-permute-start(bf16[768,256]{1,0:T(8,128)(2,1)S(1)} %get-tuple-element.43.refs_0_.refs_1_), channel_id=1, source_target_pairs={{1,2},{2,1},{5,6},{6,5},{9,10},{10,9},{13,14},{14,13},{17,18},{18,... | collective-permute-start | bytes 1179656 | tf_op jit(solution)/shard_map/ppermute | solution.py:571
  21.9 15.7 %collective-permute-start.2 = (bf16[768,256]{1,0:T(8,128)(2,1)S(1)}, bf16[768,256]{1,0:T(8,128)(2,1)S(1)}, u32[]{:S(2)}, u32[]{:S(2)}) collective-permute-start(bf16[768,256]{1,0:T(8,128)(2,1)S(1)} %get-tuple-element.42.refs_1_), channel_id=1, source_target_pairs={{1,2},{2,1},{5,6},{6,5},{9,10},{10,9},{13,14},{14,13},{17,18},{18,... | collective-permute-start | bytes 1179656 | tf_op jit(solution)/shard_map/ppermute | solution.py:571
  22.6 16.3 %collective-permute-start.7 = (bf16[768,256]{1,0:T(8,128)(2,1)S(1)}, bf16[768,256]{1,0:T(8,128)(2,1)S(1)}, u32[]{:S(2)}, u32[]{:S(2)}) collective-permute-start(bf16[768,256]{1,0:T(8,128)(2,1)S(1)} %gate.7.refs_0_), channel_id=1, source_target_pairs={{1,0},{2,3},{5,4},{6,7},{9,8},{10,11},{13,12},{14,15},{17,16},{18,... | collective-permute-start | bytes 1179656 | tf_op jit(solution)/shard_map/ppermute | solution.py:571
  31.8 17.5 %collective-permute-start.8 = (bf16[768,256]{1,0:T(8,128)(2,1)S(1)}, bf16[768,256]{1,0:T(8,128)(2,1)S(1)}, u32[]{:S(2)}, u32[]{:S(2)}) collective-permute-start(bf16[768,256]{1,0:T(8,128)(2,1)S(1)} %gate.5.refs_4_.refs_0_), channel_id=1, source_target_pairs={{1,0},{2,3},{5,4},{6,7},{9,8},{10,11},{13,12},{14,15},{17,16},{18,... | collective-permute-start | bytes 1179656 | tf_op jit(solution)/shard_map/ppermute | solution.py:571
  37.5 17.8 %collective-permute-start.5 = (bf16[768,256]{1,0:T(8,128)(2,1)S(1)}, bf16[768,256]{1,0:T(8,128)(2,1)S(1)}, u32[]{:S(2)}, u32[]{:S(2)}) collective-permute-start(bf16[768,256]{1,0:T(8,128)(2,1)S(1)} %gate.6.refs_4_.refs_0_), channel_id=1, source_target_pairs={{1,0},{2,3},{5,4},{6,7},{9,8},{10,11},{13,12},{14,15},{17,16},{18,... | collective-permute-start | bytes 1179656 | tf_op jit(solution)/shard_map/ppermute | solution.py:571
  57.8 2.3 %collective-permute-start.9 = (f32[8,128,128]{2,1,0:T(8,128)S(1)}, f32[8,128,128]{2,1,0:T(8,128)S(1)}, u32[]{:S(2)}, u32[]{:S(2)}) collective-permute-start(f32[8,128,128]{2,1,0:T(8,128)S(1)} %get-tuple-element.62), channel_id=1, source_target_pairs={{0,4},{4,0},{8,12},{12,8},{16,20},{20,16},{24,28},{28,24},{1,5},{5... | collective-permute-start | bytes 1572872 | tf_op jit(solution)/shard_map/ppermute | solution.py:490
  60.1 12.1 %copy-start = (f32[16,128,128]{2,1,0:T(8,128)S(1)}, f32[16,128,128]{2,1,0:T(8,128)}, u32[]{:S(2)}) copy-start(f32[16,128,128]{2,1,0:T(8,128)} %prior.3) | copy-start | bytes 3145732
  60.2 5.0 %collective-permute-start.13 = (bf16[4,128,128]{2,1,0:T(8,128)(2,1)S(1)}, bf16[4,128,128]{2,1,0:T(8,128)(2,1)S(1)}, u32[]{:S(2)}, u32[]{:S(2)}) collective-permute-start(bf16[4,128,128]{2,1,0:T(8,128)(2,1)S(1)} %meet.9), channel_id=1, source_target_pairs={{0,8},{4,20},{8,0},{12,28},{16,24},{20,4},{24,16},{28,12},{1,9},{5... | collective-permute-start | bytes 393224 | tf_op jit(solution)/shard_map/ppermute | solution.py:504
  61.8 5.1 %collective-permute-start.10 = (bf16[4,128,128]{2,1,0:T(8,128)(2,1)S(1)}, bf16[4,128,128]{2,1,0:T(8,128)(2,1)S(1)}, u32[]{:S(2)}, u32[]{:S(2)}) collective-permute-start(bf16[4,128,128]{2,1,0:T(8,128)(2,1)S(1)} %meet.6), channel_id=1, source_target_pairs={{0,8},{4,20},{8,0},{12,28},{16,24},{20,4},{24,16},{28,12},{1,9},{5... | collective-permute-start | bytes 393224 | tf_op jit(solution)/shard_map/ppermute | solution.py:504
  65.3 16.6 %copy-start.2 = (f32[2048]{0:T(1024)S(1)}, f32[2048]{0:T(1024)}, u32[]{:S(2)}) copy-start(f32[2048]{0:T(1024)} %param.7) | copy-start | bytes 24580
  65.3 5.0 %collective-permute-start.14 = (bf16[4,128,128]{2,1,0:T(8,128)(2,1)S(1)}, bf16[4,128,128]{2,1,0:T(8,128)(2,1)S(1)}, u32[]{:S(2)}, u32[]{:S(2)}) collective-permute-start(bf16[4,128,128]{2,1,0:T(8,128)(2,1)S(1)} %meet.10), channel_id=1, source_target_pairs={{0,16},{4,12},{8,24},{12,4},{16,0},{20,28},{24,8},{28,20},{1,17},{... | collective-permute-start | bytes 393224 | tf_op jit(solution)/shard_map/ppermute | solution.py:504
  67.0 5.0 %collective-permute-start.11 = (bf16[4,128,128]{2,1,0:T(8,128)(2,1)S(1)}, bf16[4,128,128]{2,1,0:T(8,128)(2,1)S(1)}, u32[]{:S(2)}, u32[]{:S(2)}) collective-permute-start(bf16[4,128,128]{2,1,0:T(8,128)(2,1)S(1)} %meet.7), channel_id=1, source_target_pairs={{0,16},{4,12},{8,24},{12,4},{16,0},{20,28},{24,8},{28,20},{1,17},{... | collective-permute-start | bytes 393224 | tf_op jit(solution)/shard_map/ppermute | solution.py:504
  70.4 2.5 %collective-permute-start.15 = (f32[4,128,128]{2,1,0:T(8,128)S(1)}, f32[4,128,128]{2,1,0:T(8,128)S(1)}, u32[]{:S(2)}, u32[]{:S(2)}) collective-permute-start(f32[4,128,128]{2,1,0:T(8,128)S(1)} %get-tuple-element.65), channel_id=1, source_target_pairs={{0,4},{4,0},{8,12},{12,8},{16,20},{20,16},{24,28},{28,24},{1,5},{5... | collective-permute-start | bytes 786440 | tf_op jit(solution)/shard_map/ppermute | solution.py:508
  72.1 1.6 %collective-permute-start.12 = (f32[4,128,128]{2,1,0:T(8,128)S(1)}, f32[4,128,128]{2,1,0:T(8,128)S(1)}, u32[]{:S(2)}, u32[]{:S(2)}) collective-permute-start(f32[4,128,128]{2,1,0:T(8,128)S(1)} %get-tuple-element.64), channel_id=1, source_target_pairs={{0,4},{4,0},{8,12},{12,8},{16,20},{20,16},{24,28},{28,24},{1,5},{5... | collective-permute-start | bytes 786440 | tf_op jit(solution)/shard_map/ppermute | solution.py:508
  74.4 5.5 %collective-permute-start.16 = (f32[8,256]{1,0:T(8,128)S(1)}, f32[8,256]{1,0:T(8,128)S(1)}, u32[]{:S(2)}, u32[]{:S(2)}) collective-permute-start(f32[8,256]{1,0:T(8,128)S(1)} %get-tuple-element.72.refs_0_), channel_id=1, source_target_pairs={{0,3},{1,2},{2,1},{3,0},{4,7},{5,6},{6,5},{7,4},{8,11},{9,10},{10,... | collective-permute-start | bytes 24584 | tf_op jit(solution)/shard_map/ppermute | solution.py:430
  77.3 4.5 %collective-permute-start.17 = (f32[8,256]{1,0:T(8,128)S(1)}, f32[8,256]{1,0:T(8,128)S(1)}, u32[]{:S(2)}, u32[]{:S(2)}) collective-permute-start(f32[8,256]{1,0:T(8,128)S(1)} %get-tuple-element.72.refs_0_), channel_id=1, source_target_pairs={{0,2},{1,3},{2,0},{3,1},{4,6},{5,7},{6,4},{7,5},{8,10},{9,11},{10,... | collective-permute-start | bytes 24584 | tf_op jit(solution)/shard_map/ppermute | solution.py:430
  77.3 4.5 %collective-permute-start.18 = (f32[8,256]{1,0:T(8,128)S(1)}, f32[8,256]{1,0:T(8,128)S(1)}, u32[]{:S(2)}, u32[]{:S(2)}) collective-permute-start(f32[8,256]{1,0:T(8,128)S(1)} %get-tuple-element.72.refs_0_), channel_id=1, source_target_pairs={{0,1},{1,0},{2,3},{3,2},{4,5},{5,4},{6,7},{7,6},{8,9},{9,8},{10,11... | collective-permute-start | bytes 24584 | tf_op jit(solution)/shard_map/ppermute | solution.py:430

commit v7 on v6

--- a/solution.py
+++ b/solution.py
@@ -532,7 +532,7 @@
 
     pairs, arrivals = hops(n_tensor)
     last = n_tensor - 2
-    pieces = cut_in_two(tokens_t, early)
+    pieces = [tokens_t[:early], tokens_t[early:]]
     held = [[tokens_t], pieces]
     came = {}
 

time: 83.6 us -> 83.6 us (level)
    unnamed x6 -> x4, local copies, waits for them, and re-layouts: 1.18 us -> 0.01 us
    slice x0 -> x1, local copies, waits for them, and re-layouts: none -> 1.17 us  [body(): pieces = [tokens_t[:early], tokens_t[early:]]]
  transfers between devices with their start and end apart: 19 -> 19, of which waited for: 9 -> 9; matrix products, arithmetic and copies ran while one was open for 0% -> 1% of each run, Pallas kernels for 45% -> 44%
where the time goes in v7:
time: 83.6 us; the launch traced here: 83.3 us
  Pallas kernels  41.1 us (49%)
  starting transfers between devices  20.8 us (25%)
  waiting for transfers between devices  19.7 us (24%)
  local copies, waits for them, and re-layouts  1.18 us (1%)
    pallas_call x5, Pallas kernels, project(): pl.pallas_call(functools.partial(project_kernel, counts, first, picks, we...  31.5 us
    ppermute x9, waiting for transfers between devices, body(): lax.ppermute(x, 'tensor', pairs[chain][t])  11.2 us
    ppermute x9, starting transfers between devices, body(): lax.ppermute(x, 'tensor', pairs[chain][t])  10.9 us
    ppermute x4, starting transfers between devices, earlier_states(): gots[g] = gots[g] + [lax.ppermute(message, 'context', pairs)]  5.25 us
    ppermute x4, waiting for transfers between devices, earlier_states(): gots[g] = gots[g] + [lax.ppermute(message, 'context', pairs)]  4.7 us
    ppermute x3, starting transfers between devices, terms_over_tensor(): lax.ppermute(x, 'tensor', [(i, i ^ d) for i in range(n)])  4.42 us
    ppermute x3, waiting for transfers between devices, terms_over_tensor(): lax.ppermute(x, 'tensor', [(i, i ^ d) for i in range(n)])  3.03 us
    pallas_call x1, Pallas kernels, activate(): pl.pallas_call(functools.partial(first_kernel, len(choices), width, picks...  2.36 us
  transfers between devices with their start and end apart: 19, of which 9 were waited for; matrix products, arithmetic and copies ran while one was open for 1% of the time, Pallas kernels for 44%

profile of v7, /device:TPU:0, one launch (start us, length us, event | category | flops | bytes accessed | tf_op | source)
XLA Modules:
  0.0 83.3 jit_solution(10765288103882584073)
XLA Ops:
  0.0 3.0 %collective-permute-start = (bf16[1536,256]{1,0:T(8,128)(2,1)}, bf16[1536,256]{1,0:T(8,128)(2,1)S(1)}, u32[]{:S(2)}, u32[]{:S(2)}) collective-permute-start(bf16[1536,256]{1,0:T(8,128)(2,1)} %param.4), channel_id=1, source_target_pairs={{0,1},{1,0},{2,3},{3,2},{4,5},{5,4},{6,7},{7,6},{8,9},{9,8},{10,11... | collective-permute-start | bytes 2359304 | tf_op jit(solution)/shard_map/ppermute | solution.py:571
  3.0 1.2 %fusion = (bf16[768,256]{1,0:T(8,128)(2,1)S(1)}, bf16[768,256]{1,0:T(8,128)(2,1)S(1)}) fusion(bf16[1536,256]{1,0:T(8,128)(2,1)} %param.4), kind=kLoop, calls=%fused_computation | loop fusion | bytes 1572864 | tf_op jit(solution)/shard_map/slice | solution.py:535
  4.2 0.7 collective-permute-start.1
  4.9 0.7 collective-permute-start.6
  5.6 7.9 %project.5 = (f32[256,6144]{1,0:T(8,128)S(1)}, f32[8,128]{1,0:T(8,128)S(1)}, bf16[1536,1024]{1,0:T(8,128)(2,1)S(1)}) custom-call(bf16[768,256]{1,0:T(8,128)(2,1)S(1)} %get-tuple-element.70.refs_0_, bf16[768,256]{1,0:T(8,128)(2,1)S(1)} %get-tuple-element.69.refs_1_, bf16[6144,6144]{1,0:T(8,128)(2,1)} %refs_2_.9), custom_call_target="tpu_custom_call" | custom-call | flops 4831838208 | bytes 19660800 | tf_op jit(solution)/shard_map/project/pallas_call | solution.py:140
  13.5 0.0 collective-permute-done.1.refs_0_
  13.6 1.3 %collective-permute-start.3 = (bf16[768,256]{1,0:T(8,128)(2,1)S(1)}, bf16[768,256]{1,0:T(8,128)(2,1)S(1)}, u32[]{:S(2)}, u32[]{:S(2)}) collective-permute-start(bf16[768,256]{1,0:T(8,128)(2,1)S(1)} %gate.4.refs_0_.refs_4_), channel_id=1, source_target_pairs={{1,0},{2,3},{5,4},{6,7},{9,8},{10,11},{13,12},{14,15},{17,16},{18,... | collective-permute-start | bytes 1179656 | tf_op jit(solution)/shard_map/ppermute | solution.py:571
  14.9 6.1 %collective-permute-done.x = bf16[1536,256]{1,0:T(8,128)(2,1)S(1)} collective-permute-done((bf16[1536,256]{1,0:T(8,128)(2,1)}, bf16[1536,256]{1,0:T(8,128)(2,1)S(1)}, u32[]{:S(2)}, u32[]{:S(2)}) %collective-permute-start) | collective-permute-done | bytes 786464 | tf_op jit(solution)/shard_map/ppermute | solution.py:571
  20.9 0.4 cut.1
  21.3 0.7 collective-permute-start.4
  22.0 0.7 collective-permute-start.2
  22.7 1.3 %collective-permute-start.7 = (bf16[768,256]{1,0:T(8,128)(2,1)S(1)}, bf16[768,256]{1,0:T(8,128)(2,1)S(1)}, u32[]{:S(2)}, u32[]{:S(2)}) collective-permute-start(bf16[768,256]{1,0:T(8,128)(2,1)S(1)} %gate.7.refs_0_), channel_id=1, source_target_pairs={{1,0},{2,3},{5,4},{6,7},{9,8},{10,11},{13,12},{14,15},{17,16},{18,... | collective-permute-start | bytes 1179656 | tf_op jit(solution)/shard_map/ppermute | solution.py:571
  24.0 7.9 %project.6 = (f32[256,6144]{1,0:T(8,128)S(1)}, f32[8,128]{1,0:T(8,128)S(1)}, bf16[768,1024]{1,0:T(8,128)(2,1)S(1)}) custom-call(bf16[768,256]{1,0:T(8,128)(2,1)S(1)} %get-tuple-element.39.refs_0_.refs_1_, bf16[768,256]{1,0:T(8,128)(2,1)S(1)} %get-tuple-element.38.refs_1_, bf16[6144,6144]{1,0:T(8,128)(2,1)} %refs_2_.9, ...), custom_call_target="tpu_custom_call", output_to_operand_aliasing={{0}: (5, {})} | custom-call | flops 4831838208 | bytes 19660800 | tf_op jit(solution)/shard_map/project/pallas_call | solution.py:140
  31.9 1.3 %collective-permute-start.8 = (bf16[768,256]{1,0:T(8,128)(2,1)S(1)}, bf16[768,256]{1,0:T(8,128)(2,1)S(1)}, u32[]{:S(2)}, u32[]{:S(2)}) collective-permute-start(bf16[768,256]{1,0:T(8,128)(2,1)S(1)} %gate.5.refs_4_.refs_0_), channel_id=1, source_target_pairs={{1,0},{2,3},{5,4},{6,7},{9,8},{10,11},{13,12},{14,15},{17,16},{18,... | collective-permute-start | bytes 1179656 | tf_op jit(solution)/shard_map/ppermute | solution.py:571
  33.2 4.4 %project.7 = (f32[256,6144]{1,0:T(8,128)S(1)}, f32[8,128]{1,0:T(8,128)S(1)}, bf16[768,1024]{1,0:T(8,128)(2,1)S(1)}) custom-call(bf16[768,256]{1,0:T(8,128)(2,1)S(1)} %gate.4.refs_0_.refs_4_, bf16[768,256]{1,0:T(8,128)(2,1)S(1)} %collective-permute-done.3.refs_1_, bf16[6144,6144]{1,0:T(8,128)(2,1)} %refs_2_.9, ...), custom_call_target="tpu_custom_call", output_to_operand_aliasing={{0}: (5, {})} | custom-call | flops 2415919104 | bytes 9830400 | tf_op jit(solution)/shard_map/project/pallas_call | solution.py:140
  37.7 1.3 %collective-permute-start.5 = (bf16[768,256]{1,0:T(8,128)(2,1)S(1)}, bf16[768,256]{1,0:T(8,128)(2,1)S(1)}, u32[]{:S(2)}, u32[]{:S(2)}) collective-permute-start(bf16[768,256]{1,0:T(8,128)(2,1)S(1)} %gate.6.refs_4_.refs_0_), channel_id=1, source_target_pairs={{1,0},{2,3},{5,4},{6,7},{9,8},{10,11},{13,12},{14,15},{17,16},{18,... | collective-permute-start | bytes 1179656 | tf_op jit(solution)/shard_map/ppermute | solution.py:571
  39.0 6.8 %project.8 = (f32[256,6144]{1,0:T(8,128)S(1)}, f32[8,128]{1,0:T(8,128)S(1)}, bf16[768,1024]{1,0:T(8,128)(2,1)S(1)}, bf16[768,6144]{1,0:T(8,128)(2,1)S(1)}) custom-call(bf16[768,256]{1,0:T(8,128)(2,1)S(1)} %gate.7.refs_0_, bf16[768,256]{1,0:T(8,128)(2,1)S(1)} %collective-permute-done.7.refs_1_, ...), custom_call_target="tpu_custom_call", output_to_operand_aliasing={{0}: (5, {})} | custom-call | flops 2415919104 | bytes 9830400 | tf_op jit(solution)/shard_map/project/pallas_call | solution.py:140
  45.8 3.5 %collective-permute-done.8.refs_1_ = bf16[768,256]{1,0:T(8,128)(2,1)S(1)} collective-permute-done((bf16[768,256]{1,0:T(8,128)(2,1)S(1)}, bf16[768,256]{1,0:T(8,128)(2,1)S(1)}, u32[]{:S(2)}, u32[]{:S(2)}) %collective-permute-start.8) | collective-permute-done | bytes 393248 | tf_op jit(solution)/shard_map/ppermute | solution.py:571
  49.3 4.4 %project.9 = (f32[256,6144]{1,0:T(8,128)S(1)}, f32[8,128]{1,0:T(8,128)}) custom-call(bf16[768,256]{1,0:T(8,128)(2,1)S(1)} %gate.5.refs_4_.refs_0_, bf16[768,256]{1,0:T(8,128)(2,1)S(1)} %collective-permute-done.8.refs_1_, bf16[6144,6144]{1,0:T(8,128)(2,1)} %refs_2_.9, ...), custom_call_target="tpu_custom_call", output_to_operand_aliasing={{0}: (5, {})} | custom-call | flops 2415919104 | bytes 9830400 | tf_op jit(solution)/shard_map/project/pallas_call | solution.py:140
  53.7 1.6 %collective-permute-done.5.refs_1_ = bf16[768,256]{1,0:T(8,128)(2,1)S(1)} collective-permute-done((bf16[768,256]{1,0:T(8,128)(2,1)S(1)}, bf16[768,256]{1,0:T(8,128)(2,1)S(1)}, u32[]{:S(2)}, u32[]{:S(2)}) %collective-permute-start.5) | collective-permute-done | bytes 393248 | tf_op jit(solution)/shard_map/ppermute | solution.py:571
  55.4 2.4 %activate.2 = (bf16[256,768]{1,0:T(8,128)(2,1)S(1)}, bf16[256,3072]{1,0:T(8,128)(2,1)S(1)}, f32[8,128,128]{2,1,0:T(8,128)S(1)}) custom-call(bf16[768,256]{1,0:T(8,128)(2,1)S(1)} %gate.6.refs_4_.refs_0_, bf16[768,256]{1,0:T(8,128)(2,1)S(1)} %collective-permute-done.5.refs_1_, bf16[768,6144]{1,0:T(8,128)(2,1)S(1)} %get-tuple-element.48.refs_2_.slab, ...), custom_call_target="tpu_custom_call" | custom-call | flops 1275068416 | bytes 393216 | tf_op jit(solution)/shard_map/activate/pallas_call | solution.py:262
  57.8 0.1 collective-permute-start.9
  57.8 2.2 %activate.3 = (bf16[256,3072]{1,0:T(8,128)(2,1)S(1)}, f32[8,128,128]{2,1,0:T(8,128)S(1)}) custom-call(bf16[256,768]{1,0:T(8,128)(2,1)S(1)} %get-tuple-element.54.turned, bf16[768,6144]{1,0:T(8,128)(2,1)S(1)} %get-tuple-element.48.refs_2_.slab, f32[256,6144]{1,0:T(8,128)S(1)} %get-tuple-element.52.refs_3_.total), custom_call_target="tpu_custom_call" | custom-call | flops 1275068416 | bytes 393216 | tf_op jit(solution)/shard_map/activate/pallas_call | solution.py:271
  60.1 0.0 copy-start
  60.1 0.1 meet.9
  60.2 1.6 %collective-permute-start.13 = (bf16[4,128,128]{2,1,0:T(8,128)(2,1)S(1)}, bf16[4,128,128]{2,1,0:T(8,128)(2,1)S(1)}, u32[]{:S(2)}, u32[]{:S(2)}) collective-permute-start(bf16[4,128,128]{2,1,0:T(8,128)(2,1)S(1)} %meet.9), channel_id=1, source_target_pairs={{0,8},{4,20},{8,0},{12,28},{16,24},{20,4},{24,16},{28,12},{1,9},{5... | collective-permute-start | bytes 393224 | tf_op jit(solution)/shard_map/ppermute | solution.py:504
  61.8 0.6 collective-permute-start.10
  62.4 1.5 %within.1 = (f32[256,1024]{1,0:T(8,128)S(1)}, f32[256,1024]{1,0:T(8,128)S(1)}, f32[8,128]{1,0:T(8,128)S(1)}) custom-call(bf16[256,3072]{1,0:T(8,128)(2,1)S(1)} %get-tuple-element.53.refs_0_.act, bf16[256,3072]{1,0:T(8,128)(2,1)S(1)} %get-tuple-element.55.refs_1_.act), custom_call_target="tpu_custom_call" | custom-call | flops 536870912 | bytes 3145728 | tf_op jit(solution)/shard_map/within/pallas_call | solution.py:307
  63.9 1.3 %collective-permute-done.13.refs_2_ = bf16[4,128,128]{2,1,0:T(8,128)(2,1)S(1)} collective-permute-done((bf16[4,128,128]{2,1,0:T(8,128)(2,1)S(1)}, bf16[4,128,128]{2,1,0:T(8,128)(2,1)S(1)}, u32[]{:S(2)}, u32[]{:S(2)}) %collective-permute-start.13) | collective-permute-done | bytes 131104 | tf_op jit(solution)/shard_map/ppermute | solution.py:504
  65.2 0.1 meet.10
  65.3 0.0 copy-start.1
  65.3 1.6 %collective-permute-start.14 = (bf16[4,128,128]{2,1,0:T(8,128)(2,1)S(1)}, bf16[4,128,128]{2,1,0:T(8,128)(2,1)S(1)}, u32[]{:S(2)}, u32[]{:S(2)}) collective-permute-start(bf16[4,128,128]{2,1,0:T(8,128)(2,1)S(1)} %meet.10), channel_id=1, source_target_pairs={{0,16},{4,12},{8,24},{12,4},{16,0},{20,28},{24,8},{28,20},{1,17},{... | collective-permute-start | bytes 393224 | tf_op jit(solution)/shard_map/ppermute | solution.py:504
  66.9 0.1 meet.7
  67.0 1.5 %collective-permute-start.11 = (bf16[4,128,128]{2,1,0:T(8,128)(2,1)S(1)}, bf16[4,128,128]{2,1,0:T(8,128)(2,1)S(1)}, u32[]{:S(2)}, u32[]{:S(2)}) collective-permute-start(bf16[4,128,128]{2,1,0:T(8,128)(2,1)S(1)} %meet.7), channel_id=1, source_target_pairs={{0,16},{4,12},{8,24},{12,4},{16,0},{20,28},{24,8},{28,20},{1,17},{... | collective-permute-start | bytes 393224 | tf_op jit(solution)/shard_map/ppermute | solution.py:504
  68.5 1.8 %collective-permute-done.14.refs_3_ = bf16[4,128,128]{2,1,0:T(8,128)(2,1)S(1)} collective-permute-done((bf16[4,128,128]{2,1,0:T(8,128)(2,1)S(1)}, bf16[4,128,128]{2,1,0:T(8,128)(2,1)S(1)}, u32[]{:S(2)}, u32[]{:S(2)}) %collective-permute-start.14) | collective-permute-done | bytes 131104 | tf_op jit(solution)/shard_map/ppermute | solution.py:504
  70.3 0.1 meet.11
  70.4 0.1 collective-permute-start.15
  70.5 1.5 %collective-permute-done.11.refs_3_ = bf16[4,128,128]{2,1,0:T(8,128)(2,1)S(1)} collective-permute-done((bf16[4,128,128]{2,1,0:T(8,128)(2,1)S(1)}, bf16[4,128,128]{2,1,0:T(8,128)(2,1)S(1)}, u32[]{:S(2)}, u32[]{:S(2)}) %collective-permute-start.11) | collective-permute-done | bytes 131104 | tf_op jit(solution)/shard_map/ppermute | solution.py:504
  72.0 0.1 meet.8
  72.1 0.1 collective-permute-start.12
  72.2 0.7 across.2
  72.9 0.8 collective-permute-done.12.refs_0_
  73.7 0.7 across.3
  74.4 2.9 %collective-permute-start.16 = (f32[8,256]{1,0:T(8,128)S(1)}, f32[8,256]{1,0:T(8,128)S(1)}, u32[]{:S(2)}, u32[]{:S(2)}) collective-permute-start(f32[8,256]{1,0:T(8,128)S(1)} %get-tuple-element.68.refs_0_), channel_id=1, source_target_pairs={{0,3},{1,2},{2,1},{3,0},{4,7},{5,6},{6,5},{7,4},{8,11},{9,10},{10,... | collective-permute-start | bytes 24584 | tf_op jit(solution)/shard_map/ppermute | solution.py:430
  77.3 1.5 %collective-permute-start.18 = (f32[8,256]{1,0:T(8,128)S(1)}, f32[8,256]{1,0:T(8,128)S(1)}, u32[]{:S(2)}, u32[]{:S(2)}) collective-permute-start(f32[8,256]{1,0:T(8,128)S(1)} %get-tuple-element.68.refs_0_), channel_id=1, source_target_pairs={{0,1},{1,0},{2,3},{3,2},{4,5},{5,4},{6,7},{7,6},{8,9},{9,8},{10,11... | collective-permute-start | bytes 24584 | tf_op jit(solution)/shard_map/ppermute | solution.py:430
  78.8 1.1 %collective-permute-done.16.refs_1_ = f32[8,256]{1,0:T(8,128)S(1)} collective-permute-done((f32[8,256]{1,0:T(8,128)S(1)}, f32[8,256]{1,0:T(8,128)S(1)}, u32[]{:S(2)}, u32[]{:S(2)}) %collective-permute-start.16) | collective-permute-done | bytes 8224 | tf_op jit(solution)/shard_map/ppermute | solution.py:430
  79.9 1.9 %collective-permute-done.17.refs_2_ = f32[8,256]{1,0:T(8,128)S(1)} collective-permute-done((f32[8,256]{1,0:T(8,128)S(1)}, f32[8,256]{1,0:T(8,128)S(1)}, u32[]{:S(2)}, u32[]{:S(2)}) %collective-permute-start.17) | collective-permute-done | bytes 8224 | tf_op jit(solution)/shard_map/ppermute | solution.py:430
  81.9 1.3 %normalize.1 = bf16[256,2048]{1,0:T(8,128)(2,1)} custom-call(f32[256,1024]{1,0:T(8,128)S(1)} %get-tuple-element.66.att_other, f32[256,1024]{1,0:T(8,128)S(1)} %get-tuple-element.67.att_own, f32[1,2048]{1,0:T(1,128)S(1)} %bitcast.1, f32[8,256]{1,0:T(8,128)S(1)} %get-tuple-element.68.refs_0_, f32[8,256]{1,0:T(8,128)S(1)} %collective-permute-done.16.refs_1_, ...), custom_call_target="tpu_custom_call" | custom-call | flops 1048576 | bytes 1048576 | tf_op jit(solution)/shard_map/normalize/pallas_call | solution.py:408
  (17 shorter events, 0.1 us)
Async XLA Ops:
  0.0 20.9 %collective-permute-start = (bf16[1536,256]{1,0:T(8,128)(2,1)}, bf16[1536,256]{1,0:T(8,128)(2,1)S(1)}, u32[]{:S(2)}, u32[]{:S(2)}) collective-permute-start(bf16[1536,256]{1,0:T(8,128)(2,1)} %param.4), channel_id=1, source_target_pairs={{0,1},{1,0},{2,3},{3,2},{4,5},{5,4},{6,7},{7,6},{8,9},{9,8},{10,11... | collective-permute-start | bytes 2359304 | tf_op jit(solution)/shard_map/ppermute | solution.py:571
  4.2 9.3 %collective-permute-start.1 = (bf16[768,256]{1,0:T(8,128)(2,1)S(1)}, bf16[768,256]{1,0:T(8,128)(2,1)S(1)}, u32[]{:S(2)}, u32[]{:S(2)}) collective-permute-start(bf16[768,256]{1,0:T(8,128)(2,1)S(1)} %get-tuple-element.70.refs_0_), channel_id=1, source_target_pairs={{1,2},{2,1},{5,6},{6,5},{9,10},{10,9},{13,14},{14,13},{17,18},{18,... | collective-permute-start | bytes 1179656 | tf_op jit(solution)/shard_map/ppermute | solution.py:571
  4.9 17.8 %collective-permute-start.6 = (bf16[768,256]{1,0:T(8,128)(2,1)S(1)}, bf16[768,256]{1,0:T(8,128)(2,1)S(1)}, u32[]{:S(2)}, u32[]{:S(2)}) collective-permute-start(bf16[768,256]{1,0:T(8,128)(2,1)S(1)} %get-tuple-element.69.refs_1_), channel_id=1, source_target_pairs={{1,2},{2,1},{5,6},{6,5},{9,10},{10,9},{13,14},{14,13},{17,18},{18,... | collective-permute-start | bytes 1179656 | tf_op jit(solution)/shard_map/ppermute | solution.py:571
  13.6 19.6 %collective-permute-start.3 = (bf16[768,256]{1,0:T(8,128)(2,1)S(1)}, bf16[768,256]{1,0:T(8,128)(2,1)S(1)}, u32[]{:S(2)}, u32[]{:S(2)}) collective-permute-start(bf16[768,256]{1,0:T(8,128)(2,1)S(1)} %gate.4.refs_0_.refs_4_), channel_id=1, source_target_pairs={{1,0},{2,3},{5,4},{6,7},{9,8},{10,11},{13,12},{14,15},{17,16},{18,... | collective-permute-start | bytes 1179656 | tf_op jit(solution)/shard_map/ppermute | solution.py:571
  21.3 10.6 %collective-permute-start.4 = (bf16[768,256]{1,0:T(8,128)(2,1)S(1)}, bf16[768,256]{1,0:T(8,128)(2,1)S(1)}, u32[]{:S(2)}, u32[]{:S(2)}) collective-permute-start(bf16[768,256]{1,0:T(8,128)(2,1)S(1)} %get-tuple-element.39.refs_0_.refs_1_), channel_id=1, source_target_pairs={{1,2},{2,1},{5,6},{6,5},{9,10},{10,9},{13,14},{14,13},{17,18},{18,... | collective-permute-start | bytes 1179656 | tf_op jit(solution)/shard_map/ppermute | solution.py:571
  22.0 15.7 %collective-permute-start.2 = (bf16[768,256]{1,0:T(8,128)(2,1)S(1)}, bf16[768,256]{1,0:T(8,128)(2,1)S(1)}, u32[]{:S(2)}, u32[]{:S(2)}) collective-permute-start(bf16[768,256]{1,0:T(8,128)(2,1)S(1)} %get-tuple-element.38.refs_1_), channel_id=1, source_target_pairs={{1,2},{2,1},{5,6},{6,5},{9,10},{10,9},{13,14},{14,13},{17,18},{18,... | collective-permute-start | bytes 1179656 | tf_op jit(solution)/shard_map/ppermute | solution.py:571
  22.7 16.3 %collective-permute-start.7 = (bf16[768,256]{1,0:T(8,128)(2,1)S(1)}, bf16[768,256]{1,0:T(8,128)(2,1)S(1)}, u32[]{:S(2)}, u32[]{:S(2)}) collective-permute-start(bf16[768,256]{1,0:T(8,128)(2,1)S(1)} %gate.7.refs_0_), channel_id=1, source_target_pairs={{1,0},{2,3},{5,4},{6,7},{9,8},{10,11},{13,12},{14,15},{17,16},{18,... | collective-permute-start | bytes 1179656 | tf_op jit(solution)/shard_map/ppermute | solution.py:571
  31.9 17.4 %collective-permute-start.8 = (bf16[768,256]{1,0:T(8,128)(2,1)S(1)}, bf16[768,256]{1,0:T(8,128)(2,1)S(1)}, u32[]{:S(2)}, u32[]{:S(2)}) collective-permute-start(bf16[768,256]{1,0:T(8,128)(2,1)S(1)} %gate.5.refs_4_.refs_0_), channel_id=1, source_target_pairs={{1,0},{2,3},{5,4},{6,7},{9,8},{10,11},{13,12},{14,15},{17,16},{18,... | collective-permute-start | bytes 1179656 | tf_op jit(solution)/shard_map/ppermute | solution.py:571
  37.7 17.7 %collective-permute-start.5 = (bf16[768,256]{1,0:T(8,128)(2,1)S(1)}, bf16[768,256]{1,0:T(8,128)(2,1)S(1)}, u32[]{:S(2)}, u32[]{:S(2)}) collective-permute-start(bf16[768,256]{1,0:T(8,128)(2,1)S(1)} %gate.6.refs_4_.refs_0_), channel_id=1, source_target_pairs={{1,0},{2,3},{5,4},{6,7},{9,8},{10,11},{13,12},{14,15},{17,16},{18,... | collective-permute-start | bytes 1179656 | tf_op jit(solution)/shard_map/ppermute | solution.py:571
  57.8 2.3 %collective-permute-start.9 = (f32[8,128,128]{2,1,0:T(8,128)S(1)}, f32[8,128,128]{2,1,0:T(8,128)S(1)}, u32[]{:S(2)}, u32[]{:S(2)}) collective-permute-start(f32[8,128,128]{2,1,0:T(8,128)S(1)} %get-tuple-element.58), channel_id=1, source_target_pairs={{0,4},{4,0},{8,12},{12,8},{16,20},{20,16},{24,28},{28,24},{1,5},{5... | collective-permute-start | bytes 1572872 | tf_op jit(solution)/shard_map/ppermute | solution.py:490
  60.1 12.1 %copy-start = (f32[16,128,128]{2,1,0:T(8,128)S(1)}, f32[16,128,128]{2,1,0:T(8,128)}, u32[]{:S(2)}) copy-start(f32[16,128,128]{2,1,0:T(8,128)} %prior.3) | copy-start | bytes 3145732
  60.2 5.0 %collective-permute-start.13 = (bf16[4,128,128]{2,1,0:T(8,128)(2,1)S(1)}, bf16[4,128,128]{2,1,0:T(8,128)(2,1)S(1)}, u32[]{:S(2)}, u32[]{:S(2)}) collective-permute-start(bf16[4,128,128]{2,1,0:T(8,128)(2,1)S(1)} %meet.9), channel_id=1, source_target_pairs={{0,8},{4,20},{8,0},{12,28},{16,24},{20,4},{24,16},{28,12},{1,9},{5... | collective-permute-start | bytes 393224 | tf_op jit(solution)/shard_map/ppermute | solution.py:504
  61.8 5.1 %collective-permute-start.10 = (bf16[4,128,128]{2,1,0:T(8,128)(2,1)S(1)}, bf16[4,128,128]{2,1,0:T(8,128)(2,1)S(1)}, u32[]{:S(2)}, u32[]{:S(2)}) collective-permute-start(bf16[4,128,128]{2,1,0:T(8,128)(2,1)S(1)} %meet.6), channel_id=1, source_target_pairs={{0,8},{4,20},{8,0},{12,28},{16,24},{20,4},{24,16},{28,12},{1,9},{5... | collective-permute-start | bytes 393224 | tf_op jit(solution)/shard_map/ppermute | solution.py:504
  65.3 16.6 %copy-start.1 = (f32[2048]{0:T(1024)S(1)}, f32[2048]{0:T(1024)}, u32[]{:S(2)}) copy-start(f32[2048]{0:T(1024)} %param.7) | copy-start | bytes 24580
  65.3 5.0 %collective-permute-start.14 = (bf16[4,128,128]{2,1,0:T(8,128)(2,1)S(1)}, bf16[4,128,128]{2,1,0:T(8,128)(2,1)S(1)}, u32[]{:S(2)}, u32[]{:S(2)}) collective-permute-start(bf16[4,128,128]{2,1,0:T(8,128)(2,1)S(1)} %meet.10), channel_id=1, source_target_pairs={{0,16},{4,12},{8,24},{12,4},{16,0},{20,28},{24,8},{28,20},{1,17},{... | collective-permute-start | bytes 393224 | tf_op jit(solution)/shard_map/ppermute | solution.py:504
  67.0 5.0 %collective-permute-start.11 = (bf16[4,128,128]{2,1,0:T(8,128)(2,1)S(1)}, bf16[4,128,128]{2,1,0:T(8,128)(2,1)S(1)}, u32[]{:S(2)}, u32[]{:S(2)}) collective-permute-start(bf16[4,128,128]{2,1,0:T(8,128)(2,1)S(1)} %meet.7), channel_id=1, source_target_pairs={{0,16},{4,12},{8,24},{12,4},{16,0},{20,28},{24,8},{28,20},{1,17},{... | collective-permute-start | bytes 393224 | tf_op jit(solution)/shard_map/ppermute | solution.py:504
  70.4 2.5 %collective-permute-start.15 = (f32[4,128,128]{2,1,0:T(8,128)S(1)}, f32[4,128,128]{2,1,0:T(8,128)S(1)}, u32[]{:S(2)}, u32[]{:S(2)}) collective-permute-start(f32[4,128,128]{2,1,0:T(8,128)S(1)} %get-tuple-element.61), channel_id=1, source_target_pairs={{0,4},{4,0},{8,12},{12,8},{16,20},{20,16},{24,28},{28,24},{1,5},{5... | collective-permute-start | bytes 786440 | tf_op jit(solution)/shard_map/ppermute | solution.py:508
  72.1 1.6 %collective-permute-start.12 = (f32[4,128,128]{2,1,0:T(8,128)S(1)}, f32[4,128,128]{2,1,0:T(8,128)S(1)}, u32[]{:S(2)}, u32[]{:S(2)}) collective-permute-start(f32[4,128,128]{2,1,0:T(8,128)S(1)} %get-tuple-element.60), channel_id=1, source_target_pairs={{0,4},{4,0},{8,12},{12,8},{16,20},{20,16},{24,28},{28,24},{1,5},{5... | collective-permute-start | bytes 786440 | tf_op jit(solution)/shard_map/ppermute | solution.py:508
  74.4 5.5 %collective-permute-start.16 = (f32[8,256]{1,0:T(8,128)S(1)}, f32[8,256]{1,0:T(8,128)S(1)}, u32[]{:S(2)}, u32[]{:S(2)}) collective-permute-start(f32[8,256]{1,0:T(8,128)S(1)} %get-tuple-element.68.refs_0_), channel_id=1, source_target_pairs={{0,3},{1,2},{2,1},{3,0},{4,7},{5,6},{6,5},{7,4},{8,11},{9,10},{10,... | collective-permute-start | bytes 24584 | tf_op jit(solution)/shard_map/ppermute | solution.py:430
  77.3 4.5 %collective-permute-start.17 = (f32[8,256]{1,0:T(8,128)S(1)}, f32[8,256]{1,0:T(8,128)S(1)}, u32[]{:S(2)}, u32[]{:S(2)}) collective-permute-start(f32[8,256]{1,0:T(8,128)S(1)} %get-tuple-element.68.refs_0_), channel_id=1, source_target_pairs={{0,2},{1,3},{2,0},{3,1},{4,6},{5,7},{6,4},{7,5},{8,10},{9,11},{10,... | collective-permute-start | bytes 24584 | tf_op jit(solution)/shard_map/ppermute | solution.py:430
  77.3 4.5 %collective-permute-start.18 = (f32[8,256]{1,0:T(8,128)S(1)}, f32[8,256]{1,0:T(8,128)S(1)}, u32[]{:S(2)}, u32[]{:S(2)}) collective-permute-start(f32[8,256]{1,0:T(8,128)S(1)} %get-tuple-element.68.refs_0_), channel_id=1, source_target_pairs={{0,1},{1,0},{2,3},{3,2},{4,5},{5,4},{6,7},{7,6},{8,9},{9,8},{10,11... | collective-permute-start | bytes 24584 | tf_op jit(solution)/shard_map/ppermute | solution.py:430
